TPU v7x, 32 devices: a whole 2x2x4 slice. The times are simulated.
32 devices in a mesh: dp: 8 (over z, x), mp: 4 (over y, core).
Axes of the slice: x: 2, y: 2, z: 4, core: 2. Of those that a mesh axis runs over, the one named last changes fastest.
Arguments:
- tokens: bfloat16 [8, 512, 2048], P('dp', 'mp'), may hold values from -6 to 6
- norm_gains: float32 [3, 2048], replicated, may hold values from 0.25 to 1.75
- w_query: bfloat16 [2048, 2048], P(None, 'mp'), may hold values from -0.125 to 0.125
- w_key: bfloat16 [2048, 2048], P(None, 'mp'), may hold values from -0.125 to 0.125
- w_value: bfloat16 [2048, 2048], P(None, 'mp'), may hold values from -0.125 to 0.125
- w_out: bfloat16 [2048, 2048], P('mp'), may hold values from -0.75 to 0.75
- c_query: bfloat16 [2048, 2048], P(None, 'mp'), may hold values from -0.125 to 0.125
- c_key: bfloat16 [2048, 2048], P(None, 'mp'), may hold values from -0.125 to 0.125
- c_value: bfloat16 [2048, 2048], P(None, 'mp'), may hold values from -0.125 to 0.125
- c_out: bfloat16 [2048, 2048], P('mp'), may hold values from -1.5 to 1.5
- patch_proj: bfloat16 [1664, 2048], replicated, may hold values from -0.15625 to 0.15625
- w_gate: bfloat16 [2048, 5120], P(None, 'mp'), may hold values from -0.125 to 0.125
- w_up: bfloat16 [2048, 5120], P(None, 'mp'), may hold values from -0.125 to 0.125
- w_down: bfloat16 [5120, 2048], P('mp'), may hold values from -0.078125 to 0.078125
- patches: bfloat16 [32, 256, 1664], P('dp'), may hold values from -6 to 6
- segment_ids: int32 [8, 512], P('dp'), may hold values from 0 to 3, as said below
- image_index: int32 [8, 4], P('dp'), may hold values from 0 to 3
- cotangent: bfloat16 [8, 512, 2048], P('dp', 'mp'), may hold values from -6 to 6
Outputs:
- output: bfloat16 [8, 512, 2048], P('dp', 'mp')
- tokens_grad: float32 [8, 512, 2048], P('dp', 'mp')
- norm_gains_grad: float32 [3, 2048], P(None, ('dp', 'mp'))
- w_query_grad: float32 [2048, 2048], P('dp', 'mp')
- w_key_grad: float32 [2048, 2048], P('dp', 'mp')
- w_value_grad: float32 [2048, 2048], P('dp', 'mp')
- w_out_grad: float32 [2048, 2048], P('mp', 'dp')
- c_query_grad: float32 [2048, 2048], P('dp', 'mp')
- c_key_grad: float32 [2048, 2048], P('dp', 'mp')
- c_value_grad: float32 [2048, 2048], P('dp', 'mp')
- c_out_grad: float32 [2048, 2048], P('mp', 'dp')
- patch_proj_grad: float32 [1664, 2048], P(None, ('dp', 'mp'))
- w_gate_grad: float32 [2048, 5120], P('dp', 'mp')
- w_up_grad: float32 [2048, 5120], P('dp', 'mp')
- w_down_grad: float32 [5120, 2048], P('mp', 'dp')
Inputs may be any that keep to these rules, and one draw needn't show every extreme that they name: `segment_ids`: within each packed row the ids run from 0 to 3 without falling, and every id is present. `image_index`: rows held at index g of dp read the images g * 4 to g * 4 + 3.
All inputs are finite; a program needn't handle non-finite values.
Results may differ from a plain program's by a relative error of at most 0.033.
Values may be sent and summed in bfloat16 or wider, within the bound.
A program may use at most 256 MiB of HBM per device.

v0:
```python
import jax
import jax.numpy as jnp
from jax import lax
from jax.sharding import PartitionSpec as P

HEAD_DIM = 128
SEGS = 4


EPSILON = 1e-06


def rms_norm(rows_in, gain):
    return rows_in * lax.rsqrt(jnp.mean(rows_in * rows_in, axis=-1, keepdims=True) + EPSILON) * gain


def matmul(left, right):
    return jnp.dot(left, right, preferred_element_type=jnp.float32)


def attend_block(queries, key_rows, value_rows, allowed):
    score_scale = queries.shape[-1] ** (-0.5)
    scores = (
        jnp.einsum("shd,thd->hst", queries, key_rows, preferred_element_type=jnp.float32)
        * score_scale
    )
    scores = jnp.where(allowed[None], scores, -1000000000.0)
    row_max = jnp.max(scores, axis=-1, keepdims=True)
    exponent = jnp.exp(scores - row_max)
    row_total = jnp.sum(exponent, axis=-1, keepdims=True)
    weights = (exponent / row_total).astype(jnp.bfloat16)
    attended = jnp.einsum("hst,thd->shd", weights, value_rows, preferred_element_type=jnp.float32)
    return (attended.astype(jnp.bfloat16), (row_max + jnp.log(row_total))[..., 0])


def attend_back(queries, key_rows, value_rows, allowed, log_total, grad_out):
    score_scale = queries.shape[-1] ** (-0.5)
    scores = (
        jnp.einsum("shd,thd->hst", queries, key_rows, preferred_element_type=jnp.float32)
        * score_scale
    )
    scores = jnp.where(allowed[None], scores, -1000000000.0)
    weights = jnp.exp(scores - log_total[..., None])
    grad_weights = jnp.einsum(
        "shd,thd->hst", grad_out, value_rows, preferred_element_type=jnp.float32
    )
    inner_sum = jnp.sum(weights * grad_weights, axis=-1, keepdims=True)
    grad_scores = (weights * (grad_weights - inner_sum)).astype(jnp.bfloat16)
    grad_query = (
        jnp.einsum("hst,thd->shd", grad_scores, key_rows, preferred_element_type=jnp.float32)
        * score_scale
    )
    grad_key = (
        jnp.einsum("hst,shd->thd", grad_scores, queries, preferred_element_type=jnp.float32)
        * score_scale
    )
    grad_value = jnp.einsum(
        "hst,shd->thd", weights.astype(jnp.bfloat16), grad_out, preferred_element_type=jnp.float32
    )
    return (grad_query, grad_key, grad_value)


def gated_unit(gate_arg, up_arg):
    return jax.nn.gelu(gate_arg, approximate=True) * up_arg


def shards(
    tokens,
    norm_gains,
    w_query,
    w_key,
    w_value,
    w_out,
    c_query,
    c_key,
    c_value,
    c_out,
    patch_proj,
    w_gate,
    w_up,
    w_down,
    patches,
    segment_ids,
    image_index,
    cotangent,
):
    rows_here = segment_ids.shape[0]
    length = segment_ids.shape[1]
    local_heads = w_query.shape[1] // HEAD_DIM
    patch_rows = patches.shape[0] * patches.shape[1]
    positions = jnp.arange(length, dtype=jnp.int32)
    causal = positions[None, :] <= positions[:, None]
    seg_slots = jnp.arange(SEGS, dtype=jnp.int32)
    token_image = jnp.sum(
        jnp.where(segment_ids[:, :, None] == seg_slots, image_index[:, None, :], 0), axis=-1
    )
    patch_image = jnp.arange(patch_rows, dtype=jnp.int32) // patches.shape[1]

    def heads_view(arr):
        return arr.reshape(arr.shape[:-1] + (local_heads, HEAD_DIM))

    def flat_rows(arr):
        return arr.reshape(rows_here, length, local_heads * HEAD_DIM)

    def widen_rows(local_rows):
        return lax.all_gather(local_rows, "mp", axis=1, tiled=True)

    def narrow(partial_sum):
        return lax.psum_scatter(
            partial_sum.astype(jnp.bfloat16), "mp", scatter_dimension=1, tiled=True
        ).astype(jnp.float32)

    def gather_grad(grad_local):
        return lax.all_gather(grad_local.astype(jnp.bfloat16), "mp", axis=1, tiled=True)

    def sum_grad(partial_sum):
        return lax.psum_scatter(
            partial_sum.astype(jnp.bfloat16), "mp", scatter_dimension=1, tiled=True
        ).astype(jnp.float32)

    def self_allowed(segment_row):
        return (segment_row[:, None] == segment_row[None, :]) & causal

    def self_forward(row_parts):
        queries_row, keys_row, values_row, segment_row = row_parts
        return attend_block(queries_row, keys_row, values_row, self_allowed(segment_row))

    def self_backward(row_parts):
        queries_row, keys_row, values_row, segment_row, log_row, grad_row = row_parts
        return attend_back(
            queries_row, keys_row, values_row, self_allowed(segment_row), log_row, grad_row
        )

    residual = tokens.astype(jnp.float32)
    normed_one_local = rms_norm(residual, norm_gains[0]).astype(jnp.bfloat16)
    normed_one = widen_rows(normed_one_local)
    queries = matmul(normed_one, w_query).astype(jnp.bfloat16)
    key_rows = matmul(normed_one, w_key).astype(jnp.bfloat16)
    value_rows = matmul(normed_one, w_value).astype(jnp.bfloat16)
    self_mixed, self_log = lax.map(
        self_forward,
        (heads_view(queries), heads_view(key_rows), heads_view(value_rows), segment_ids),
    )
    self_mixed = flat_rows(self_mixed)
    after_self = residual + narrow(matmul(self_mixed, w_out))
    normed_two_local = rms_norm(after_self, norm_gains[1]).astype(jnp.bfloat16)
    normed_two = widen_rows(normed_two_local)
    cross_queries = matmul(normed_two, c_query).astype(jnp.bfloat16)
    patch_flat = patches.reshape(patch_rows, patches.shape[2])
    projected = matmul(patch_flat, patch_proj).astype(jnp.bfloat16)
    cross_keys = matmul(projected, c_key).astype(jnp.bfloat16)
    cross_values = matmul(projected, c_value).astype(jnp.bfloat16)

    def cross_allowed(image_row):
        return image_row[:, None] == patch_image[None, :]

    def cross_forward(row_parts):
        queries_row, image_row = row_parts
        return attend_block(
            queries_row, heads_view(cross_keys), heads_view(cross_values), cross_allowed(image_row)
        )

    def cross_backward(row_parts):
        queries_row, image_row, log_row, grad_row = row_parts
        return attend_back(
            queries_row,
            heads_view(cross_keys),
            heads_view(cross_values),
            cross_allowed(image_row),
            log_row,
            grad_row,
        )

    cross_mixed, cross_log = lax.map(cross_forward, (heads_view(cross_queries), token_image))
    cross_mixed = flat_rows(cross_mixed)
    after_cross = after_self + narrow(matmul(cross_mixed, c_out))
    normed_three_local = rms_norm(after_cross, norm_gains[2]).astype(jnp.bfloat16)
    normed_three = widen_rows(normed_three_local)
    gate_pre = matmul(normed_three, w_gate)
    up_pre = matmul(normed_three, w_up)
    hidden = gated_unit(gate_pre, up_pre).astype(jnp.bfloat16)
    output = (after_cross + narrow(matmul(hidden, w_down))).astype(jnp.bfloat16)
    grad_rows = cotangent.astype(jnp.float32)
    normed_full = normed_three
    grad_branch = gather_grad(grad_rows)
    grad_hidden = jnp.einsum("rsd,fd->rsf", grad_branch, w_down, preferred_element_type=jnp.float32)
    unused, gate_pull = jax.vjp(gated_unit, gate_pre, up_pre)
    grad_gate, grad_up = gate_pull(grad_hidden)
    grad_gate = grad_gate.astype(jnp.bfloat16)
    grad_up = grad_up.astype(jnp.bfloat16)
    grad_w_down = jnp.einsum("rsf,rsd->fd", hidden, grad_branch, preferred_element_type=jnp.float32)
    grad_w_gate = jnp.einsum(
        "rsd,rsf->df", normed_full, grad_gate, preferred_element_type=jnp.float32
    )
    grad_w_up = jnp.einsum("rsd,rsf->df", normed_full, grad_up, preferred_element_type=jnp.float32)
    grad_normed = sum_grad(
        jnp.einsum("rsf,df->rsd", grad_gate, w_gate, preferred_element_type=jnp.float32)
        + jnp.einsum("rsf,df->rsd", grad_up, w_up, preferred_element_type=jnp.float32)
    )
    unused, norm_pull = jax.vjp(rms_norm, after_cross, norm_gains[2])
    grad_input, grad_gain_three = norm_pull(grad_normed)
    grad_rows = grad_rows + grad_input
    normed_full = normed_two
    grad_branch = gather_grad(grad_rows)
    grad_attended = jnp.einsum(
        "rsd,ed->rse", grad_branch, c_out, preferred_element_type=jnp.float32
    ).astype(jnp.bfloat16)
    grad_c_out = jnp.einsum(
        "rse,rsd->ed", cross_mixed, grad_branch, preferred_element_type=jnp.float32
    )
    grad_cq, grad_ck, grad_cv = lax.map(
        cross_backward,
        (heads_view(cross_queries), token_image, cross_log, heads_view(grad_attended)),
    )
    grad_cq = flat_rows(grad_cq).astype(jnp.bfloat16)
    grad_ck = jnp.sum(grad_ck, axis=0).reshape(patch_rows, -1).astype(jnp.bfloat16)
    grad_cv = jnp.sum(grad_cv, axis=0).reshape(patch_rows, -1).astype(jnp.bfloat16)
    grad_c_query = jnp.einsum(
        "rsd,rse->de", normed_full, grad_cq, preferred_element_type=jnp.float32
    )
    grad_c_key = jnp.einsum("pd,pe->de", projected, grad_ck, preferred_element_type=jnp.float32)
    grad_c_value = jnp.einsum("pd,pe->de", projected, grad_cv, preferred_element_type=jnp.float32)
    projected_part = jnp.einsum(
        "pe,de->pd", grad_ck, c_key, preferred_element_type=jnp.float32
    ) + jnp.einsum("pe,de->pd", grad_cv, c_value, preferred_element_type=jnp.float32)
    grad_projected = lax.psum_scatter(
        projected_part.astype(jnp.bfloat16), "mp", scatter_dimension=0, tiled=True
    )
    share_rows = grad_projected.shape[0]
    patch_share = lax.dynamic_slice_in_dim(
        patch_flat, lax.axis_index("mp") * share_rows, share_rows, 0
    )
    grad_patch_proj = jnp.einsum(
        "pv,pd->vd", patch_share, grad_projected, preferred_element_type=jnp.float32
    )
    grad_normed = sum_grad(
        jnp.einsum("rse,de->rsd", grad_cq, c_query, preferred_element_type=jnp.float32)
    )
    unused, norm_pull = jax.vjp(rms_norm, after_self, norm_gains[1])
    grad_input, grad_gain_two = norm_pull(grad_normed)
    grad_rows = grad_rows + grad_input
    normed_full = normed_one
    grad_branch = gather_grad(grad_rows)
    grad_attended = jnp.einsum(
        "rsd,ed->rse", grad_branch, w_out, preferred_element_type=jnp.float32
    ).astype(jnp.bfloat16)
    grad_w_out = jnp.einsum(
        "rse,rsd->ed", self_mixed, grad_branch, preferred_element_type=jnp.float32
    )
    grad_sq, grad_sk, grad_sv = lax.map(
        self_backward,
        (
            heads_view(queries),
            heads_view(key_rows),
            heads_view(value_rows),
            segment_ids,
            self_log,
            heads_view(grad_attended),
        ),
    )
    grad_sq = flat_rows(grad_sq).astype(jnp.bfloat16)
    grad_sk = flat_rows(grad_sk).astype(jnp.bfloat16)
    grad_sv = flat_rows(grad_sv).astype(jnp.bfloat16)
    grad_w_query = jnp.einsum(
        "rsd,rse->de", normed_full, grad_sq, preferred_element_type=jnp.float32
    )
    grad_w_key = jnp.einsum("rsd,rse->de", normed_full, grad_sk, preferred_element_type=jnp.float32)
    grad_w_value = jnp.einsum(
        "rsd,rse->de", normed_full, grad_sv, preferred_element_type=jnp.float32
    )
    grad_normed = sum_grad(
        jnp.einsum("rse,de->rsd", grad_sq, w_query, preferred_element_type=jnp.float32)
        + jnp.einsum("rse,de->rsd", grad_sk, w_key, preferred_element_type=jnp.float32)
        + jnp.einsum("rse,de->rsd", grad_sv, w_value, preferred_element_type=jnp.float32)
    )
    unused, norm_pull = jax.vjp(rms_norm, residual, norm_gains[0])
    grad_input, grad_gain_one = norm_pull(grad_normed)
    grad_rows = grad_rows + grad_input
    gain_terms = jnp.stack([grad_gain_one, grad_gain_two, grad_gain_three])
    gain_total, patch_total = (
        lax.psum_scatter(gain_terms, ("dp", "mp"), scatter_dimension=1, tiled=True),
        lax.psum_scatter(grad_patch_proj, ("dp", "mp"), scatter_dimension=1, tiled=True),
    )
    (
        sum_query,
        sum_key,
        sum_value,
        sum_out,
        sum_cquery,
        sum_ckey,
        sum_cvalue,
        sum_cout,
        sum_gate,
        sum_up,
        sum_down,
    ) = (
        lax.psum_scatter(grad_w_query, "dp", scatter_dimension=0, tiled=True),
        lax.psum_scatter(grad_w_key, "dp", scatter_dimension=0, tiled=True),
        lax.psum_scatter(grad_w_value, "dp", scatter_dimension=0, tiled=True),
        lax.psum_scatter(grad_w_out, "dp", scatter_dimension=1, tiled=True),
        lax.psum_scatter(grad_c_query, "dp", scatter_dimension=0, tiled=True),
        lax.psum_scatter(grad_c_key, "dp", scatter_dimension=0, tiled=True),
        lax.psum_scatter(grad_c_value, "dp", scatter_dimension=0, tiled=True),
        lax.psum_scatter(grad_c_out, "dp", scatter_dimension=1, tiled=True),
        lax.psum_scatter(grad_w_gate, "dp", scatter_dimension=0, tiled=True),
        lax.psum_scatter(grad_w_up, "dp", scatter_dimension=0, tiled=True),
        lax.psum_scatter(grad_w_down, "dp", scatter_dimension=1, tiled=True),
    )
    return (
        output,
        grad_rows,
        gain_total,
        sum_query,
        sum_key,
        sum_value,
        sum_out,
        sum_cquery,
        sum_ckey,
        sum_cvalue,
        sum_cout,
        patch_total,
        sum_gate,
        sum_up,
        sum_down,
    )


def solution(mesh):
    return jax.shard_map(
        shards,
        mesh=mesh,
        in_specs=(
            P("dp", "mp", None),
            P(),
            P(None, "mp"),
            P(None, "mp"),
            P(None, "mp"),
            P("mp", None),
            P(None, "mp"),
            P(None, "mp"),
            P(None, "mp"),
            P("mp", None),
            P(),
            P(None, "mp"),
            P(None, "mp"),
            P("mp", None),
            P("dp", None, None),
            P("dp", None),
            P("dp", None),
            P("dp", "mp", None),
        ),
        out_specs=(
            P("dp", "mp", None),
            P("dp", "mp", None),
            P(None, ("dp", "mp")),
            P("dp", "mp"),
            P("dp", "mp"),
            P("dp", "mp"),
            P("mp", "dp"),
            P("dp", "mp"),
            P("dp", "mp"),
            P("dp", "mp"),
            P("mp", "dp"),
            P(None, ("dp", "mp")),
            P("dp", "mp"),
            P("dp", "mp"),
            P("mp", "dp"),
        ),
        check_vma=False,
    )
```

profile of v0, /device:TPU:0, one launch (start us, length us, event | category | flops | bytes accessed | tf_op | source)
XLA Modules:
  0.0 2077.5 jit_solution(7135586434089200670)
XLA Ops:
  14.4 23.7 %all-gather.7.cloned.1.call-done = bf16[1,512,2048]{2,1,0:T(8,128)(2,1)} async-done(((bf16[1,128,2048]{2,1,0:T(8,128)(2,1)}), bf16[1,512,2048]{2,1,0:T(8,128)(2,1)}) %all-gather.7.cloned.1.call-update) | async-done | bytes 2097168 | tf_op jit(solution)/shard_map/all_gather | solution.py:106
  55.2 30.3 %reduce-scatter.23.cloned.1.call-done = bf16[1,128,2048]{2,1,0:T(8,128)(2,1)} async-done(((bf16[1,512,2048]{2,1,0:T(8,128)(2,1)}), bf16[1,128,2048]{2,1,0:T(8,128)(2,1)}) %reduce-scatter.23.cloned.1.call-update) | async-done | bytes 524304 | tf_op jit(solution)/shard_map/reduce_scatter | solution.py:109
  126.7 31.5 %reduce-scatter.25.cloned.1.call-done = bf16[1,128,2048]{2,1,0:T(8,128)(2,1)} async-done(((bf16[1,512,2048]{2,1,0:T(8,128)(2,1)}), bf16[1,128,2048]{2,1,0:T(8,128)(2,1)}) %reduce-scatter.25.cloned.1.call-update) | async-done | bytes 524304 | tf_op jit(solution)/shard_map/reduce_scatter | solution.py:109
  163.1 22.1 %all-gather.11.cloned.1.call-done = bf16[1,512,2048]{2,1,0:T(8,128)(2,1)} async-done(((bf16[1,128,2048]{2,1,0:T(8,128)(2,1)}), bf16[1,512,2048]{2,1,0:T(8,128)(2,1)}) %all-gather.11.cloned.1.call-update) | async-done | bytes 2097168 | tf_op jit(solution)/shard_map/all_gather | solution.py:106
  209.2 10.3 multiply_convert_fusion.2
  232.1 31.6 %reduce-scatter.29.cloned.1.call-done = bf16[1,128,2048]{2,1,0:T(8,128)(2,1)} async-done(((bf16[1,512,2048]{2,1,0:T(8,128)(2,1)}), bf16[1,128,2048]{2,1,0:T(8,128)(2,1)}) %reduce-scatter.29.cloned.1.call-update) | async-done | bytes 524304 | tf_op jit(solution)/shard_map/reduce_scatter | solution.py:117
  268.8 22.7 %all-gather.15.cloned.1.call-done = bf16[1,512,2048]{2,1,0:T(8,128)(2,1)} async-done(((bf16[1,128,2048]{2,1,0:T(8,128)(2,1)}), bf16[1,512,2048]{2,1,0:T(8,128)(2,1)}) %all-gather.15.cloned.1.call-update) | async-done | bytes 2097168 | tf_op jit(solution)/shard_map/all_gather | solution.py:114
  316.3 24.0 %reduce-scatter.31.cloned.1.call-done = bf16[1,128,2048]{2,1,0:T(8,128)(2,1)} async-done(((bf16[1,512,2048]{2,1,0:T(8,128)(2,1)}), bf16[1,128,2048]{2,1,0:T(8,128)(2,1)}) %reduce-scatter.31.cloned.1.call-update) | async-done | bytes 524304 | tf_op jit(solution)/shard_map/reduce_scatter | solution.py:117
  342.2 32.0 %reduce-scatter.27.cloned.1.call-done = bf16[1,128,2048]{2,1,0:T(8,128)(2,1)} async-done(((bf16[1,512,2048]{2,1,0:T(8,128)(2,1)}), bf16[1,128,2048]{2,1,0:T(8,128)(2,1)}) %reduce-scatter.27.cloned.1.call-update) | async-done | bytes 524304 | tf_op jit(solution)/shard_map/reduce_scatter | solution.py:109
  378.4 22.7 %all-gather.17.cloned.1.call-done = bf16[1,512,2048]{2,1,0:T(8,128)(2,1)} async-done(((bf16[1,128,2048]{2,1,0:T(8,128)(2,1)}), bf16[1,512,2048]{2,1,0:T(8,128)(2,1)}) %all-gather.17.cloned.1.call-update) | async-done | bytes 2097168 | tf_op jit(solution)/shard_map/all_gather | solution.py:114
  431.8 15.5 reduce-scatter.33.cloned.1.call-done
  534.0 97.4 %reduce-scatter.61.cloned.1.call-done = f32[64,3]{1,0:T(8,128)} async-done(((f32[2048,3]{1,0:T(8,128)}), f32[64,3]{1,0:T(8,128)}) %reduce-scatter.61.cloned.1.call-update) | async-done | bytes 784
  632.8 87.1 %reduce-scatter.49.cloned.1.call-done = f32[512,256]{1,0:T(8,128)} async-done(((f32[512,2048]{1,0:T(8,128)}), f32[512,256]{1,0:T(8,128)}) %reduce-scatter.49.cloned.1.call-update) | async-done | bytes 524304 | tf_op jit(solution)/shard_map/reduce_scatter | solution.py:304
  719.9 92.2 %reduce-scatter.47.cloned.1.call-done = f32[256,512]{1,0:T(8,128)} async-done(((f32[2048,512]{1,0:T(8,128)}), f32[256,512]{1,0:T(8,128)}) %reduce-scatter.47.cloned.1.call-update) | async-done | bytes 524304 | tf_op jit(solution)/shard_map/reduce_scatter | solution.py:303
  812.1 91.7 %reduce-scatter.45.cloned.1.call-done = f32[256,512]{1,0:T(8,128)} async-done(((f32[2048,512]{1,0:T(8,128)}), f32[256,512]{1,0:T(8,128)}) %reduce-scatter.45.cloned.1.call-update) | async-done | bytes 524304 | tf_op jit(solution)/shard_map/reduce_scatter | solution.py:302
  903.8 92.4 %reduce-scatter.43.cloned.1.call-done = f32[256,512]{1,0:T(8,128)} async-done(((f32[2048,512]{1,0:T(8,128)}), f32[256,512]{1,0:T(8,128)}) %reduce-scatter.43.cloned.1.call-update) | async-done | bytes 524304 | tf_op jit(solution)/shard_map/reduce_scatter | solution.py:301
  996.2 182.4 %reduce-scatter.59.cloned.1.call-done = f32[1280,256]{1,0:T(8,128)} async-done(((f32[1280,2048]{1,0:T(8,128)}), f32[1280,256]{1,0:T(8,128)}) %reduce-scatter.59.cloned.1.call-update) | async-done | bytes 1310736 | tf_op jit(solution)/shard_map/reduce_scatter | solution.py:307
  1178.6 181.2 %reduce-scatter.57.cloned.1.call-done = f32[256,1280]{1,0:T(8,128)} async-done(((f32[2048,1280]{1,0:T(8,128)}), f32[256,1280]{1,0:T(8,128)}) %reduce-scatter.57.cloned.1.call-update) | async-done | bytes 1310736 | tf_op jit(solution)/shard_map/reduce_scatter | solution.py:306
  1359.8 181.3 %reduce-scatter.55.cloned.1.call-done = f32[256,1280]{1,0:T(8,128)} async-done(((f32[2048,1280]{1,0:T(8,128)}), f32[256,1280]{1,0:T(8,128)}) %reduce-scatter.55.cloned.1.call-update) | async-done | bytes 1310736 | tf_op jit(solution)/shard_map/reduce_scatter | solution.py:305
  1541.1 91.6 %reduce-scatter.41.cloned.1.call-done = f32[512,256]{1,0:T(8,128)} async-done(((f32[512,2048]{1,0:T(8,128)}), f32[512,256]{1,0:T(8,128)}) %reduce-scatter.41.cloned.1.call-update) | async-done | bytes 524304 | tf_op jit(solution)/shard_map/reduce_scatter | solution.py:300
  1632.7 92.5 %reduce-scatter.37.cloned.1.call-done = f32[256,512]{1,0:T(8,128)} async-done(((f32[2048,512]{1,0:T(8,128)}), f32[256,512]{1,0:T(8,128)}) %reduce-scatter.37.cloned.1.call-update) | async-done | bytes 524304 | tf_op jit(solution)/shard_map/reduce_scatter | solution.py:298
  1725.2 91.9 %reduce-scatter.35.cloned.1.call-done = f32[256,512]{1,0:T(8,128)} async-done(((f32[2048,512]{1,0:T(8,128)}), f32[256,512]{1,0:T(8,128)}) %reduce-scatter.35.cloned.1.call-update) | async-done | bytes 524304 | tf_op jit(solution)/shard_map/reduce_scatter | solution.py:297
  1817.1 92.5 %reduce-scatter.39.cloned.1.call-done = f32[256,512]{1,0:T(8,128)} async-done(((f32[2048,512]{1,0:T(8,128)}), f32[256,512]{1,0:T(8,128)}) %reduce-scatter.39.cloned.1.call-update) | async-done | bytes 524304 | tf_op jit(solution)/shard_map/reduce_scatter | solution.py:299
  1909.6 160.9 %reduce-scatter.53.cloned.1.call-done = f32[1664,64]{0,1:T(8,128)} async-done(((f32[1664,2048]{0,1:T(8,128)}), f32[1664,64]{0,1:T(8,128)}) %reduce-scatter.53.cloned.1.call-update) | async-done | bytes 426000 | tf_op jit(solution)/shard_map/reduce_scatter | solution.py:282
  (244 shorter events, 260.8 us)
Async XLA Ops:
  12.7 72.8 %reduce-scatter.23.cloned.1.call-start = ((), (), s32[]{:S(2)}) async-start(), calls=%async_computation.21 | async-start | bytes 2621440 | tf_op jit(solution)/shard_map/reduce_scatter | solution.py:109
  53.8 58.0 %all-gather.9.cloned.1.call-start = ((), (), s32[]{:S(2)}) async-start(), calls=%async_computation.22 | async-start | bytes 2621440 | tf_op jit(solution)/shard_map/all_gather | solution.py:106
  89.1 69.2 %reduce-scatter.25.cloned.1.call-start = ((), (), s32[]{:S(2)}) async-start(), calls=%async_computation.23 | async-start | bytes 2621440 | tf_op jit(solution)/shard_map/reduce_scatter | solution.py:109
  126.7 58.5 %all-gather.11.cloned.1.call-start = ((), (), s32[]{:S(2)}) async-start(), calls=%async_computation.24 | async-start | bytes 2621440 | tf_op jit(solution)/shard_map/all_gather | solution.py:106
  163.0 100.6 %reduce-scatter.29.cloned.1.call-start = ((), (), s32[]{:S(2)}) async-start(), calls=%async_computation.27 | async-start | bytes 2621440 | tf_op jit(solution)/shard_map/reduce_scatter | solution.py:117
  232.0 59.4 %all-gather.15.cloned.1.call-start = ((), (), s32[]{:S(2)}) async-start(), calls=%async_computation.28 | async-start | bytes 2621440 | tf_op jit(solution)/shard_map/all_gather | solution.py:114
  268.7 71.6 %reduce-scatter.31.cloned.1.call-start = ((), (), s32[]{:S(2)}) async-start(), calls=%async_computation.29 | async-start | bytes 2621440 | tf_op jit(solution)/shard_map/reduce_scatter | solution.py:117
  308.7 65.4 %reduce-scatter.27.cloned.1.call-start = ((), (), s32[]{:S(2)}) async-start(), calls=%async_computation.25 | async-start | bytes 2621440 | tf_op jit(solution)/shard_map/reduce_scatter | solution.py:109
  315.9 85.3 %all-gather.17.cloned.1.call-start = ((), (), s32[]{:S(2)}) async-start(), calls=%async_computation.30 | async-start | bytes 2621440 | tf_op jit(solution)/shard_map/all_gather | solution.py:114
  378.4 68.9 %reduce-scatter.33.cloned.1.call-start = ((), (), s32[]{:S(2)}) async-start(), calls=%async_computation.31 | async-start | bytes 2621440 | tf_op jit(solution)/shard_map/reduce_scatter | solution.py:117
  415.7 106.6 %reduce-scatter.51.cloned.1.call-start = ((), (), s32[]{:S(2)}) async-start(), calls=%async_computation.40 | async-start | bytes 5242880 | tf_op jit(solution)/shard_map/reduce_scatter | solution.py:226
  431.8 199.6 %reduce-scatter.61.cloned.1.call-start = ((), (), s32[]{:S(2)}) async-start(), calls=%async_computation.45 | async-start | bytes 1081344
  450.5 269.4 %reduce-scatter.49.cloned.1.call-start = ((), (), s32[]{:S(2)}) async-start(), calls=%async_computation.39 | async-start | bytes 4718592 | tf_op jit(solution)/shard_map/reduce_scatter | solution.py:304
  455.7 356.4 %reduce-scatter.47.cloned.1.call-start = ((), (), s32[]{:S(2)}) async-start(), calls=%async_computation.38 | async-start | bytes 4718592 | tf_op jit(solution)/shard_map/reduce_scatter | solution.py:303
  463.2 440.6 %reduce-scatter.45.cloned.1.call-start = ((), (), s32[]{:S(2)}) async-start(), calls=%async_computation.37 | async-start | bytes 4718592 | tf_op jit(solution)/shard_map/reduce_scatter | solution.py:302
  470.3 525.9 %reduce-scatter.43.cloned.1.call-start = ((), (), s32[]{:S(2)}) async-start(), calls=%async_computation.36 | async-start | bytes 4718592 | tf_op jit(solution)/shard_map/reduce_scatter | solution.py:301
  475.3 703.3 %reduce-scatter.59.cloned.1.call-start = ((), (), s32[]{:S(2)}) async-start(), calls=%async_computation.44 | async-start | bytes 11796480 | tf_op jit(solution)/shard_map/reduce_scatter | solution.py:307
  484.1 875.6 %reduce-scatter.57.cloned.1.call-start = ((), (), s32[]{:S(2)}) async-start(), calls=%async_computation.43 | async-start | bytes 11796480 | tf_op jit(solution)/shard_map/reduce_scatter | solution.py:306
  493.0 1048.1 %reduce-scatter.55.cloned.1.call-start = ((), (), s32[]{:S(2)}) async-start(), calls=%async_computation.42 | async-start | bytes 11796480 | tf_op jit(solution)/shard_map/reduce_scatter | solution.py:305
  502.2 1130.6 %reduce-scatter.41.cloned.1.call-start = ((), (), s32[]{:S(2)}) async-start(), calls=%async_computation.35 | async-start | bytes 4718592 | tf_op jit(solution)/shard_map/reduce_scatter | solution.py:300
  507.2 1218.0 %reduce-scatter.37.cloned.1.call-start = ((), (), s32[]{:S(2)}) async-start(), calls=%async_computation.33 | async-start | bytes 4718592 | tf_op jit(solution)/shard_map/reduce_scatter | solution.py:298
  512.2 1304.9 %reduce-scatter.35.cloned.1.call-start = ((), (), s32[]{:S(2)}) async-start(), calls=%async_computation.32 | async-start | bytes 4718592 | tf_op jit(solution)/shard_map/reduce_scatter | solution.py:297
  517.3 1392.4 %reduce-scatter.39.cloned.1.call-start = ((), (), s32[]{:S(2)}) async-start(), calls=%async_computation.34 | async-start | bytes 4718592 | tf_op jit(solution)/shard_map/reduce_scatter | solution.py:299
  522.3 1548.2 %reduce-scatter.53.cloned.1.call-start = ((), (), s32[]{:S(2)}) async-start(), calls=%async_computation.41 | async-start | bytes 14057472 | tf_op jit(solution)/shard_map/reduce_scatter | solution.py:282
  (57 other events, 349.3 us)
Sparse Core Ops, SparseCore 0:
  12.8 25.2 all-gather.6
  54.0 31.4 reduce-scatter.22
  89.2 22.5 all-gather.8
  126.8 31.4 reduce-scatter.24
  162.6 22.5 all-gather.10
  232.1 31.4 reduce-scatter.28
  268.8 22.5 all-gather.14
  308.8 31.4 reduce-scatter.30
  342.7 31.4 reduce-scatter.26
  415.8 31.4 reduce-scatter.32
  449.8 44.4 reduce-scatter.50
  496.6 134.7 reduce-scatter.60
  635.4 84.3 reduce-scatter.48
  724.3 87.6 reduce-scatter.46
  816.1 87.6 reduce-scatter.44
  908.3 87.8 reduce-scatter.42
  1000.4 178.1 reduce-scatter.58
  1182.6 177.1 reduce-scatter.56
  1363.9 177.1 reduce-scatter.54
  1545.3 87.3 reduce-scatter.40
  1637.4 87.7 reduce-scatter.36
  1729.3 87.7 reduce-scatter.34
  1821.8 87.8 reduce-scatter.38
  1912.4 158.0 reduce-scatter.52
  (2 shorter events, 45.1 us)
where the time goes:
time: 2080 us
  waiting for transfers between devices  1810 us (87%)
  matrix products  203 us (10%)
  other arithmetic  35.2 us (2%)
    reduce_scatter x1, waiting for transfers between devices, shards(): lax.psum_scatter(grad_w_down, 'dp', scatter_dimension=1, tiled=True)  182 us
    reduce_scatter x1, waiting for transfers between devices, shards(): lax.psum_scatter(grad_w_gate, 'dp', scatter_dimension=0, tiled=True)  181 us
    reduce_scatter x1, waiting for transfers between devices, shards(): lax.psum_scatter(grad_w_up, 'dp', scatter_dimension=0, tiled=True)  181 us
    reduce_scatter x1, waiting for transfers between devices, shards(): lax.psum_scatter(grad_patch_proj, ('dp', 'mp'), scatter_dimension=1, tile...  161 us
    unnamed x27, waiting for transfers between devices  98.3 us
    reduce_scatter x3, waiting for transfers between devices, narrow(): lax.psum_scatter(partial_sum.astype(jnp.bfloat16), 'mp', scatter_dimensio...  93.8 us
    reduce_scatter x1, waiting for transfers between devices, shards(): lax.psum_scatter(grad_w_value, 'dp', scatter_dimension=0, tiled=True)  92.5 us
    reduce_scatter x1, waiting for transfers between devices, shards(): lax.psum_scatter(grad_w_key, 'dp', scatter_dimension=0, tiled=True)  92.5 us
  transfers between devices with their start and end apart: 26, of which 25 were waited for; matrix products, arithmetic and copies ran while one was open for 7% of the time, Pallas kernels for 0%

commit v1 on v0

--- a/solution.py
+++ b/solution.py
@@ -277,35 +277,24 @@
     grad_input, grad_gain_one = norm_pull(grad_normed)
     grad_rows = grad_rows + grad_input
     gain_terms = jnp.stack([grad_gain_one, grad_gain_two, grad_gain_three])
-    gain_total, patch_total = (
-        lax.psum_scatter(gain_terms, ("dp", "mp"), scatter_dimension=1, tiled=True),
-        lax.psum_scatter(grad_patch_proj, ("dp", "mp"), scatter_dimension=1, tiled=True),
-    )
-    (
-        sum_query,
-        sum_key,
-        sum_value,
-        sum_out,
-        sum_cquery,
-        sum_ckey,
-        sum_cvalue,
-        sum_cout,
-        sum_gate,
-        sum_up,
-        sum_down,
-    ) = (
-        lax.psum_scatter(grad_w_query, "dp", scatter_dimension=0, tiled=True),
-        lax.psum_scatter(grad_w_key, "dp", scatter_dimension=0, tiled=True),
-        lax.psum_scatter(grad_w_value, "dp", scatter_dimension=0, tiled=True),
-        lax.psum_scatter(grad_w_out, "dp", scatter_dimension=1, tiled=True),
-        lax.psum_scatter(grad_c_query, "dp", scatter_dimension=0, tiled=True),
-        lax.psum_scatter(grad_c_key, "dp", scatter_dimension=0, tiled=True),
-        lax.psum_scatter(grad_c_value, "dp", scatter_dimension=0, tiled=True),
-        lax.psum_scatter(grad_c_out, "dp", scatter_dimension=1, tiled=True),
-        lax.psum_scatter(grad_w_gate, "dp", scatter_dimension=0, tiled=True),
-        lax.psum_scatter(grad_w_up, "dp", scatter_dimension=0, tiled=True),
-        lax.psum_scatter(grad_w_down, "dp", scatter_dimension=1, tiled=True),
-    )
+    def sum_rows(partial, axes, dim):
+        return lax.psum_scatter(
+            partial.astype(jnp.bfloat16), axes, scatter_dimension=dim, tiled=True
+        ).astype(jnp.float32)
+
+    gain_total = lax.psum_scatter(gain_terms, ("dp", "mp"), scatter_dimension=1, tiled=True)
+    patch_total = sum_rows(grad_patch_proj, ("dp", "mp"), 1)
+    sum_query = sum_rows(grad_w_query, "dp", 0)
+    sum_key = sum_rows(grad_w_key, "dp", 0)
+    sum_value = sum_rows(grad_w_value, "dp", 0)
+    sum_out = sum_rows(grad_w_out, "dp", 1)
+    sum_cquery = sum_rows(grad_c_query, "dp", 0)
+    sum_ckey = sum_rows(grad_c_key, "dp", 0)
+    sum_cvalue = sum_rows(grad_c_value, "dp", 0)
+    sum_cout = sum_rows(grad_c_out, "dp", 1)
+    sum_gate = sum_rows(grad_w_gate, "dp", 0)
+    sum_up = sum_rows(grad_w_up, "dp", 0)
+    sum_down = sum_rows(grad_w_down, "dp", 1)
     return (
         output,
         grad_rows,

time: 2080 us -> 1680 us (0.81)
  waiting for transfers between devices: 1810 us -> 1390 us
  other arithmetic: 35.2 us -> 58 us
    reduce_scatter x12, waiting for transfers between devices: 1440 us -> 998 us  [sum_rows(): lax.psum_scatter(partial.astype(jnp.bfloat16), axes, scatter_dimension=di...]
    unnamed x27, waiting for transfers between devices: 98.3 us -> 133 us
    convert_element_type x0 -> x12, other arithmetic: none -> 22.8 us  [sum_rows(): return lax.psum_scatter(partial.astype(jnp.bfloat16), axes, scatter_dimen...]
  transfers between devices with their start and end apart: 26 -> 26, of which waited for: 25 -> 24; matrix products, arithmetic and copies ran while one was open for 7% -> 9% of each run, Pallas kernels for 0% -> 0%
where the time goes in v1:
time: 1680 us; the launch traced here: 1670 us
  waiting for transfers between devices  1390 us (83%)
  matrix products  192 us (11%)
  other arithmetic  58 us (3%)
    reduce_scatter x12, waiting for transfers between devices, sum_rows(): lax.psum_scatter(partial.astype(jnp.bfloat16), axes, scatter_dimension=di...  998 us
    unnamed x27, waiting for transfers between devices  133 us
    reduce_scatter x3, waiting for transfers between devices, narrow(): lax.psum_scatter(partial_sum.astype(jnp.bfloat16), 'mp', scatter_dimensio...  93.8 us
    reduce_scatter x3, waiting for transfers between devices, sum_grad(): lax.psum_scatter(partial_sum.astype(jnp.bfloat16), 'mp', scatter_dimensio...  55.5 us
    all_gather x3, waiting for transfers between devices, gather_grad(): lax.all_gather(grad_local.astype(jnp.bfloat16), 'mp', axis=1, tiled=True)  54.5 us
    dot_general x12, matrix products, matmul(): return jnp.dot(left, right, preferred_element_type=jnp.float32)  54.1 us
    all_gather x3, waiting for transfers between devices, widen_rows(): return lax.all_gather(local_rows, 'mp', axis=1, tiled=True)  51.1 us
  transfers between devices with their start and end apart: 26, of which 24 were waited for; matrix products, arithmetic and copies ran while one was open for 9% of the time, Pallas kernels for 0%

profile of v1, /device:TPU:0, one launch (start us, length us, event | category | flops | bytes accessed | tf_op | source)
XLA Modules:
  0.0 1668.2 jit_solution(11060960893077053828)
XLA Ops:
  14.5 23.7 %all-gather.7.cloned.1.call-done = bf16[1,512,2048]{2,1,0:T(8,128)(2,1)} async-done(((bf16[1,128,2048]{2,1,0:T(8,128)(2,1)}), bf16[1,512,2048]{2,1,0:T(8,128)(2,1)}) %all-gather.7.cloned.1.call-update) | async-done | bytes 2097168 | tf_op jit(solution)/shard_map/all_gather | solution.py:106
  55.2 30.3 %reduce-scatter.23.cloned.1.call-done = bf16[1,128,2048]{2,1,0:T(8,128)(2,1)} async-done(((bf16[1,512,2048]{2,1,0:T(8,128)(2,1)}), bf16[1,128,2048]{2,1,0:T(8,128)(2,1)}) %reduce-scatter.23.cloned.1.call-update) | async-done | bytes 524304 | tf_op jit(solution)/shard_map/reduce_scatter | solution.py:109
  89.7 10.1 convolution_convert_fusion.4
  126.8 31.5 %reduce-scatter.25.cloned.1.call-done = bf16[1,128,2048]{2,1,0:T(8,128)(2,1)} async-done(((bf16[1,512,2048]{2,1,0:T(8,128)(2,1)}), bf16[1,128,2048]{2,1,0:T(8,128)(2,1)}) %reduce-scatter.25.cloned.1.call-update) | async-done | bytes 524304 | tf_op jit(solution)/shard_map/reduce_scatter | solution.py:109
  163.1 22.1 %all-gather.11.cloned.1.call-done = bf16[1,512,2048]{2,1,0:T(8,128)(2,1)} async-done(((bf16[1,128,2048]{2,1,0:T(8,128)(2,1)}), bf16[1,512,2048]{2,1,0:T(8,128)(2,1)}) %all-gather.11.cloned.1.call-update) | async-done | bytes 2097168 | tf_op jit(solution)/shard_map/all_gather | solution.py:106
  209.3 10.4 multiply_convert_fusion.2
  232.2 31.5 %reduce-scatter.29.cloned.1.call-done = bf16[1,128,2048]{2,1,0:T(8,128)(2,1)} async-done(((bf16[1,512,2048]{2,1,0:T(8,128)(2,1)}), bf16[1,128,2048]{2,1,0:T(8,128)(2,1)}) %reduce-scatter.29.cloned.1.call-update) | async-done | bytes 524304 | tf_op jit(solution)/shard_map/reduce_scatter | solution.py:117
  268.9 22.7 %all-gather.15.cloned.1.call-done = bf16[1,512,2048]{2,1,0:T(8,128)(2,1)} async-done(((bf16[1,128,2048]{2,1,0:T(8,128)(2,1)}), bf16[1,512,2048]{2,1,0:T(8,128)(2,1)}) %all-gather.15.cloned.1.call-update) | async-done | bytes 2097168 | tf_op jit(solution)/shard_map/all_gather | solution.py:114
  316.5 23.9 %reduce-scatter.31.cloned.1.call-done = bf16[1,128,2048]{2,1,0:T(8,128)(2,1)} async-done(((bf16[1,512,2048]{2,1,0:T(8,128)(2,1)}), bf16[1,128,2048]{2,1,0:T(8,128)(2,1)}) %reduce-scatter.31.cloned.1.call-update) | async-done | bytes 524304 | tf_op jit(solution)/shard_map/reduce_scatter | solution.py:117
  342.3 32.0 %reduce-scatter.27.cloned.1.call-done = bf16[1,128,2048]{2,1,0:T(8,128)(2,1)} async-done(((bf16[1,512,2048]{2,1,0:T(8,128)(2,1)}), bf16[1,128,2048]{2,1,0:T(8,128)(2,1)}) %reduce-scatter.27.cloned.1.call-update) | async-done | bytes 524304 | tf_op jit(solution)/shard_map/reduce_scatter | solution.py:109
  378.6 22.7 %all-gather.17.cloned.1.call-done = bf16[1,512,2048]{2,1,0:T(8,128)(2,1)} async-done(((bf16[1,128,2048]{2,1,0:T(8,128)(2,1)}), bf16[1,512,2048]{2,1,0:T(8,128)(2,1)}) %all-gather.17.cloned.1.call-update) | async-done | bytes 2097168 | tf_op jit(solution)/shard_map/all_gather | solution.py:114
  504.2 97.3 %reduce-scatter.59.cloned.1.call-done = bf16[1280,256]{1,0:T(8,128)(2,1)} async-done(((bf16[1280,2048]{1,0:T(8,128)(2,1)}), bf16[1280,256]{1,0:T(8,128)(2,1)}) %reduce-scatter.59.cloned.1.call-update) | async-done | bytes 655376 | tf_op jit(solution)/shard_map/reduce_scatter | solution.py:281
  603.7 104.0 %reduce-scatter.57.cloned.1.call-done = bf16[256,1280]{1,0:T(8,128)(2,1)} async-done(((bf16[2048,1280]{1,0:T(8,128)(2,1)}), bf16[256,1280]{1,0:T(8,128)(2,1)}) %reduce-scatter.57.cloned.1.call-update) | async-done | bytes 655376 | tf_op jit(solution)/shard_map/reduce_scatter | solution.py:281
  709.9 104.0 %reduce-scatter.55.cloned.1.call-done = bf16[256,1280]{1,0:T(8,128)(2,1)} async-done(((bf16[2048,1280]{1,0:T(8,128)(2,1)}), bf16[256,1280]{1,0:T(8,128)(2,1)}) %reduce-scatter.55.cloned.1.call-update) | async-done | bytes 655376 | tf_op jit(solution)/shard_map/reduce_scatter | solution.py:281
  816.1 69.3 %reduce-scatter.49.cloned.1.call-done = bf16[512,256]{1,0:T(8,128)(2,1)} async-done(((bf16[512,2048]{1,0:T(8,128)(2,1)}), bf16[512,256]{1,0:T(8,128)(2,1)}) %reduce-scatter.49.cloned.1.call-update) | async-done | bytes 262160 | tf_op jit(solution)/shard_map/reduce_scatter | solution.py:281
  887.1 68.7 %reduce-scatter.47.cloned.1.call-done = bf16[256,512]{1,0:T(8,128)(2,1)} async-done(((bf16[2048,512]{1,0:T(8,128)(2,1)}), bf16[256,512]{1,0:T(8,128)(2,1)}) %reduce-scatter.47.cloned.1.call-update) | async-done | bytes 262160 | tf_op jit(solution)/shard_map/reduce_scatter | solution.py:281
  957.7 68.8 %reduce-scatter.45.cloned.1.call-done = bf16[256,512]{1,0:T(8,128)(2,1)} async-done(((bf16[2048,512]{1,0:T(8,128)(2,1)}), bf16[256,512]{1,0:T(8,128)(2,1)}) %reduce-scatter.45.cloned.1.call-update) | async-done | bytes 262160 | tf_op jit(solution)/shard_map/reduce_scatter | solution.py:281
  1028.2 68.5 %reduce-scatter.43.cloned.1.call-done = bf16[256,512]{1,0:T(8,128)(2,1)} async-done(((bf16[2048,512]{1,0:T(8,128)(2,1)}), bf16[256,512]{1,0:T(8,128)(2,1)}) %reduce-scatter.43.cloned.1.call-update) | async-done | bytes 262160 | tf_op jit(solution)/shard_map/reduce_scatter | solution.py:281
  1098.5 69.3 %reduce-scatter.41.cloned.1.call-done = bf16[512,256]{1,0:T(8,128)(2,1)} async-done(((bf16[512,2048]{1,0:T(8,128)(2,1)}), bf16[512,256]{1,0:T(8,128)(2,1)}) %reduce-scatter.41.cloned.1.call-update) | async-done | bytes 262160 | tf_op jit(solution)/shard_map/reduce_scatter | solution.py:281
  1169.6 68.8 %reduce-scatter.39.cloned.1.call-done = bf16[256,512]{1,0:T(8,128)(2,1)} async-done(((bf16[2048,512]{1,0:T(8,128)(2,1)}), bf16[256,512]{1,0:T(8,128)(2,1)}) %reduce-scatter.39.cloned.1.call-update) | async-done | bytes 262160 | tf_op jit(solution)/shard_map/reduce_scatter | solution.py:281
  1240.2 68.7 %reduce-scatter.37.cloned.1.call-done = bf16[256,512]{1,0:T(8,128)(2,1)} async-done(((bf16[2048,512]{1,0:T(8,128)(2,1)}), bf16[256,512]{1,0:T(8,128)(2,1)}) %reduce-scatter.37.cloned.1.call-update) | async-done | bytes 262160 | tf_op jit(solution)/shard_map/reduce_scatter | solution.py:281
  1310.6 68.6 %reduce-scatter.35.cloned.1.call-done = bf16[256,512]{1,0:T(8,128)(2,1)} async-done(((bf16[2048,512]{1,0:T(8,128)(2,1)}), bf16[256,512]{1,0:T(8,128)(2,1)}) %reduce-scatter.35.cloned.1.call-update) | async-done | bytes 262160 | tf_op jit(solution)/shard_map/reduce_scatter | solution.py:281
  1383.9 131.6 %reduce-scatter.61.cloned.1.call-done = f32[64,3]{1,0:T(8,128)} async-done(((f32[2048,3]{1,0:T(8,128)}), f32[64,3]{1,0:T(8,128)}) %reduce-scatter.61.cloned.1.call-update) | async-done | bytes 784
  1516.9 142.6 %reduce-scatter.53.cloned.1.call-done = bf16[1664,64]{0,1:T(8,128)(2,1)} async-done(((bf16[1664,2048]{0,1:T(8,128)(2,1)}), bf16[1664,64]{0,1:T(8,128)(2,1)}) %reduce-scatter.53.cloned.1.call-update) | async-done | bytes 213008 | tf_op jit(solution)/shard_map/reduce_scatter | solution.py:281
  (256 shorter events, 261.9 us)
Async XLA Ops:
  12.8 72.7 %reduce-scatter.23.cloned.1.call-start = ((), (), s32[]{:S(2)}) async-start(), calls=%async_computation.21 | async-start | bytes 2621440 | tf_op jit(solution)/shard_map/reduce_scatter | solution.py:109
  53.9 58.0 %all-gather.9.cloned.1.call-start = ((), (), s32[]{:S(2)}) async-start(), calls=%async_computation.22 | async-start | bytes 2621440 | tf_op jit(solution)/shard_map/all_gather | solution.py:106
  89.2 69.1 %reduce-scatter.25.cloned.1.call-start = ((), (), s32[]{:S(2)}) async-start(), calls=%async_computation.23 | async-start | bytes 2621440 | tf_op jit(solution)/shard_map/reduce_scatter | solution.py:109
  126.7 58.5 %all-gather.11.cloned.1.call-start = ((), (), s32[]{:S(2)}) async-start(), calls=%async_computation.24 | async-start | bytes 2621440 | tf_op jit(solution)/shard_map/all_gather | solution.py:106
  163.1 100.7 %reduce-scatter.29.cloned.1.call-start = ((), (), s32[]{:S(2)}) async-start(), calls=%async_computation.27 | async-start | bytes 2621440 | tf_op jit(solution)/shard_map/reduce_scatter | solution.py:117
  232.1 59.4 %all-gather.15.cloned.1.call-start = ((), (), s32[]{:S(2)}) async-start(), calls=%async_computation.28 | async-start | bytes 2621440 | tf_op jit(solution)/shard_map/all_gather | solution.py:114
  268.8 71.6 %reduce-scatter.31.cloned.1.call-start = ((), (), s32[]{:S(2)}) async-start(), calls=%async_computation.29 | async-start | bytes 2621440 | tf_op jit(solution)/shard_map/reduce_scatter | solution.py:117
  308.8 65.4 %reduce-scatter.27.cloned.1.call-start = ((), (), s32[]{:S(2)}) async-start(), calls=%async_computation.25 | async-start | bytes 2621440 | tf_op jit(solution)/shard_map/reduce_scatter | solution.py:109
  316.0 85.2 %all-gather.17.cloned.1.call-start = ((), (), s32[]{:S(2)}) async-start(), calls=%async_computation.30 | async-start | bytes 2621440 | tf_op jit(solution)/shard_map/all_gather | solution.py:114
  378.5 116.2 %reduce-scatter.33.cloned.1.call-start = ((), (), s32[]{:S(2)}) async-start(), calls=%async_computation.31 | async-start | bytes 2621440 | tf_op jit(solution)/shard_map/reduce_scatter | solution.py:117
  415.9 82.1 %reduce-scatter.51.cloned.1.call-start = ((), (), s32[]{:S(2)}) async-start(), calls=%async_computation.40 | async-start | bytes 5242880 | tf_op jit(solution)/shard_map/reduce_scatter | solution.py:226
  431.9 169.5 %reduce-scatter.59.cloned.1.call-start = ((), (), s32[]{:S(2)}) async-start(), calls=%async_computation.44 | async-start | bytes 5898240 | tf_op jit(solution)/shard_map/reduce_scatter | solution.py:281
  439.6 268.1 %reduce-scatter.57.cloned.1.call-start = ((), (), s32[]{:S(2)}) async-start(), calls=%async_computation.43 | async-start | bytes 5898240 | tf_op jit(solution)/shard_map/reduce_scatter | solution.py:281
  447.1 366.8 %reduce-scatter.55.cloned.1.call-start = ((), (), s32[]{:S(2)}) async-start(), calls=%async_computation.42 | async-start | bytes 5898240 | tf_op jit(solution)/shard_map/reduce_scatter | solution.py:281
  454.3 431.1 %reduce-scatter.49.cloned.1.call-start = ((), (), s32[]{:S(2)}) async-start(), calls=%async_computation.39 | async-start | bytes 2359296 | tf_op jit(solution)/shard_map/reduce_scatter | solution.py:281
  459.4 496.5 %reduce-scatter.47.cloned.1.call-start = ((), (), s32[]{:S(2)}) async-start(), calls=%async_computation.38 | async-start | bytes 2359296 | tf_op jit(solution)/shard_map/reduce_scatter | solution.py:281
  466.0 560.4 %reduce-scatter.45.cloned.1.call-start = ((), (), s32[]{:S(2)}) async-start(), calls=%async_computation.37 | async-start | bytes 2359296 | tf_op jit(solution)/shard_map/reduce_scatter | solution.py:281
  472.3 624.5 %reduce-scatter.43.cloned.1.call-start = ((), (), s32[]{:S(2)}) async-start(), calls=%async_computation.36 | async-start | bytes 2359296 | tf_op jit(solution)/shard_map/reduce_scatter | solution.py:281
  476.9 690.9 %reduce-scatter.41.cloned.1.call-start = ((), (), s32[]{:S(2)}) async-start(), calls=%async_computation.35 | async-start | bytes 2359296 | tf_op jit(solution)/shard_map/reduce_scatter | solution.py:281
  481.5 756.9 %reduce-scatter.39.cloned.1.call-start = ((), (), s32[]{:S(2)}) async-start(), calls=%async_computation.34 | async-start | bytes 2359296 | tf_op jit(solution)/shard_map/reduce_scatter | solution.py:281
  485.9 822.9 %reduce-scatter.37.cloned.1.call-start = ((), (), s32[]{:S(2)}) async-start(), calls=%async_computation.33 | async-start | bytes 2359296 | tf_op jit(solution)/shard_map/reduce_scatter | solution.py:281
  490.3 889.0 %reduce-scatter.35.cloned.1.call-start = ((), (), s32[]{:S(2)}) async-start(), calls=%async_computation.32 | async-start | bytes 2359296 | tf_op jit(solution)/shard_map/reduce_scatter | solution.py:281
  494.7 1020.8 %reduce-scatter.61.cloned.1.call-start = ((), (), s32[]{:S(2)}) async-start(), calls=%async_computation.45 | async-start | bytes 1081344
  497.9 1161.5 %reduce-scatter.53.cloned.1.call-start = ((), (), s32[]{:S(2)}) async-start(), calls=%async_computation.41 | async-start | bytes 7028736 | tf_op jit(solution)/shard_map/reduce_scatter | solution.py:281
  (57 other events, 820.6 us)
Sparse Core Ops, SparseCore 0:
  12.9 25.2 all-gather.6
  54.0 31.4 reduce-scatter.22
  126.8 31.4 reduce-scatter.24
  186.6 22.5 all-gather.12
  232.3 31.4 reduce-scatter.28
  268.9 22.5 all-gather.14
  309.0 31.4 reduce-scatter.30
  342.8 31.4 reduce-scatter.26
  378.6 22.6 all-gather.16
  416.0 31.4 reduce-scatter.32
  450.0 44.4 reduce-scatter.50
  498.4 102.9 reduce-scatter.58
  605.3 102.3 reduce-scatter.56
  711.5 102.2 reduce-scatter.54
  817.6 67.6 reduce-scatter.48
  889.1 66.6 reduce-scatter.46
  959.8 66.5 reduce-scatter.44
  1030.2 66.4 reduce-scatter.42
  1100.7 67.0 reduce-scatter.40
  1171.8 66.5 reduce-scatter.38
  1242.3 66.4 reduce-scatter.36
  1312.6 66.5 reduce-scatter.34
  1381.6 133.8 reduce-scatter.60
  1517.7 141.7 reduce-scatter.52
  (2 shorter events, 45.0 us)

commit v2 on v1

v2 whole, which is shorter than its diff:
```python
import jax
import jax.numpy as jnp
from jax import lax
from jax.sharding import PartitionSpec as P

HEAD_DIM = 128
SEGS = 4
EPSILON = 1e-06
MASKED = -1000000000.0
F32 = jnp.float32
BF16 = jnp.bfloat16


def matmul(left, right):
    return jnp.dot(left, right, preferred_element_type=F32)


def product(spec, left, right):
    return jnp.einsum(spec, left, right, preferred_element_type=F32)


def rows_dot(left, right):
    return lax.dot_general(left, right, (((0,), (0,)), ((), ())), preferred_element_type=F32)


def cols_dot(left, right):
    return lax.dot_general(left, right, (((1,), (1,)), ((), ())), preferred_element_type=F32)


def tie(value, after):
    return lax.optimization_barrier((value, after))[0]


def inverse_rms(rows):
    return lax.rsqrt(jnp.mean(rows * rows, axis=-1, keepdims=True) + EPSILON)


def norm_rows(rows, gain):
    return (rows * inverse_rms(rows) * gain).astype(BF16)


def norm_back(rows, gain, grad):
    inv = inverse_rms(rows)
    weighted = gain * grad
    inner = jnp.mean(rows * weighted, axis=-1, keepdims=True)
    grad_rows = inv * weighted - rows * (inv * inv * inv) * inner
    return grad_rows, jnp.sum(grad * rows * inv, axis=0)


def plain_scores(queries, keys, allowed):
    scores = product("shd,thd->hst", queries, keys) * (HEAD_DIM ** (-0.5))
    return jnp.where(allowed[None], scores, MASKED)


def by_head(arr):
    return arr.reshape(arr.shape[0], -1, HEAD_DIM)


def flat_heads(arr):
    return arr.reshape(arr.shape[0], -1).astype(BF16)


def plain_attend(queries, keys, values, allowed):
    scores = plain_scores(by_head(queries), by_head(keys), allowed)
    top = jnp.max(scores, axis=-1, keepdims=True)
    exponent = jnp.exp(scores - top)
    total = jnp.sum(exponent, axis=-1, keepdims=True)
    weights = (exponent / total).astype(BF16)
    return flat_heads(product("hst,thd->shd", weights, by_head(values))), top + jnp.log(total)


def plain_back(queries, keys, values, allowed, log_total, grad_out):
    queries, keys, values, grad_out = [by_head(v) for v in (queries, keys, values, grad_out)]
    weights = jnp.exp(plain_scores(queries, keys, allowed) - log_total)
    grad_weights = product("shd,thd->hst", grad_out, values)
    inner = jnp.sum(weights * grad_weights, axis=-1, keepdims=True)
    grad_scores = (weights * (grad_weights - inner)).astype(BF16)
    scale = HEAD_DIM ** (-0.5)
    grad_queries = product("hst,thd->shd", grad_scores, keys) * scale
    grad_keys = product("hst,shd->thd", grad_scores, queries) * scale
    grad_values = product("hst,shd->thd", weights.astype(BF16), grad_out)
    return [flat_heads(v) for v in (grad_queries, grad_keys, grad_values)]


def gated_unit(gate_arg, up_arg):
    return jax.nn.gelu(gate_arg, approximate=True) * up_arg


def layer(n_dp, n_mp):
    lanes = n_dp // 2
    paired = n_dp == 8

    def swap(value, axis, size, bit):
        return lax.ppermute(value, axis, [(i, i ^ bit) for i in range(size)])

    def core(value):
        return swap(value, "mp", n_mp, 1)

    def chip(value):
        return swap(value, "mp", n_mp, 2)

    def beside(value):
        return swap(value, "dp", n_dp, 1)

    def gather(mine):
        far = chip(mine)
        return jnp.concatenate([mine, far, core(mine), core(far)], axis=0)

    def scatter_rows(partial):
        step = partial.shape[0] // 4
        block = [partial[k * step : (k + 1) * step] for k in range(4)]
        far = (block[1].astype(F32) + core(block[3]).astype(F32)).astype(BF16)
        far_in = chip(far)
        return block[0].astype(F32) + core(block[2]).astype(F32) + far_in.astype(F32)

    def line_place():
        z = lax.axis_index("dp") // 2
        number = lambda value: jnp.asarray(value).astype(jnp.int32)
        return lax.axis_index("dp") % 2, number(z >= 2), number((z == 1) | (z == 2))

    def outer_swap(value):
        return swap(value, "dp", n_dp, 2)

    def inner_swap(value):
        pairs = []
        for d in range(n_dp):
            for m in range(n_mp):
                inner = d // 2 in (1, 2)
                to = (d ^ 6) * n_mp + m if inner else d * n_mp + (m ^ 1)
                pairs.append((d * n_mp + m, to))
        return lax.ppermute(value, ("dp", "mp"), pairs)

    def line_steps(near, far):
        inner = line_place()[2]
        incoming = outer_swap(far)
        yield
        sums = (far.astype(F32) + incoming.astype(F32)).astype(BF16)
        crossed = inner_swap(sums)
        yield
        mine = jnp.where(
                inner == 1,
                (near[:1].astype(F32) + crossed[1:].astype(F32)).astype(BF16),
                near[1:],
            )
        last = outer_swap(mine)
        yield
        total = jnp.where(inner == 1, near[1], near[0]).astype(F32) + last[0].astype(F32)
        return total + jnp.where(inner == 1, crossed[0].astype(F32), 0.0)

    def split_columns(value):
        if not paired:
            return (value,)
        x = lax.axis_index("dp") % 2
        half, width = value.shape[0] // 2, value.shape[1] // n_dp
        wanted = jnp.concatenate(
            [
                jnp.where(
                    x == 0,
                    value[:half, (2 * z + 1) * width : (2 * z + 2) * width],
                    value[:half, 2 * z * width : (2 * z + 1) * width],
                )
                for z in range(lanes)
            ],
            axis=1,
        )
        low = beside(wanted)
        return value, low, core(low)

    def weight_grad(split, grad, rows_first, grad_far=None):
        if paired:
            if grad_far is None:
                grad_far = beside(grad)
            grads = grad if grad.ndim == 3 else grad[None]
            grads_far = grad_far if grad.ndim == 3 else grad_far[None]
            x, flip, inner = line_place()
            own, low, high = split
            half = low.shape[0]
            width = own.shape[1] // 8
            own = jnp.concatenate(
                [
                    jnp.where(
                        x == 0,
                        own[:, 2 * z * width : (2 * z + 1) * width],
                        own[:, (2 * z + 1) * width : (2 * z + 2) * width],
                    )
                    for z in range(4)
                ],
                axis=1,
            )
            part = (
                product("td,nte->dne", own, grads)
                + product("td,nte->dne", low, grads_far[:, :half])
                + product("td,nte->dne", high, grads_far[:, half:])
            ).astype(BF16)
            part = part.reshape(4, width, grads.shape[0], grads.shape[2]).transpose(0, 2, 1, 3)
            near = jnp.where(flip == 1, jnp.stack([part[3], part[2]]), part[:2])
            far = jnp.where(flip == 1, jnp.stack([part[1], part[0]]), part[2:])
            total = yield from line_steps(near, far)
        else:
            grads = grad if grad.ndim == 3 else grad[None]
            partial = product("td,nte->dne", split[0], grads).astype(BF16)
            total = lax.psum_scatter(partial, "dp", scatter_dimension=0, tiled=True)
            total = total.astype(F32).transpose(1, 0, 2)
        return [total[n] if rows_first else total[n].T for n in range(total.shape[0])]

    results = {}

    def advance(name, work):
        try:
            next(work)
        except StopIteration as stop:
            results[name] = stop.value
            return False
        return True

    def total_sum(value):
        for bit in (1, 2):
            value = value + swap(value, "mp", n_mp, bit)
        if not paired:
            return lax.psum(value, "dp")
        for bit in (1, 2, 4):
            value = value + swap(value, "dp", n_dp, bit)
        return value

    def shards(
        tokens, norm_gains, w_query, w_key, w_value, w_out, c_query, c_key, c_value, c_out,
        patch_proj, w_gate, w_up, w_down, patches, segment_ids, image_index, cotangent,
    ):
        length = segment_ids.shape[1]
        model = tokens.shape[2]
        patch_rows = patches.shape[0] * patches.shape[1]
        m = lax.axis_index("mp")
        order = [m, m ^ 2, m ^ 1, m ^ 3]

        def blocks(arr, axis=0):
            step = arr.shape[axis] // 4
            return jnp.concatenate(
                [lax.dynamic_slice_in_dim(arr, k * step, step, axis) for k in order], axis=axis
            )

        places = blocks(jnp.arange(length, dtype=jnp.int32))
        segment_row = blocks(segment_ids[0])
        slots = jnp.arange(SEGS, dtype=jnp.int32)
        token_image = jnp.sum(
            jnp.where(segment_row[:, None] == slots, image_index[0][None, :], 0), axis=-1
        )
        patch_image = blocks(jnp.arange(patch_rows, dtype=jnp.int32) // patches.shape[1])

        residual = tokens[0].astype(F32)
        normed_one = gather(norm_rows(residual, norm_gains[0]))
        patch_own = blocks(patches.reshape(patch_rows, patches.shape[2]))
        projected = gather(matmul(patch_own[: patch_rows // 4], patch_proj).astype(BF16))
        cross_keys = matmul(projected, c_key).astype(BF16)
        cross_values = matmul(projected, c_value).astype(BF16)
        grad_three = gather(cotangent[0])
        grad_hidden = product("sd,fd->sf", grad_three, w_down)
        queries = matmul(normed_one, w_query).astype(BF16)
        key_rows = matmul(normed_one, w_key).astype(BF16)
        value_rows = matmul(normed_one, w_value).astype(BF16)
        self_allowed = (segment_row[:, None] == segment_row[None, :]) & (
            places[None, :] <= places[:, None]
        )
        cross_allowed = token_image[:, None] == patch_image[None, :]
        self_mixed, self_log = plain_attend(queries, key_rows, value_rows, self_allowed)
        after_self = residual + scatter_rows(matmul(self_mixed, w_out).astype(BF16))
        normed_two = gather(norm_rows(after_self, norm_gains[1]))
        cross_queries = matmul(normed_two, c_query).astype(BF16)
        cross_mixed, cross_log = plain_attend(
            cross_queries, cross_keys, cross_values, cross_allowed
        )
        after_cross = after_self + scatter_rows(matmul(cross_mixed, c_out).astype(BF16))
        normed_three = gather(norm_rows(after_cross, norm_gains[2]))
        gate_pre, up_pre = matmul(normed_three, w_gate), matmul(normed_three, w_up)
        hidden, pull = jax.vjp(gated_unit, gate_pre, up_pre)
        hidden = hidden.astype(BF16)
        grad_gate, grad_up = [g.astype(BF16) for g in pull(grad_hidden)]
        results.clear()
        running = []

        def begin(name, *args):
            running.append((name, weight_grad(*args)))
            turn()

        def turn():
            for item in running[:2]:
                if not advance(*item):
                    running.remove(item)

        split_three = split_columns(normed_three)
        if paired:
            hidden_far = beside(hidden)
            gate_far = beside(tie(grad_gate, hidden_far))
            up_far = beside(tie(grad_up, gate_far))
        else:
            hidden_far = gate_far = up_far = None
        grad_normed = scatter_rows(
            (
                product("sf,df->sd", grad_gate, w_gate) + product("sf,df->sd", grad_up, w_up)
            ).astype(BF16)
        )
        begin("down", split_columns(grad_three), hidden, False, hidden_far)
        grad_input, gain_three = norm_back(after_cross, norm_gains[2], grad_normed)
        grad_rows = cotangent[0].astype(F32) + grad_input
        begin("gate", split_three, grad_gate, True, gate_far)

        grad_two = gather(grad_rows.astype(BF16))
        turn()
        grad_mixed = product("sd,ed->se", grad_two, c_out).astype(BF16)
        begin("up", split_three, grad_up, True, up_far)
        grad_cq, grad_ck, grad_cv = plain_back(
            cross_queries, cross_keys, cross_values, cross_allowed, cross_log, grad_mixed
        )
        grad_ckv = jnp.stack([grad_ck, grad_cv])
        output = after_cross + scatter_rows(matmul(hidden, w_down).astype(BF16))
        turn()
        grad_normed = scatter_rows(product("se,de->sd", grad_cq, c_query).astype(BF16))
        grad_input, gain_two = norm_back(after_self, norm_gains[1], grad_normed)
        grad_rows = grad_rows + grad_input
        begin("c_out", split_columns(grad_two), cross_mixed, False)
        begin("c_query", split_columns(normed_two), grad_cq, True)
        begin("c_pair", split_columns(projected), grad_ckv, True)

        grad_one = gather(grad_rows.astype(BF16))
        grad_mixed = product("sd,ed->se", grad_one, w_out).astype(BF16)
        grad_self = jnp.stack(
            plain_back(queries, key_rows, value_rows, self_allowed, self_log, grad_mixed)
        )
        grad_normed = scatter_rows(
            (
                product("se,de->sd", grad_self[0], w_query)
                + product("se,de->sd", grad_self[1], w_key)
                + product("se,de->sd", grad_self[2], w_value)
            ).astype(BF16)
        )
        grad_input, gain_one = norm_back(residual, norm_gains[0], grad_normed)
        grad_rows = grad_rows + grad_input
        gain_total = total_sum(jnp.stack([gain_one, gain_two, gain_three]))
        share = model // (n_dp * n_mp)
        gain_total = lax.dynamic_slice_in_dim(
            gain_total, (lax.axis_index("dp") * n_mp + m) * share, share, 1
        )
        begin("w_out", split_columns(grad_one), self_mixed, False)
        begin("w_qkv", split_columns(normed_one), grad_self, True)

        width = model // (n_dp * n_mp)

        def projected_block(k):
            def rows_of(weight):
                cut = weight.reshape(n_dp, n_mp, width, weight.shape[1])
                return lax.dynamic_index_in_dim(cut, k, 1, keepdims=False).reshape(
                    n_dp * width, weight.shape[1]
                )

            return (
                cols_dot(grad_ckv[0], rows_of(c_key)) + cols_dot(grad_ckv[1], rows_of(c_value))
            ).astype(BF16)

        def swap_blocks(value, size):
            starts = [size * (k ^ 1) for k in range(value.shape[0] // size)]
            return jnp.concatenate([value[at : at + size] for at in starts], axis=0)

        block = [projected_block(k) for k in order]
        half, quarter = patch_rows // 2, patch_rows // 4
        far = block[1].astype(F32) + swap_blocks(core(block[3]), half).astype(F32)
        near = block[0].astype(F32) + swap_blocks(core(block[2]), half).astype(F32)
        grad_projected = near + swap_blocks(chip(far.astype(BF16)), quarter).astype(F32)
        patch_partial = rows_dot(grad_projected.astype(BF16), patch_own).astype(BF16)

        def patch_sum():
            if not paired:
                return lax.psum_scatter(
                    patch_partial, "dp", scatter_dimension=0, tiled=True
                ).astype(F32)
            x = lax.axis_index("dp") % 2
            parts = patch_partial.reshape(lanes, 2, width, patches.shape[2])
            sent = beside(lax.dynamic_index_in_dim(parts, 1 - x, 1, keepdims=False))
            kept = lax.dynamic_index_in_dim(parts, x, 1, keepdims=False)
            summed = (kept.astype(F32) + sent.astype(F32)).astype(BF16)[:, None]
            flip = line_place()[1] == 1
            near, far = (
                jnp.where(flip, jnp.stack([summed[3 - a], summed[3 - b]]), summed[a : b + 1])
                for a, b in ((0, 1), (2, 3))
            )
            total = yield from line_steps(near, far)
            return total[0]

        running.append(("patch", patch_sum()))
        while running:
            turn()
        [sum_down], [sum_gate], [sum_up] = results["down"], results["gate"], results["up"]
        [sum_cout], [sum_cquery], [sum_out] = results["c_out"], results["c_query"], results["w_out"]
        sum_ckey, sum_cvalue = results["c_pair"]
        sum_query, sum_key, sum_value = results["w_qkv"]
        patch_total = results["patch"].T
        return (
            output.astype(BF16)[None], grad_rows[None], gain_total,
            sum_query, sum_key, sum_value, sum_out,
            sum_cquery, sum_ckey, sum_cvalue, sum_cout,
            patch_total, sum_gate, sum_up, sum_down,
        )

    return shards


def solution(mesh):
    columns, rows = P(None, "mp"), P("mp", None)
    return jax.shard_map(
        layer(mesh.shape["dp"], mesh.shape["mp"]),
        mesh=mesh,
        in_specs=(
            P("dp", "mp", None), P(), columns, columns, columns, rows, columns, columns, columns,
            rows, P(), columns, columns, rows, P("dp", None, None), P("dp", None), P("dp", None),
            P("dp", "mp", None),
        ),
        out_specs=(
            P("dp", "mp", None), P("dp", "mp", None), P(None, ("dp", "mp")),
            P("dp", "mp"), P("dp", "mp"), P("dp", "mp"), P("mp", "dp"),
            P("dp", "mp"), P("dp", "mp"), P("dp", "mp"), P("mp", "dp"),
            P(None, ("dp", "mp")), P("dp", "mp"), P("dp", "mp"), P("mp", "dp"),
        ),
        check_vma=False,
    )
```

time: 1680 us -> 680 us (0.40)
  waiting for transfers between devices: 1390 us -> 265 us
  starting transfers between devices: 2.59 us -> 96.2 us
  local copies, waits for them, and re-layouts: 14.5 us -> 47.7 us
  other arithmetic: 58 us -> 90.7 us
  matrix products: 192 us -> 166 us
    reduce_scatter x19 -> x0, waiting for transfers between devices: 1150 us -> none  [the longest x12 998 us: sum_rows(): lax.psum_scatter(partial.astype(jnp.bfloat16), axes, scatter_dimension=di...]
    ppermute x0 -> x97, waiting for transfers between devices: none -> 265 us  [the longest x88 265 us: swap(): return lax.ppermute(value, axis, [(i, i ^ bit) for i in range(size)])]
    unnamed x27 -> x0, waiting for transfers between devices: 133 us -> none
    all_gather x6 -> x0, waiting for transfers between devices: 106 us -> none  [the longest x3 54.5 us: gather_grad(): lax.all_gather(grad_local.astype(jnp.bfloat16), 'mp', axis=1, tiled=True)]
    ppermute x0 -> x97, starting transfers between devices: none -> 96.2 us  [the longest x88 96 us: swap(): return lax.ppermute(value, axis, [(i, i ^ bit) for i in range(size)])]
    select_n x1 -> x39, other arithmetic: 0.01 us -> 27.7 us  [the longest x9 8.85 us: line_steps(): jnp.where(inner == 1, (near[:1].astype(F32) + crossed[1:].astype(F32)).as...]
    dot_general x47 -> x65, matrix products: 192 us -> 166 us  [the longest x45 109 us: product(): return jnp.einsum(spec, left, right, preferred_element_type=F32)]
    convert_element_type x19 -> x23, other arithmetic: 39.6 us -> 18.8 us  [the longest x9 8.63 us: line_steps(): sums = (far.astype(F32) + incoming.astype(F32)).astype(BF16)]
  transfers between devices with their start and end apart: 26 -> 97, of which waited for: 24 -> 29; matrix products, arithmetic and copies ran while one was open for 9% -> 42% of each run, Pallas kernels for 0% -> 0%
where the time goes in v2:
time: 680 us; the launch traced here: 669 us
  waiting for transfers between devices  265 us (39%)
  matrix products  166 us (24%)
  starting transfers between devices  96.2 us (14%)
  other arithmetic  90.7 us (13%)
  local copies, waits for them, and re-layouts  47.7 us (7%)
    ppermute x88, waiting for transfers between devices, swap(): return lax.ppermute(value, axis, [(i, i ^ bit) for i in range(size)])  265 us
    dot_general x45, matrix products, product(): return jnp.einsum(spec, left, right, preferred_element_type=F32)  109 us
    ppermute x88, starting transfers between devices, swap(): return lax.ppermute(value, axis, [(i, i ^ bit) for i in range(size)])  96 us
    dot_general x12, matrix products, matmul(): return jnp.dot(left, right, preferred_element_type=F32)  38.8 us
    unnamed x303, local copies, waits for them, and re-layouts  21.5 us
  transfers between devices with their start and end apart: 97, of which 29 were waited for; matrix products, arithmetic and copies ran while one was open for 42% of the time, Pallas kernels for 0%

profile of v2, /device:TPU:0, one launch (start us, length us, event | category | flops | bytes accessed | tf_op | source)
XLA Modules:
  0.0 669.0 jit_solution(15297942661315120535)
XLA Ops:
  23.8 8.0 %collective-permute-done.21 = bf16[128,2048]{1,0:T(8,128)(2,1)} collective-permute-done((bf16[128,2048]{1,0:T(8,128)(2,1)}, bf16[128,2048]{1,0:T(8,128)(2,1)}, u32[]{:S(2)}, u32[]{:S(2)}) %collective-permute-start.21) | collective-permute-done | bytes 524320 | tf_op jit(solution)/shard_map/ppermute | solution.py:94
  75.1 8.0 %collective-permute-done.9 = bf16[128,2048]{1,0:T(8,128)(2,1)S(1)} collective-permute-done((bf16[128,2048]{1,0:T(8,128)(2,1)S(1)}, bf16[128,2048]{1,0:T(8,128)(2,1)S(1)}, u32[]{:S(2)}, u32[]{:S(2)}) %collective-permute-start.9) | collective-permute-done | bytes 524320 | tf_op jit(solution)/shard_map/ppermute | solution.py:94
  106.5 9.6 %collective-permute-done.14 = bf16[128,2048]{1,0:T(8,128)(2,1)S(1)} collective-permute-done((bf16[128,2048]{1,0:T(8,128)(2,1)S(1)}, bf16[128,2048]{1,0:T(8,128)(2,1)S(1)}, u32[]{:S(2)}, u32[]{:S(2)}) %collective-permute-start.14) | collective-permute-done | bytes 524320 | tf_op jit(solution)/shard_map/ppermute | solution.py:94
  119.6 10.7 %collective-permute-done.15 = bf16[128,2048]{1,0:T(8,128)(2,1)S(1)} collective-permute-done((bf16[128,2048]{1,0:T(8,128)(2,1)S(1)}, bf16[128,2048]{1,0:T(8,128)(2,1)S(1)}, u32[]{:S(2)}, u32[]{:S(2)}) %collective-permute-start.15) | collective-permute-done | bytes 524320 | tf_op jit(solution)/shard_map/ppermute | solution.py:94
  141.2 10.6 %multiply_convert_fusion.2 = (bf16[512,1280]{1,0:T(8,128)(2,1)}, bf16[512,1280]{1,0:T(8,128)(2,1)}, bf16[512,1280]{1,0:T(8,128)(2,1)}) fusion(f32[512,1280]{1,0:T(8,128)} %fusion.238, f32[512,1280]{1,0:T(8,128)} %fusion.237, bf16[1280,2048]{1,0:T(8,128)(2,1)} %param.31, bf16[128,2048]{1,0:T(8,128)(2,1)S(1)} %collective-permute-done.23, ...), kind=kOutput, calls=%fused_computation.68 | convolution fusion | flops 2709782528 | bytes 16515072 | tf_op jit(solution)/shard_map/sd,fd->sf/dot_general | solution.py:19
  188.7 9.0 %collective-permute-done.26 = bf16[128,2048]{1,0:T(8,128)(2,1)S(1)} collective-permute-done((bf16[128,2048]{1,0:T(8,128)(2,1)S(1)}, bf16[128,2048]{1,0:T(8,128)(2,1)S(1)}, u32[]{:S(2)}, u32[]{:S(2)}) %collective-permute-start.26) | collective-permute-done | bytes 524320 | tf_op jit(solution)/shard_map/ppermute | solution.py:94
  199.3 9.0 %collective-permute-done.20 = bf16[128,2048]{1,0:T(8,128)(2,1)S(1)} collective-permute-done((bf16[128,2048]{1,0:T(8,128)(2,1)S(1)}, bf16[128,2048]{1,0:T(8,128)(2,1)S(1)}, u32[]{:S(2)}, u32[]{:S(2)}) %collective-permute-start.20) | collective-permute-done | bytes 524320 | tf_op jit(solution)/shard_map/ppermute | solution.py:94
  216.3 7.7 %collective-permute-done.27 = bf16[128,2048]{1,0:T(8,128)(2,1)S(1)} collective-permute-done((bf16[128,2048]{1,0:T(8,128)(2,1)S(1)}, bf16[128,2048]{1,0:T(8,128)(2,1)S(1)}, u32[]{:S(2)}, u32[]{:S(2)}) %collective-permute-start.27) | collective-permute-done | bytes 524320 | tf_op jit(solution)/shard_map/ppermute | solution.py:94
  276.8 17.7 %collective-permute-done.83 = bf16[512,1280]{1,0:T(8,128)(2,1)S(1)} collective-permute-done((bf16[512,1280]{1,0:T(8,128)(2,1)}, bf16[512,1280]{1,0:T(8,128)(2,1)S(1)}, u32[]{:S(2)}, u32[]{:S(2)}) %collective-permute-start.83) | collective-permute-done | bytes 1310752 | tf_op jit(solution)/shard_map/ppermute | solution.py:94
  298.7 8.7 %collective-permute-done.57 = bf16[512,512]{0,1:T(8,128)(2,1)S(1)} collective-permute-done((bf16[512,512]{0,1:T(8,128)(2,1)S(1)}, bf16[512,512]{0,1:T(8,128)(2,1)S(1)}, u32[]{:S(2)}, u32[]{:S(2)}) %collective-permute-start.57) | collective-permute-done | bytes 524320 | tf_op jit(solution)/shard_map/ppermute | solution.py:94
  320.2 8.7 %collective-permute-done.71 = bf16[2,1,256,512]{3,2,1,0:T(8,128)(2,1)S(1)} collective-permute-done((bf16[2,1,256,512]{3,2,1,0:T(8,128)(2,1)S(1)}, bf16[2,1,256,512]{3,2,1,0:T(8,128)(2,1)S(1)}, u32[]{:S(2)}, u32[]{:S(2)}) %collective-permute-start.71) | collective-permute-done | bytes 524320 | tf_op jit(solution)/shard_map/ppermute | solution.py:94
  334.3 9.7 %collective-permute-done.59 = bf16[2,1,256,512]{3,2,1,0:T(8,128)(2,1)S(1)} collective-permute-done((bf16[2,1,256,512]{3,2,1,0:T(8,128)(2,1)S(1)}, bf16[2,1,256,512]{3,2,1,0:T(8,128)(2,1)S(1)}, u32[]{:S(2)}, u32[]{:S(2)}) %collective-permute-start.59) | collective-permute-done | bytes 524320 | tf_op jit(solution)/shard_map/ppermute | solution.py:94
  346.9 9.4 %collective-permute-done.33 = bf16[128,2048]{1,0:T(8,128)(2,1)S(1)} collective-permute-done((bf16[128,2048]{1,0:T(8,128)(2,1)S(1)}, bf16[128,2048]{1,0:T(8,128)(2,1)S(1)}, u32[]{:S(2)}, u32[]{:S(2)}) %collective-permute-start.33) | collective-permute-done | bytes 524320 | tf_op jit(solution)/shard_map/ppermute | solution.py:94
  368.0 21.5 %collective-permute-done.85 = bf16[2,1,256,1280]{3,2,1,0:T(8,128)(2,1)S(1)} collective-permute-done((bf16[2,1,256,1280]{3,2,1,0:T(8,128)(2,1)S(1)}, bf16[2,1,256,1280]{3,2,1,0:T(8,128)(2,1)S(1)}, u32[]{:S(2)}, u32[]{:S(2)}) %collective-permute-start.85) | collective-permute-done | bytes 1310752 | tf_op jit(solution)/shard_map/ppermute | solution.py:94
  407.6 7.5 %fusion.16 = bf16[512,1664]{1,0:T(8,128)(2,1)} fusion(bf16[256,1664]{1,0:T(8,128)(2,1)} %get-tuple-element.71, bf16[256,1664]{1,0:T(8,128)(2,1)} %get-tuple-element.72, bf16[256,1664]{1,0:T(8,128)(2,1)} %get-tuple-element.70, bf16[256,1664]{1,0:T(8,128)(2,1)} %copy-done.87, bf16[512,512]{1,0:T(8,128)(2,1)} %get-tuple-element.170, ...), kind=kOutput, calls=%fused_computation.53 | convolution fusion | flops 2305622016 | bytes 10878976 | tf_op jit(solution)/shard_map/dot_general | solution.py:23
  417.2 24.2 %collective-permute-done.63 = bf16[2,1024,512]{2,1,0:T(8,128)(2,1)} collective-permute-done((bf16[2,1024,512]{2,1,0:T(8,128)(2,1)}, bf16[2,1024,512]{2,1,0:T(8,128)(2,1)}, u32[]{:S(2)}, u32[]{:S(2)}) %collective-permute-start.63) | collective-permute-done | bytes 2097184 | tf_op jit(solution)/shard_map/ppermute | solution.py:94
  505.9 8.2 %collective-permute-done.38 = bf16[128,2048]{1,0:T(8,128)(2,1)S(1)} collective-permute-done((bf16[128,2048]{1,0:T(8,128)(2,1)S(1)}, bf16[128,2048]{1,0:T(8,128)(2,1)S(1)}, u32[]{:S(2)}, u32[]{:S(2)}) %collective-permute-start.38) | collective-permute-done | bytes 524320 | tf_op jit(solution)/shard_map/ppermute | solution.py:94
  525.7 7.3 %collective-permute-done.53 = bf16[2,1,256,512]{3,2,1,0:T(8,128)(2,1)S(1)} collective-permute-done((bf16[2,1,256,512]{3,2,1,0:T(8,128)(2,1)S(1)}, bf16[2,1,256,512]{3,2,1,0:T(8,128)(2,1)S(1)}, u32[]{:S(2)}, u32[]{:S(2)}) %collective-permute-start.53) | collective-permute-done | bytes 524320 | tf_op jit(solution)/shard_map/ppermute | solution.py:94
  558.4 13.3 %collective-permute-done.43 = f32[3,2048]{1,0:T(4,128)S(1)} collective-permute-done((f32[3,2048]{1,0:T(4,128)S(1)}, f32[3,2048]{1,0:T(4,128)S(1)}, u32[]{:S(2)}, u32[]{:S(2)}) %collective-permute-start.43) | collective-permute-done | bytes 24608 | tf_op jit(solution)/shard_map/ppermute | solution.py:94
  572.5 8.9 %collective-permute-start.55 = (bf16[1,1,256,512]{3,2,1,0:T(8,128)(2,1)S(1)}, bf16[1,1,256,512]{3,2,1,0:T(8,128)(2,1)S(1)}, u32[]{:S(2)}, u32[]{:S(2)}) collective-permute-start(bf16[1,1,256,512]{3,2,1,0:T(8,128)(2,1)S(1)} %fusion.143), channel_id=1, source_target_pairs={{0,8},{4,12},{8,0},{12,4},{16,24},{20,28},{24,16},{28,20},{1,9},{5... | collective-permute-start | bytes 786440 | tf_op jit(solution)/shard_map/ppermute | solution.py:94
  582.2 25.3 %collective-permute-done.87 = bf16[1,1,256,1280]{3,2,1,0:T(8,128)(2,1)S(1)} collective-permute-done((bf16[1,1,256,1280]{3,2,1,0:T(8,128)(2,1)S(1)}, bf16[1,1,256,1280]{3,2,1,0:T(8,128)(2,1)S(1)}, u32[]{:S(2)}, u32[]{:S(2)}) %collective-permute-start.87) | collective-permute-done | bytes 655392 | tf_op jit(solution)/shard_map/ppermute | solution.py:94
  624.2 11.4 %collective-permute-done.67 = bf16[1,2,256,512]{3,2,1,0:T(8,128)(2,1)S(1)} collective-permute-done((bf16[1,2,256,512]{3,2,1,0:T(8,128)(2,1)S(1)}, bf16[1,2,256,512]{3,2,1,0:T(8,128)(2,1)S(1)}, u32[]{:S(2)}, u32[]{:S(2)}) %collective-permute-start.67) | collective-permute-done | bytes 524320 | tf_op jit(solution)/shard_map/ppermute | solution.py:94
  638.4 12.0 %collective-permute-start.49 = (bf16[1,3,256,512]{3,2,1,0:T(8,128)(2,1)S(1)}, bf16[1,3,256,512]{3,2,1,0:T(8,128)(2,1)S(1)}, u32[]{:S(2)}, u32[]{:S(2)}) collective-permute-start(bf16[1,3,256,512]{3,2,1,0:T(8,128)(2,1)S(1)} %fusion.113), channel_id=1, source_target_pairs={{0,8},{4,12},{8,0},{12,4},{16,24},{20,28},{24,16},{28,20},{1,9},{5... | collective-permute-start | bytes 2359304 | tf_op jit(solution)/shard_map/ppermute | solution.py:94
  654.0 11.8 %collective-permute-done.49 = bf16[1,3,256,512]{3,2,1,0:T(8,128)(2,1)S(1)} collective-permute-done((bf16[1,3,256,512]{3,2,1,0:T(8,128)(2,1)S(1)}, bf16[1,3,256,512]{3,2,1,0:T(8,128)(2,1)S(1)}, u32[]{:S(2)}, u32[]{:S(2)}) %collective-permute-start.49) | collective-permute-done | bytes 786464 | tf_op jit(solution)/shard_map/ppermute | solution.py:94
  (705 shorter events, 387.2 us)
Async XLA Ops:
  7.8 48.2 %collective-permute-start.22 = (bf16[128,2048]{1,0:T(8,128)(2,1)}, bf16[128,2048]{1,0:T(8,128)(2,1)}, u32[]{:S(2)}, u32[]{:S(2)}) collective-permute-start(bf16[128,2048]{1,0:T(8,128)(2,1)} %bitcast.408), channel_id=1, source_target_pairs={{0,1},{1,0},{2,3},{3,2},{4,5},{5,4},{6,7},{7,6},{8,9},{9,8},{10,11... | collective-permute-start | bytes 1572872 | tf_op jit(solution)/shard_map/ppermute | solution.py:94
  16.4 39.9 %collective-permute-start.6 = (bf16[256,2048]{1,0:T(8,128)(2,1)}, bf16[256,2048]{1,0:T(8,128)(2,1)}, u32[]{:S(2)}, u32[]{:S(2)}) collective-permute-start(bf16[256,2048]{1,0:T(8,128)(2,1)} %convolution_convert_fusion.4), channel_id=1, source_target_pairs={{0,2},{1,3},{2,0},{3,1},{4,6},{5,7},{6,4},{7,5},{8,10},{9,11},{10,... | collective-permute-start | bytes 3145736 | tf_op jit(solution)/shard_map/ppermute | solution.py:94
  56.3 128.4 %collective-permute-start.92 = (bf16[256,1024]{1,0:T(8,128)(2,1)S(1)}, bf16[256,1024]{1,0:T(8,128)(2,1)S(1)}, u32[]{:S(2)}, u32[]{:S(2)}) collective-permute-start(bf16[256,1024]{1,0:T(8,128)(2,1)S(1)} %pad_maximum_fusion.16), channel_id=1, source_target_pairs={{0,4},{4,0},{8,12},{12,8},{16,20},{20,16},{24,28},{28,24},{1,5},{5... | collective-permute-start | bytes 1572872 | tf_op jit(solution)/shard_map/ppermute | solution.py:94
  151.8 59.1 %collective-permute-start.82 = (bf16[512,1280]{1,0:T(8,128)(2,1)}, bf16[512,1280]{1,0:T(8,128)(2,1)S(1)}, u32[]{:S(2)}, u32[]{:S(2)}) collective-permute-start(bf16[512,1280]{1,0:T(8,128)(2,1)} %get-tuple-element.65), channel_id=1, source_target_pairs={{0,4},{4,0},{8,12},{12,8},{16,20},{20,16},{24,28},{28,24},{1,5},{5... | collective-permute-start | bytes 3932168 | tf_op jit(solution)/shard_map/ppermute | solution.py:94
  188.1 212.5 %collective-permute-start.44 = (bf16[256,1024]{1,0:T(8,128)(2,1)}, bf16[256,1024]{1,0:T(8,128)(2,1)}, u32[]{:S(2)}, u32[]{:S(2)}) collective-permute-start(bf16[256,1024]{1,0:T(8,128)(2,1)} %pad_maximum_fusion.11), channel_id=1, source_target_pairs={{0,4},{4,0},{8,12},{12,8},{16,20},{20,16},{24,28},{28,24},{1,5},{5... | collective-permute-start | bytes 1572872 | tf_op jit(solution)/shard_map/ppermute | solution.py:94
  226.3 37.3 %collective-permute-start.69 = (bf16[512,512]{0,1:T(8,128)(2,1)}, bf16[512,512]{0,1:T(8,128)(2,1)}, u32[]{:S(2)}, u32[]{:S(2)}) collective-permute-start(bf16[512,512]{0,1:T(8,128)(2,1)} %bitcast.19), channel_id=1, source_target_pairs={{0,4},{4,0},{8,12},{12,8},{16,20},{20,16},{24,28},{28,24},{1,5},{5... | collective-permute-start | bytes 1572872 | tf_op jit(solution)/shard_map/ppermute | solution.py:94
  227.8 81.4 %collective-permute-start.58 = (bf16[256,1024]{1,0:T(8,128)(2,1)}, bf16[256,1024]{1,0:T(8,128)(2,1)}, u32[]{:S(2)}, u32[]{:S(2)}) collective-permute-start(bf16[256,1024]{1,0:T(8,128)(2,1)} %collective-permute-done.56), channel_id=1, source_target_pairs={{0,1},{1,0},{2,3},{3,2},{4,5},{5,4},{6,7},{7,6},{8,9},{9,8},{10,11... | collective-permute-start | bytes 1572872 | tf_op jit(solution)/shard_map/ppermute | solution.py:94
  228.0 68.9 %collective-permute-start.84 = (bf16[256,1024]{1,0:T(8,128)(2,1)S(1)}, bf16[256,1024]{1,0:T(8,128)(2,1)S(1)}, u32[]{:S(2)}, u32[]{:S(2)}) collective-permute-start(bf16[256,1024]{1,0:T(8,128)(2,1)S(1)} %collective-permute-done.81), channel_id=1, source_target_pairs={{0,1},{1,0},{2,3},{3,2},{4,5},{5,4},{6,7},{7,6},{8,9},{9,8},{10,11... | collective-permute-start | bytes 1572872 | tf_op jit(solution)/shard_map/ppermute | solution.py:94
  273.5 41.0 %collective-permute-start.94 = (bf16[2,1,256,1280]{3,2,1,0:T(8,128)(2,1)S(1)}, bf16[2,1,256,1280]{3,2,1,0:T(8,128)(2,1)S(1)}, u32[]{:S(2)}, u32[]{:S(2)}) collective-permute-start(bf16[2,1,256,1280]{3,2,1,0:T(8,128)(2,1)S(1)} %copy-done.80), channel_id=1, source_target_pairs={{0,8},{4,12},{8,0},{12,4},{16,24},{20,28},{24,16},{28,20},{1,9},{5... | collective-permute-start | bytes 3932168 | tf_op jit(solution)/shard_map/ppermute | solution.py:94
  307.4 38.3 %collective-permute-start.74 = (bf16[1024,512]{1,0:T(8,128)(2,1)S(1)}, bf16[1024,512]{1,0:T(8,128)(2,1)S(1)}, u32[]{:S(2)}, u32[]{:S(2)}) collective-permute-start(bf16[1024,512]{1,0:T(8,128)(2,1)S(1)} %copy-done.83), channel_id=1, source_target_pairs={{0,1},{1,0},{2,3},{3,2},{4,5},{5,4},{6,7},{7,6},{8,9},{9,8},{10,11... | collective-permute-start | bytes 3145736 | tf_op jit(solution)/shard_map/ppermute | solution.py:94
  356.4 45.8 %collective-permute-start.62 = (bf16[512,1024]{1,0:T(8,128)(2,1)}, bf16[512,1024]{1,0:T(8,128)(2,1)}, u32[]{:S(2)}, u32[]{:S(2)}) collective-permute-start(bf16[512,1024]{1,0:T(8,128)(2,1)} %pad_maximum_fusion.9), channel_id=1, source_target_pairs={{0,4},{4,0},{8,12},{12,8},{16,20},{20,16},{24,28},{28,24},{1,5},{5... | collective-permute-start | bytes 3145736 | tf_op jit(solution)/shard_map/ppermute | solution.py:94
  362.3 42.6 %collective-permute-start.76 = (bf16[1024,512]{1,0:T(8,128)(2,1)}, bf16[1024,512]{1,0:T(8,128)(2,1)}, u32[]{:S(2)}, u32[]{:S(2)}) collective-permute-start(bf16[1024,512]{1,0:T(8,128)(2,1)} %add_convert_fusion.12), channel_id=1, source_target_pairs={{0,2},{1,3},{2,0},{3,1},{4,6},{5,7},{6,4},{7,5},{8,10},{9,11},{10,... | collective-permute-start | bytes 3145736 | tf_op jit(solution)/shard_map/ppermute | solution.py:94
  392.6 48.9 %collective-permute-start.63 = (bf16[2,1024,512]{2,1,0:T(8,128)(2,1)}, bf16[2,1024,512]{2,1,0:T(8,128)(2,1)}, u32[]{:S(2)}, u32[]{:S(2)}) collective-permute-start(bf16[2,1024,512]{2,1,0:T(8,128)(2,1)} %pad_maximum_fusion.7), channel_id=1, source_target_pairs={{0,4},{4,0},{8,12},{12,8},{16,20},{20,16},{24,28},{28,24},{1,5},{5... | collective-permute-start | bytes 6291464 | tf_op jit(solution)/shard_map/ppermute | solution.py:94
  400.6 74.3 %collective-permute-start.51 = (bf16[512,512]{0,1:T(8,128)(2,1)}, bf16[512,512]{0,1:T(8,128)(2,1)}, u32[]{:S(2)}, u32[]{:S(2)}) collective-permute-start(bf16[512,512]{0,1:T(8,128)(2,1)} %bitcast.479), channel_id=1, source_target_pairs={{0,4},{4,0},{8,12},{12,8},{16,20},{20,16},{24,28},{28,24},{1,5},{5... | collective-permute-start | bytes 1572872 | tf_op jit(solution)/shard_map/ppermute | solution.py:94
  402.1 149.8 %collective-permute-start.46 = (bf16[256,1024]{1,0:T(8,128)(2,1)}, bf16[256,1024]{1,0:T(8,128)(2,1)}, u32[]{:S(2)}, u32[]{:S(2)}) collective-permute-start(bf16[256,1024]{1,0:T(8,128)(2,1)} %collective-permute-done.44), channel_id=1, source_target_pairs={{0,1},{1,0},{2,3},{3,2},{4,5},{5,4},{6,7},{7,6},{8,9},{9,8},{10,11... | collective-permute-start | bytes 1572872 | tf_op jit(solution)/shard_map/ppermute | solution.py:94
  402.9 42.9 %collective-permute-start.64 = (bf16[512,1024]{1,0:T(8,128)(2,1)}, bf16[512,1024]{1,0:T(8,128)(2,1)}, u32[]{:S(2)}, u32[]{:S(2)}) collective-permute-start(bf16[512,1024]{1,0:T(8,128)(2,1)} %collective-permute-done.62), channel_id=1, source_target_pairs={{0,1},{1,0},{2,3},{3,2},{4,5},{5,4},{6,7},{7,6},{8,9},{9,8},{10,11... | collective-permute-start | bytes 3145736 | tf_op jit(solution)/shard_map/ppermute | solution.py:94
  404.8 45.8 %collective-permute-start.34 = (bf16[128,2048]{1,0:T(8,128)(2,1)S(1)}, bf16[128,2048]{1,0:T(8,128)(2,1)}, u32[]{:S(2)}, u32[]{:S(2)}) collective-permute-start(bf16[128,2048]{1,0:T(8,128)(2,1)S(1)} %copy-done.34), channel_id=1, source_target_pairs={{0,1},{1,0},{2,3},{3,2},{4,5},{5,4},{6,7},{7,6},{8,9},{9,8},{10,11... | collective-permute-start | bytes 1572872 | tf_op jit(solution)/shard_map/ppermute | solution.py:94
  452.5 47.3 %collective-permute-start.89 = (bf16[2,1,256,1280]{3,2,1,0:T(8,128)(2,1)}, bf16[2,1,256,1280]{3,2,1,0:T(8,128)(2,1)}, u32[]{:S(2)}, u32[]{:S(2)}) collective-permute-start(bf16[2,1,256,1280]{3,2,1,0:T(8,128)(2,1)} %maximum_select_fusion.3), channel_id=1, source_target_pairs={{0,8},{4,12},{8,0},{12,4},{16,24},{20,28},{24,16},{28,20},{1,9},{5... | collective-permute-start | bytes 3932168 | tf_op jit(solution)/shard_map/ppermute | solution.py:94
  474.9 42.2 %collective-permute-start.86 = (bf16[2,1,256,1280]{3,2,1,0:T(8,128)(2,1)}, bf16[2,1,256,1280]{3,2,1,0:T(8,128)(2,1)}, u32[]{:S(2)}, u32[]{:S(2)}) collective-permute-start(bf16[2,1,256,1280]{3,2,1,0:T(8,128)(2,1)} %add_convert_fusion.10), channel_id=1, source_target_pairs={{0,1},{1,0},{2,3},{3,2},{4,5},{5,4},{6,7},{7,6},{8,16},{9,17},{10,... | collective-permute-start | bytes 3932168 | tf_op jit(solution)/shard_map/ppermute | solution.py:131
  504.3 45.4 %collective-permute-start.45 = (bf16[3,512,512]{2,1,0:T(8,128)(2,1)S(1)}, bf16[3,512,512]{2,1,0:T(8,128)(2,1)S(1)}, u32[]{:S(2)}, u32[]{:S(2)}) collective-permute-start(bf16[3,512,512]{2,1,0:T(8,128)(2,1)S(1)} %copy-done.79), channel_id=1, source_target_pairs={{0,4},{4,0},{8,12},{12,8},{16,20},{20,16},{24,28},{28,24},{1,5},{5... | collective-permute-start | bytes 4718600 | tf_op jit(solution)/shard_map/ppermute | solution.py:94
  525.6 95.1 %collective-permute-start.90 = (bf16[2,1,256,1280]{3,2,1,0:T(8,128)(2,1)}, bf16[2,1,256,1280]{3,2,1,0:T(8,128)(2,1)}, u32[]{:S(2)}, u32[]{:S(2)}) collective-permute-start(bf16[2,1,256,1280]{3,2,1,0:T(8,128)(2,1)} %add_convert_fusion.9), channel_id=1, source_target_pairs={{0,1},{1,0},{2,3},{3,2},{4,5},{5,4},{6,7},{7,6},{8,16},{9,17},{10,... | collective-permute-start | bytes 3932168 | tf_op jit(solution)/shard_map/ppermute | solution.py:131
  555.4 54.5 %collective-permute-start.47 = (bf16[2,3,256,512]{3,2,1,0:T(8,128)(2,1)S(1)}, bf16[2,3,256,512]{3,2,1,0:T(8,128)(2,1)S(1)}, u32[]{:S(2)}, u32[]{:S(2)}) collective-permute-start(bf16[2,3,256,512]{3,2,1,0:T(8,128)(2,1)S(1)} %get-tuple-element.75), channel_id=1, source_target_pairs={{0,8},{4,12},{8,0},{12,4},{16,24},{20,28},{24,16},{28,20},{1,9},{5... | collective-permute-start | bytes 4718600 | tf_op jit(solution)/shard_map/ppermute | solution.py:94
  572.4 46.7 %collective-permute-start.66 = (bf16[2,2,256,512]{3,2,1,0:T(8,128)(2,1)}, bf16[2,2,256,512]{3,2,1,0:T(8,128)(2,1)}, u32[]{:S(2)}, u32[]{:S(2)}) collective-permute-start(bf16[2,2,256,512]{3,2,1,0:T(8,128)(2,1)} %add_convert_fusion.18), channel_id=1, source_target_pairs={{0,1},{1,0},{2,3},{3,2},{4,5},{5,4},{6,7},{7,6},{8,16},{9,17},{10,... | collective-permute-start | bytes 3145736 | tf_op jit(solution)/shard_map/ppermute | solution.py:131
  572.5 40.5 %collective-permute-start.55 = (bf16[1,1,256,512]{3,2,1,0:T(8,128)(2,1)S(1)}, bf16[1,1,256,512]{3,2,1,0:T(8,128)(2,1)S(1)}, u32[]{:S(2)}, u32[]{:S(2)}) collective-permute-start(bf16[1,1,256,512]{3,2,1,0:T(8,128)(2,1)S(1)} %fusion.143), channel_id=1, source_target_pairs={{0,8},{4,12},{8,0},{12,4},{16,24},{20,28},{24,16},{28,20},{1,9},{5... | collective-permute-start | bytes 786440 | tf_op jit(solution)/shard_map/ppermute | solution.py:94
  (223 other events, 2607.4 us)

commit v3 on v2

v3 whole, which is shorter than its diff:
```python
import functools

import jax
import jax.numpy as jnp
from jax import lax
from jax.experimental import pallas as pl
from jax.experimental.pallas import tpu as pltpu
from jax.sharding import PartitionSpec as P

HEAD_DIM = 128
SEGS = 4
EPSILON = 1e-06
MASKED = -1000000000.0
F32 = jnp.float32
BF16 = jnp.bfloat16


def matmul(left, right):
    return jnp.dot(left, right, preferred_element_type=F32)


def product(spec, left, right):
    return jnp.einsum(spec, left, right, preferred_element_type=F32)


def rows_dot(left, right):
    return lax.dot_general(left, right, (((0,), (0,)), ((), ())), preferred_element_type=F32)


def cols_dot(left, right):
    return lax.dot_general(left, right, (((1,), (1,)), ((), ())), preferred_element_type=F32)


def tie(value, after):
    return lax.optimization_barrier((value, after))[0]


def inverse_rms(rows):
    return lax.rsqrt(jnp.mean(rows * rows, axis=-1, keepdims=True) + EPSILON)


def norm_rows(rows, gain):
    return (rows * inverse_rms(rows) * gain).astype(BF16)


def norm_back(rows, gain, grad):
    inv = inverse_rms(rows)
    weighted = gain * grad
    inner = jnp.mean(rows * weighted, axis=-1, keepdims=True)
    grad_rows = inv * weighted - rows * (inv * inv * inv) * inner
    return grad_rows, jnp.sum(grad * rows * inv, axis=0)


def plain_scores(queries, keys, allowed):
    scores = product("shd,thd->hst", queries, keys) * (HEAD_DIM ** (-0.5))
    return jnp.where(allowed[None], scores, MASKED)


def by_head(arr):
    return arr.reshape(arr.shape[0], -1, HEAD_DIM)


def flat_heads(arr):
    return arr.reshape(arr.shape[0], -1).astype(BF16)


def plain_attend(queries, keys, values, allowed):
    scores = plain_scores(by_head(queries), by_head(keys), allowed)
    top = jnp.max(scores, axis=-1, keepdims=True)
    exponent = jnp.exp(scores - top)
    total = jnp.sum(exponent, axis=-1, keepdims=True)
    weights = (exponent / total).astype(BF16)
    return flat_heads(product("hst,thd->shd", weights, by_head(values))), top + jnp.log(total)


def plain_back(queries, keys, values, allowed, log_total, grad_out):
    queries, keys, values, grad_out = [by_head(v) for v in (queries, keys, values, grad_out)]
    weights = jnp.exp(plain_scores(queries, keys, allowed) - log_total)
    grad_weights = product("shd,thd->hst", grad_out, values)
    inner = jnp.sum(weights * grad_weights, axis=-1, keepdims=True)
    grad_scores = (weights * (grad_weights - inner)).astype(BF16)
    scale = HEAD_DIM ** (-0.5)
    grad_queries = product("hst,thd->shd", grad_scores, keys) * scale
    grad_keys = product("hst,shd->thd", grad_scores, queries) * scale
    grad_values = product("hst,shd->thd", weights.astype(BF16), grad_out)
    return [flat_heads(v) for v in (grad_queries, grad_keys, grad_values)]


VMEM_LIMIT = 20 * 2**20
ANY = pl.BlockSpec(memory_space=pl.ANY)


def params(grid_rank):
    return pltpu.CompilerParams(
        dimension_semantics=("arbitrary",) * grid_rank, vmem_limit_bytes=VMEM_LIMIT
    )


def cost(flops, size):
    return pl.CostEstimate(flops=flops, bytes_accessed=size, transcendentals=0)


def assemble_kernel(*refs):
    *blocks, out_ref = refs
    step = blocks[0].shape[0]
    for k, block in enumerate(blocks):
        out_ref[k * step : (k + 1) * step] = block[...]


def assemble(blocks):
    step, width = blocks[0].shape
    columns = 512
    return pl.pallas_call(
        assemble_kernel,
        grid=(width // columns,),
        in_specs=[pl.BlockSpec((step, columns), lambda j: (0, j))] * len(blocks),
        out_specs=pl.BlockSpec((len(blocks) * step, columns), lambda j: (0, j)),
        out_shape=jax.ShapeDtypeStruct((len(blocks) * step, width), blocks[0].dtype),
        compiler_params=params(1),
        cost_estimate=cost(0, 4 * len(blocks) * step * width),
    )(*blocks)


def copy_kernel(at_ref, in_ref, out_ref):
    out_ref[...] = in_ref[...]


def pick_rows(at, arr, step):
    count, width = at.shape[0], arr.shape[1]
    return pl.pallas_call(
        copy_kernel,
        grid_spec=pltpu.PrefetchScalarGridSpec(
            num_scalar_prefetch=1,
            grid=(count,),
            in_specs=[pl.BlockSpec((step, width), lambda k, at: (at[k], 0))],
            out_specs=pl.BlockSpec((step, width), lambda k, at: (k, 0)),
        ),
        out_shape=jax.ShapeDtypeStruct((count * step, width), arr.dtype),
        compiler_params=params(1),
        cost_estimate=cost(0, 4 * count * step * width),
    )(at, arr)


def pick_columns(at, arr, rows, width):
    count = at.shape[0]
    return pl.pallas_call(
        copy_kernel,
        grid_spec=pltpu.PrefetchScalarGridSpec(
            num_scalar_prefetch=1,
            grid=(count,),
            in_specs=[pl.BlockSpec((rows, width), lambda k, at: (0, at[k]))],
            out_specs=pl.BlockSpec((rows, width), lambda k, at: (0, k)),
        ),
        out_shape=jax.ShapeDtypeStruct((rows, count * width), arr.dtype),
        compiler_params=params(1),
        cost_estimate=cost(0, 4 * count * rows * width),
    )(at, arr)


def add_kernel(left_ref, right_ref, out_ref):
    out_ref[...] = (left_ref[...].astype(F32) + right_ref[...].astype(F32)).astype(BF16)


def add_swapped(left, right, size):
    width = left.shape[1]
    block = pl.BlockSpec((size, width), lambda k: (k, 0))
    return pl.pallas_call(
        add_kernel,
        grid=(left.shape[0] // size,),
        in_specs=[block, pl.BlockSpec((size, width), lambda k: (k + 1 - 2 * (k % 2), 0))],
        out_specs=block,
        out_shape=jax.ShapeDtypeStruct(left.shape, BF16),
        compiler_params=params(1),
        cost_estimate=cost(left.size, 6 * left.size),
    )(left, right)


def pair_kernel(at_ref, a_ref, lo_ref, hi_ref, g_ref, far_ref, *rest):
    half = lo_ref.shape[0]
    total = rows_dot(a_ref[...], g_ref[...])
    total += rows_dot(lo_ref[...], far_ref[:half])
    total += rows_dot(hi_ref[...], far_ref[half:])
    rest[-1][0] = total.astype(BF16)


def pair_grad(at, own, low, high, grad, grad_far, after):
    length, units = grad.shape
    width = own.shape[1] // 8
    whole = pl.BlockSpec((length, units), lambda k, at: (0, 0))
    side = pl.BlockSpec((length // 2, width), lambda k, at: (0, k))
    return pl.pallas_call(
        pair_kernel,
        grid_spec=pltpu.PrefetchScalarGridSpec(
            num_scalar_prefetch=1,
            grid=(4,),
            in_specs=[
                pl.BlockSpec((length, width), lambda k, at: (0, at[k])), side, side, whole, whole,
            ] + [ANY] * len(after),
            out_specs=pl.BlockSpec((1, width, units), lambda k, at: (k, 0, 0)),
        ),
        out_shape=jax.ShapeDtypeStruct((4, width, units), BF16),
        compiler_params=params(1),
        cost_estimate=cost(
            16 * length * width * units, 2 * units * (2 * length + 4 * width) + 16 * length * width
        ),
    )(at, own, low, high, grad, grad_far, *after)


def merge_kernel(in_ref, part_ref, out_ref):
    keep = jnp.where(pl.program_id(0) > 0, in_ref[...].astype(F32), 0.0)
    out_ref[...] = (part_ref[...].astype(F32) + keep).astype(BF16)


def merge(part, incoming):
    block = (1,) + part.shape[1:]
    return pl.pallas_call(
        merge_kernel,
        grid=(4,),
        in_specs=[
            pl.BlockSpec(block, lambda k: (jnp.maximum(k - 1, 0), 0, 0)),
            pl.BlockSpec(block, lambda k: (k, 0, 0)),
        ],
        out_specs=pl.BlockSpec(block, lambda k: (k, 0, 0)),
        out_shape=jax.ShapeDtypeStruct(part.shape, BF16),
        compiler_params=params(1),
        cost_estimate=cost(part.size, 6 * part.size),
    )(incoming, part)


def cross_kernel(at_ref, part_ref, in_ref, out_ref):
    keep = jnp.where(at_ref[0] == 1, in_ref[...].astype(F32), 0.0)
    out_ref[...] = (part_ref[...].astype(F32) + keep).astype(BF16)


def cross_add(inner, part, crossed):
    block = (1,) + part.shape[1:]
    return pl.pallas_call(
        cross_kernel,
        grid_spec=pltpu.PrefetchScalarGridSpec(
            num_scalar_prefetch=1,
            grid=(2,),
            in_specs=[
                pl.BlockSpec(block, lambda k, at: (k, 0, 0)),
                pl.BlockSpec(block, lambda k, at: (1 - k, 0, 0)),
            ],
            out_specs=pl.BlockSpec(block, lambda k, at: (k, 0, 0)),
        ),
        out_shape=jax.ShapeDtypeStruct((2,) + part.shape[1:], BF16),
        compiler_params=params(1),
        cost_estimate=cost(crossed.size, 6 * crossed.size),
    )(inner, part, crossed)


def add_rows(target, *sources):
    step = 32

    def body(i, carry):
        rows = pl.ds(pl.multiple_of(i * step, step), step)
        total = sources[0][rows].astype(F32)
        for source in sources[1:]:
            total = total + source[rows].astype(F32)
        target[rows] = total.astype(target.dtype)
        return carry

    lax.fori_loop(0, target.shape[0] // step, body, 0)


def line_kernel(ready, count, *refs):
    parts, outs, refs = refs[:count], refs[count : 2 * count], refs[2 * count :]
    late = range(ready, count)
    from_outer = dict(zip(late, refs[: count - ready]))
    refs = refs[count - ready :]
    from_inner = dict(zip(late, refs[: count - ready]))
    refs = refs[count - ready :]
    last, refs = refs[:count], refs[count:]
    send_out, got_out, send_in, got_in, send_last, got_last = refs
    dp, mp = lax.axis_index("dp"), lax.axis_index("mp")
    z, x = dp // 2, dp % 2
    beside = ((z + 1 - 2 * (z % 2)) * 2 + x, mp)
    across = ((3 - z) * 2 + x, mp)
    inner = (z == 1) | (z == 2)
    outer = (z == 0) | (z == 3)
    where = pl.DeviceIdType.MESH
    barrier = pltpu.get_barrier_semaphore()
    pl.semaphore_signal(barrier, inc=1, device_id=beside, device_id_type=where)

    def copy(source, target, sent, got, device):
        return pltpu.make_async_remote_copy(
            src_ref=source, dst_ref=target, send_sem=sent, recv_sem=got,
            device_id=device, device_id_type=where,
        )

    def copy_out(g):
        return copy(
            parts[g].at[pl.ds(1, 3)], from_outer[g], send_out.at[g], got_out.at[g], beside
        )

    def copy_in(g):
        return copy(
            from_outer[g].at[pl.ds(1, 2)], from_inner[g], send_in.at[g], got_in.at[g], across
        )

    def copy_last(g):
        source = parts[g].at[0] if g < ready else from_inner[g].at[1]
        return copy(source, last[g], send_last.at[g], got_last.at[g], beside)

    @pl.when(outer)
    def _():
        pl.semaphore_wait(barrier, 1)
        for g in late:
            copy_out(g).start()
        for g in range(count):
            copy_last(g).wait_recv()
            add_rows(outs[g], parts[g].at[0], last[g])
        for g in late:
            copy_out(g).wait_send()

    @pl.when(inner)
    def _():
        pl.semaphore_signal(barrier, inc=1, device_id=across, device_id_type=where)
        pl.semaphore_wait(barrier, 2)
        for g in range(ready):
            copy_last(g).start()

        def finish(g):
            copy_in(g).wait_recv()
            add_rows(outs[g], parts[g].at[1], from_outer[g].at[0], from_inner[g].at[0])
            add_rows(from_inner[g].at[1], parts[g].at[0], from_inner[g].at[1])
            copy_last(g).start()

        for g in range(ready):
            add_rows(outs[g], parts[g].at[1])
        for g in late:
            copy_out(g).wait_recv()
            for k in (1, 2):
                add_rows(from_outer[g].at[k], parts[g].at[k + 1], from_outer[g].at[k])
            copy_in(g).start()
            if g > ready:
                finish(g - 1)
        finish(count - 1)
        for g in late:
            copy_in(g).wait_send()
        for g in range(count):
            copy_last(g).wait_send()


def line_sums(ready_parts, late_parts):
    parts = list(ready_parts) + list(late_parts)
    ready, count = len(ready_parts), len(parts)
    vmem = pl.BlockSpec(memory_space=pltpu.VMEM)
    blocks = lambda size, arr: pltpu.VMEM((size,) + arr.shape[1:], BF16)
    size = sum(p.size for p in parts)
    return pl.pallas_call(
        functools.partial(line_kernel, ready, count),
        in_specs=[vmem] * count,
        out_specs=[vmem] * count,
        out_shape=[jax.ShapeDtypeStruct(p.shape[1:], F32) for p in parts],
        scratch_shapes=[blocks(3, p) for p in late_parts]
        + [blocks(2, p) for p in late_parts]
        + [pltpu.VMEM(p.shape[1:], BF16) for p in parts]
        + [pltpu.SemaphoreType.DMA((count,))] * 6,
        compiler_params=pltpu.CompilerParams(
            collective_id=0, has_side_effects=True, vmem_limit_bytes=56 * 2**20
        ),
        cost_estimate=cost(4 * size, 20 * size),
    )(*parts)


def gated_unit(gate_arg, up_arg):
    return jax.nn.gelu(gate_arg, approximate=True) * up_arg


def layer(n_dp, n_mp):
    lanes = n_dp // 2
    paired = n_dp == 8

    def swap(value, axis, size, bit):
        return lax.ppermute(value, axis, [(i, i ^ bit) for i in range(size)])

    def core(value):
        return swap(value, "mp", n_mp, 1)

    def chip(value):
        return swap(value, "mp", n_mp, 2)

    def beside(value):
        return swap(value, "dp", n_dp, 1)

    def gather(mine):
        far = chip(mine)
        return assemble([mine, far, core(mine), core(far)])

    def gather_after(mine, after):
        return gather(tie(mine, after))

    def scatter_rows(partial):
        step = partial.shape[0] // 4
        block = [partial[k * step : (k + 1) * step] for k in range(4)]
        far = (block[1].astype(F32) + core(block[3]).astype(F32)).astype(BF16)
        far_in = chip(far)
        return block[0].astype(F32) + core(block[2]).astype(F32) + far_in.astype(F32)

    def line_place():
        z = lax.axis_index("dp") // 2
        number = lambda value: jnp.asarray(value).astype(jnp.int32)
        return lax.axis_index("dp") % 2, number(z >= 2), number((z == 1) | (z == 2))

    def outer_swap(value):
        return swap(value, "dp", n_dp, 2)

    def inner_swap(value):
        pairs = []
        for d in range(n_dp):
            for m in range(n_mp):
                inner = d // 2 in (1, 2)
                to = (d ^ 6) * n_mp + m if inner else d * n_mp + (m ^ 1)
                pairs.append((d * n_mp + m, to))
        return lax.ppermute(value, ("dp", "mp"), pairs)

    def lane_columns(parity):
        flip = line_place()[1]
        k = jnp.arange(4, dtype=jnp.int32)
        return 2 * (k + flip * (3 - 2 * k)) + parity

    def split_columns(value):
        if not paired:
            return (value,)
        x = line_place()[0]
        wanted = pick_columns(
            lane_columns(1 - x), value, value.shape[0] // 2, value.shape[1] // n_dp
        )
        low = beside(wanted)
        return value, low, core(low)

    def shards(
        tokens, norm_gains, w_query, w_key, w_value, w_out, c_query, c_key, c_value, c_out,
        patch_proj, w_gate, w_up, w_down, patches, segment_ids, image_index, cotangent,
    ):
        length = segment_ids.shape[1]
        model = tokens.shape[2]
        patch_rows = patches.shape[0] * patches.shape[1]
        m = lax.axis_index("mp")
        order = [m, m ^ 2, m ^ 1, m ^ 3]

        def blocks(arr, axis=0):
            step = arr.shape[axis] // 4
            return jnp.concatenate(
                [lax.dynamic_slice_in_dim(arr, k * step, step, axis) for k in order], axis=axis
            )

        places = blocks(jnp.arange(length, dtype=jnp.int32))
        segment_row = blocks(segment_ids[0])
        slots = jnp.arange(SEGS, dtype=jnp.int32)
        token_image = jnp.sum(
            jnp.where(segment_row[:, None] == slots, image_index[0][None, :], 0), axis=-1
        )
        patch_image = blocks(jnp.arange(patch_rows, dtype=jnp.int32) // patches.shape[1])

        residual = tokens[0].astype(F32)
        normed_one_mine = norm_rows(residual, norm_gains[0])
        normed_one = gather(normed_one_mine)
        patch_own = pick_rows(
            jnp.stack(order).astype(jnp.int32), patches.reshape(patch_rows, patches.shape[2]), patch_rows // 4
        )
        patch_mine = tie(patch_own[: patch_rows // 4], normed_one_mine)
        projected = gather(matmul(patch_mine, patch_proj).astype(BF16))
        queries = matmul(normed_one, w_query).astype(BF16)
        key_rows = matmul(normed_one, w_key).astype(BF16)
        value_rows = matmul(normed_one, w_value).astype(BF16)
        self_allowed = (segment_row[:, None] == segment_row[None, :]) & (
            places[None, :] <= places[:, None]
        )
        cross_allowed = token_image[:, None] == patch_image[None, :]
        self_mixed, self_log = plain_attend(queries, key_rows, value_rows, self_allowed)
        after_self = residual + scatter_rows(matmul(self_mixed, w_out).astype(BF16))
        split_one = split_columns(normed_one)
        cross_keys = matmul(projected, c_key).astype(BF16)
        cross_values = matmul(projected, c_value).astype(BF16)
        normed_two = gather(norm_rows(after_self, norm_gains[1]))
        grad_three = gather_after(cotangent[0], normed_two)
        cross_queries = matmul(normed_two, c_query).astype(BF16)
        cross_mixed, cross_log = plain_attend(
            cross_queries, cross_keys, cross_values, cross_allowed
        )
        split_patch = split_columns(projected)
        cross_mixed = tie(cross_mixed, split_one)
        after_cross = after_self + scatter_rows(matmul(cross_mixed, c_out).astype(BF16))
        split_two = split_columns(normed_two)
        split_cotangent = split_columns(grad_three)
        grad_hidden = tie(product("sd,fd->sf", grad_three, w_down), ())
        normed_three = gather(norm_rows(after_cross, norm_gains[2]))
        normed_three = tie(normed_three, (grad_hidden, split_patch))
        gate_pre, up_pre = matmul(normed_three, w_gate), matmul(normed_three, w_up)
        hidden, pull = jax.vjp(gated_unit, gate_pre, up_pre)
        hidden = hidden.astype(BF16)
        grad_gate, grad_up = [g.astype(BF16) for g in pull(grad_hidden)]

        results, turned = {}, {}

        def line(name, split, grad, grad_far, rows_first, after=()):
            turned[name] = not rows_first
            if not paired:
                partial = product("td,te->de", split[0], grad).astype(BF16)
                total = lax.psum_scatter(partial, "dp", scatter_dimension=0, tiled=True)
                results[name] = total.astype(F32)
                return ()
            results[name] = pair_grad(
                lane_columns(line_place()[0]), *split, grad, grad_far, after
            )
            return (results[name],)

        def line_early(name):
            if paired:
                part = results[name]
                part = merge(part, outer_swap(part[1:]))
                inner = line_place()[2]
                results[name] = cross_add(inner.reshape(1), part, inner_swap(part[2:]))

        far_of = beside if paired else (lambda value: value)
        hidden_far, gate_far, up_far = far_of(hidden), far_of(grad_gate), far_of(grad_up)
        split_three = split_columns(normed_three)
        grad_normed = scatter_rows(
            (
                product("sf,df->sd", grad_gate, w_gate) + product("sf,df->sd", grad_up, w_up)
            ).astype(BF16)
        )
        grad_input, gain_three = norm_back(after_cross, norm_gains[2], grad_normed)
        grad_rows = cotangent[0].astype(F32) + grad_input
        grad_two = gather(grad_rows.astype(BF16))
        sent = line("down", split_cotangent, hidden, hidden_far, False)
        line_early("down")

        grad_two = tie(grad_two, sent)
        grad_mixed = product("sd,ed->se", grad_two, c_out).astype(BF16)
        mixed_far = far_of(cross_mixed)
        grad_cq, grad_ck, grad_cv = plain_back(
            cross_queries, cross_keys, cross_values, cross_allowed, cross_log, grad_mixed
        )
        sent = line("gate", split_three, grad_gate, gate_far, True, sent)
        line_early("gate")
        grad_cq = tie(grad_cq, sent)
        grad_normed = scatter_rows(product("se,de->sd", grad_cq, c_query).astype(BF16))
        grad_input, gain_two = norm_back(after_self, norm_gains[1], grad_normed)
        grad_rows = grad_rows + grad_input
        cq_far, ck_far, cv_far = far_of(grad_cq), far_of(grad_ck), far_of(grad_cv)
        split_grad_two = split_columns(grad_two)
        grad_one = gather(grad_rows.astype(BF16))
        sent = line("up", split_three, grad_up, up_far, True, sent)
        line_early("up")

        grad_one = tie(grad_one, sent)
        grad_mixed = product("sd,ed->se", grad_one, w_out).astype(BF16)
        grad_sq, grad_sk, grad_sv = plain_back(
            queries, key_rows, value_rows, self_allowed, self_log, grad_mixed
        )
        sent = line("c_out", split_grad_two, cross_mixed, mixed_far, False, sent)
        sent = line("c_query", split_two, grad_cq, cq_far, True, sent)
        grad_sq, grad_sk, grad_sv = tie((grad_sq, grad_sk, grad_sv), sent)
        grad_normed = scatter_rows(
            (
                product("se,de->sd", grad_sq, w_query)
                + product("se,de->sd", grad_sk, w_key)
                + product("se,de->sd", grad_sv, w_value)
            ).astype(BF16)
        )
        grad_input, gain_one = norm_back(residual, norm_gains[0], grad_normed)
        grad_rows = grad_rows + grad_input
        sent = line("c_key", split_patch, grad_ck, ck_far, True, sent)
        sent = line("c_value", split_patch, grad_cv, cv_far, True, sent)
        self_far = far_of(self_mixed)
        sq_far, sk_far, sv_far = far_of(grad_sq), far_of(grad_sk), far_of(grad_sv)
        output = after_cross + scatter_rows(matmul(tie(hidden, sent), w_down).astype(BF16))
        sent = line("w_out", split_columns(grad_one), self_mixed, self_far, False, sent)
        sent = line("w_query", split_one, grad_sq, sq_far, True, sent)
        sent = line("w_key", split_one, grad_sk, sk_far, True, sent)
        sent = line("w_value", split_one, grad_sv, sv_far, True, sent)

        width = model // (n_dp * n_mp)

        def projected_block(k):
            def rows_of(weight):
                cut = weight.reshape(n_dp, n_mp, width, weight.shape[1])
                return lax.dynamic_index_in_dim(cut, k, 1, keepdims=False).reshape(
                    n_dp * width, weight.shape[1]
                )

            return (cols_dot(grad_ck, rows_of(c_key)) + cols_dot(grad_cv, rows_of(c_value))).astype(
                BF16
            )

        block = [projected_block(k) for k in order]
        half, quarter = patch_rows // 2, patch_rows // 4
        far = add_swapped(block[1], core(block[3]), half)
        near = add_swapped(block[0], core(block[2]), half)
        grad_projected = add_swapped(near, chip(far), quarter)
        patch_partial = rows_dot(grad_projected, patch_own).astype(BF16)
        if paired:
            x, flip, unused = line_place()
            parts = patch_partial.reshape(4, 2, width, patches.shape[2])
            sent = beside(lax.dynamic_index_in_dim(parts, 1 - x, 1, keepdims=False))
            kept = lax.dynamic_index_in_dim(parts, x, 1, keepdims=False)
            summed = kept.astype(F32) + sent.astype(F32)
            results["patch"] = jnp.where(flip == 1, summed[::-1], summed).astype(BF16)
            early = ["down", "gate", "up"]
            late = ["c_out", "c_query", "c_key", "c_value", "w_out", "w_query", "w_key", "w_value"]
            late.append("patch")
            sums = line_sums([results[n] for n in early], [results[n] for n in late])
            results.update(zip(early + late, sums))
        else:
            results["patch"] = lax.psum_scatter(
                patch_partial, "dp", scatter_dimension=0, tiled=True
            ).astype(F32)
        turned["patch"] = True
        results = {n: v.T if turned[n] else v for n, v in results.items()}
        patch_total = results["patch"]
        gain_total = lax.psum_scatter(
            jnp.stack([gain_one, gain_two, gain_three]),
            ("dp", "mp"), scatter_dimension=1, tiled=True,
        )
        sum_query, sum_key, sum_value = results["w_query"], results["w_key"], results["w_value"]
        sum_cquery, sum_ckey, sum_cvalue = results["c_query"], results["c_key"], results["c_value"]
        sum_out, sum_cout, sum_down = results["w_out"], results["c_out"], results["down"]
        sum_gate, sum_up = results["gate"], results["up"]
        return (
            output.astype(BF16)[None], grad_rows[None], gain_total,
            sum_query, sum_key, sum_value, sum_out,
            sum_cquery, sum_ckey, sum_cvalue, sum_cout,
            patch_total, sum_gate, sum_up, sum_down,
        )

    return shards


def solution(mesh):
    columns, rows = P(None, "mp"), P("mp", None)
    return jax.shard_map(
        layer(mesh.shape["dp"], mesh.shape["mp"]),
        mesh=mesh,
        in_specs=(
            P("dp", "mp", None), P(), columns, columns, columns, rows, columns, columns, columns,
            rows, P(), columns, columns, rows, P("dp", None, None), P("dp", None), P("dp", None),
            P("dp", "mp", None),
        ),
        out_specs=(
            P("dp", "mp", None), P("dp", "mp", None), P(None, ("dp", "mp")),
            P("dp", "mp"), P("dp", "mp"), P("dp", "mp"), P("mp", "dp"),
            P("dp", "mp"), P("dp", "mp"), P("dp", "mp"), P("mp", "dp"),
            P(None, ("dp", "mp")), P("dp", "mp"), P("dp", "mp"), P("mp", "dp"),
        ),
        check_vma=False,
    )
```

time: 680 us -> 908 us (1.34)
  Pallas kernels: 0 us -> 278 us
  waiting for transfers between devices: 265 us -> 347 us
  matrix products: 166 us -> 89.1 us
  other arithmetic: 90.7 us -> 28.3 us
  starting transfers between devices: 96.2 us -> 56.3 us
  local copies, waits for them, and re-layouts: 47.7 us -> 82.1 us
  between operations: 3.51 us -> 16.6 us
    pallas_call x0 -> x36, Pallas kernels: none -> 278 us  [the longest x1 194 us: line_sums(): pl.pallas_call(functools.partial(line_kernel, ready, count), in_specs=[vm...]
    ppermute x88 -> x71, waiting for transfers between devices: 265 us -> 347 us  [swap(): return lax.ppermute(value, axis, [(i, i ^ bit) for i in range(size)])]
    dot_general x45 -> x21, matrix products: 109 us -> 44.5 us  [product(): return jnp.einsum(spec, left, right, preferred_element_type=F32)]
    ppermute x88 -> x71, starting transfers between devices: 96 us -> 55.3 us  [swap(): return lax.ppermute(value, axis, [(i, i ^ bit) for i in range(size)])]
    select_n x38 -> x0, other arithmetic: 27.7 us -> none  [the longest x9 8.85 us: line_steps(): jnp.where(inner == 1, (near[:1].astype(F32) + crossed[1:].astype(F32)).as...]
    unnamed x303 -> x340, local copies, waits for them, and re-layouts: 21.5 us -> 47.4 us
    concatenate x14 -> x0, other arithmetic: 12 us -> none  [the longest x7 6.51 us: gather(): return jnp.concatenate([mine, far, core(mine), core(far)], axis=0)]
    convert_element_type x5 -> x8, local copies, waits for them, and re-layouts: 4.2 us -> 15.1 us  [flat_heads(): return arr.reshape(arr.shape[0], -1).astype(BF16)]
  transfers between devices with their start and end apart: 97 -> 75, of which waited for: 29 -> 20; matrix products, arithmetic and copies ran while one was open for 42% -> 14% of each run, Pallas kernels for 0% -> 31%
where the time goes in v3:
time: 908 us; the launch traced here: 897 us
  waiting for transfers between devices  347 us (38%)
  Pallas kernels  278 us (31%)
  matrix products  89.1 us (10%)
  local copies, waits for them, and re-layouts  82.1 us (9%)
  starting transfers between devices  56.3 us (6%)
  other arithmetic  28.3 us (3%)
  between operations  16.6 us (2%)
    ppermute x71, waiting for transfers between devices, swap(): return lax.ppermute(value, axis, [(i, i ^ bit) for i in range(size)])  347 us
    pallas_call x1, Pallas kernels, line_sums(): pl.pallas_call(functools.partial(line_kernel, ready, count), in_specs=[vm...  194 us
    ppermute x71, starting transfers between devices, swap(): return lax.ppermute(value, axis, [(i, i ^ bit) for i in range(size)])  55.3 us
    pallas_call x11, Pallas kernels, pair_grad(): pl.pallas_call(pair_kernel, grid_spec=pltpu.PrefetchScalarGridSpec(num_sc...  54.1 us
    unnamed x340, local copies, waits for them, and re-layouts  47.4 us
    dot_general x21, matrix products, product(): return jnp.einsum(spec, left, right, preferred_element_type=F32)  44.5 us
    dot_general x12, matrix products, matmul(): return jnp.dot(left, right, preferred_element_type=F32)  30.4 us
  transfers between devices with their start and end apart: 75, of which 20 were waited for; matrix products, arithmetic and copies ran while one was open for 14% of the time, Pallas kernels for 31%

profile of v3, /device:TPU:0, one launch (start us, length us, event | category | flops | bytes accessed | tf_op | source)
XLA Modules:
  0.0 897.2 jit_solution(14884864670391266227)
XLA Ops:
  14.8 11.9 %collective-permute-done.refs_1_ = bf16[128,2048]{1,0:T(8,128)(2,1)S(1)} collective-permute-done((bf16[128,2048]{1,0:T(8,128)(2,1)S(1)}, bf16[128,2048]{1,0:T(8,128)(2,1)S(1)}, u32[]{:S(2)}, u32[]{:S(2)}) %collective-permute-start) | collective-permute-done | bytes 524320 | tf_op jit(solution)/shard_map/ppermute | solution.py:378
  61.1 19.1 %collective-permute-done.6.refs_1_ = bf16[256,2048]{1,0:T(8,128)(2,1)} collective-permute-done((bf16[256,2048]{1,0:T(8,128)(2,1)}, bf16[256,2048]{1,0:T(8,128)(2,1)}, u32[]{:S(2)}, u32[]{:S(2)}) %collective-permute-start.6) | collective-permute-done | bytes 1048608 | tf_op jit(solution)/shard_map/ppermute | solution.py:378
  81.1 9.8 %collective-permute-done.5 = bf16[128,2048]{1,0:T(8,128)(2,1)S(1)} collective-permute-done((bf16[128,2048]{1,0:T(8,128)(2,1)S(1)}, bf16[128,2048]{1,0:T(8,128)(2,1)S(1)}, u32[]{:S(2)}, u32[]{:S(2)}) %collective-permute-start.5) | collective-permute-done | bytes 524320 | tf_op jit(solution)/shard_map/ppermute | solution.py:378
  99.6 6.2 collective-permute-done.9.refs_1_
  131.6 8.6 collective-permute-done.20.refs_1_
  140.3 10.8 %collective-permute-done.16 = bf16[128,2048]{1,0:T(8,128)(2,1)S(1)} collective-permute-done((bf16[128,2048]{1,0:T(8,128)(2,1)S(1)}, bf16[128,2048]{1,0:T(8,128)(2,1)S(1)}, u32[]{:S(2)}, u32[]{:S(2)}) %collective-permute-start.16) | collective-permute-done | bytes 524320 | tf_op jit(solution)/shard_map/ppermute | solution.py:378
  156.4 8.9 collective-permute-done.17.refs_1_
  171.9 6.2 multiply_convert_fusion.2
  197.6 5.4 collective-permute-done.31.lo_ref
  215.2 86.6 %collective-permute-done.38.lo_ref = bf16[256,1024]{1,0:T(8,128)(2,1)S(1)} collective-permute-done((bf16[256,1024]{1,0:T(8,128)(2,1)S(1)}, bf16[256,1024]{1,0:T(8,128)(2,1)S(1)}, u32[]{:S(2)}, u32[]{:S(2)}) %collective-permute-start.38) | collective-permute-done | bytes 524320 | tf_op jit(solution)/shard_map/ppermute | solution.py:378
  309.2 6.1 shard_map.299.rest_0_.part_ref
  318.7 6.1 shard_map.302.rest_0_.part_ref
  326.4 6.1 shard_map.304.rest_0_.part_ref
  376.2 4.9 collective-permute-done.42.lo_ref
  393.9 42.5 %collective-permute-done.41.far_ref = bf16[512,512]{1,0:T(8,128)(2,1)S(1)} collective-permute-done((bf16[512,512]{1,0:T(8,128)(2,1)S(1)}, bf16[512,512]{1,0:T(8,128)(2,1)S(1)}, u32[]{:S(2)}, u32[]{:S(2)}) %collective-permute-start.41) | collective-permute-done | bytes 524320 | tf_op jit(solution)/shard_map/ppermute | solution.py:378
  442.6 6.3 shard_map.307.rest_0_.refs_5_
  465.1 17.1 %collective-permute-done.62.in_ref = bf16[3,256,1280]{2,1,0:T(8,128)(2,1)S(1)} collective-permute-done((bf16[3,256,1280]{2,1,0:T(8,128)(2,1)S(1)}, bf16[3,256,1280]{2,1,0:T(8,128)(2,1)S(1)}, u32[]{:S(2)}, u32[]{:S(2)}) %collective-permute-start.62) | collective-permute-done | bytes 1966112 | tf_op jit(solution)/shard_map/ppermute | solution.py:378
  488.5 35.9 %collective-permute-done.60.in_ref = bf16[3,256,1280]{2,1,0:T(8,128)(2,1)S(1)} collective-permute-done((bf16[3,256,1280]{2,1,0:T(8,128)(2,1)S(1)}, bf16[3,256,1280]{2,1,0:T(8,128)(2,1)S(1)}, u32[]{:S(2)}, u32[]{:S(2)}) %collective-permute-start.60) | collective-permute-done | bytes 1966112 | tf_op jit(solution)/shard_map/ppermute | solution.py:378
  527.8 37.0 %collective-permute-done.58.in_ref = bf16[3,256,1280]{2,1,0:T(8,128)(2,1)S(1)} collective-permute-done((bf16[3,256,1280]{2,1,0:T(8,128)(2,1)S(1)}, bf16[3,256,1280]{2,1,0:T(8,128)(2,1)S(1)}, u32[]{:S(2)}, u32[]{:S(2)}) %collective-permute-start.58) | collective-permute-done | bytes 1966112 | tf_op jit(solution)/shard_map/ppermute | solution.py:378
  614.2 19.2 %collective-permute-done.64.lo_ref = bf16[256,1024]{1,0:T(8,128)(2,1)} collective-permute-done((bf16[256,1024]{1,0:T(8,128)(2,1)S(1)}, bf16[256,1024]{1,0:T(8,128)(2,1)}, u32[]{:S(2)}, u32[]{:S(2)}) %collective-permute-start.64) | collective-permute-done | bytes 524320 | tf_op jit(solution)/shard_map/ppermute | solution.py:378
  636.7 8.3 collective-permute-done.57
  648.6 4.7 shard_map.317.rest_0_.refs_7_
  660.1 7.0 collective-permute-done.68.far_ref
  682.1 194.0 %shard_map.324 = (f32[256,1280]{1,0:T(8,128)}, f32[256,1280]{1,0:T(8,128)}, f32[256,1280]{1,0:T(8,128)}, f32[256,512]{1,0:T(8,128)}, f32[256,512]{1,0:T(8,128)},...) custom-call(bf16[2,256,1280]{2,1,0:T(8,128)(2,1)} %copy-done.41, ...), custom_call_target="tpu_custom_call" | custom-call | flops 26345472 | bytes 131727360 | tf_op jit(solution)/shard_map/pallas_call | solution.py:353
  (628 shorter events, 311.8 us)
Async XLA Ops:
  7.2 873.8 %reduce-scatter.4.cloned.1.call-start = ((), (), s32[]{:S(2)}) async-start(), calls=%async_computation.1 | async-start | bytes 1081344
  80.5 41.4 %collective-permute-start.13 = (bf16[256,1024]{1,0:T(8,128)(2,1)S(1)}, bf16[256,1024]{1,0:T(8,128)(2,1)S(1)}, u32[]{:S(2)}, u32[]{:S(2)}) collective-permute-start(bf16[256,1024]{1,0:T(8,128)(2,1)S(1)} %collective-permute-done.12.lo_ref), channel_id=1, source_target_pairs={{0,1},{1,0},{2,3},{3,2},{4,5},{5,4},{6,7},{7,6},{8,9},{9,8},{10,11... | collective-permute-start | bytes 1572872 | tf_op jit(solution)/shard_map/ppermute | solution.py:378
  203.0 115.4 %collective-permute-start.40 = (bf16[512,1280]{1,0:T(8,128)(2,1)}, bf16[512,1280]{1,0:T(8,128)(2,1)}, u32[]{:S(2)}, u32[]{:S(2)}) collective-permute-start(bf16[512,1280]{1,0:T(8,128)(2,1)} %get-tuple-element.136.g_ref), channel_id=1, source_target_pairs={{0,4},{4,0},{8,12},{12,8},{16,20},{20,16},{24,28},{28,24},{1,5},{5... | collective-permute-start | bytes 3932168 | tf_op jit(solution)/shard_map/ppermute | solution.py:378
  205.7 120.7 %collective-permute-start.45 = (bf16[512,1280]{1,0:T(8,128)(2,1)}, bf16[512,1280]{1,0:T(8,128)(2,1)}, u32[]{:S(2)}, u32[]{:S(2)}) collective-permute-start(bf16[512,1280]{1,0:T(8,128)(2,1)} %get-tuple-element.135.g_ref), channel_id=1, source_target_pairs={{0,4},{4,0},{8,12},{12,8},{16,20},{20,16},{24,28},{28,24},{1,5},{5... | collective-permute-start | bytes 3932168 | tf_op jit(solution)/shard_map/ppermute | solution.py:378
  206.0 101.4 %collective-permute-start.33 = (bf16[512,1280]{1,0:T(8,128)(2,1)}, bf16[512,1280]{1,0:T(8,128)(2,1)}, u32[]{:S(2)}, u32[]{:S(2)}) collective-permute-start(bf16[512,1280]{1,0:T(8,128)(2,1)} %get-tuple-element.44.g_ref), channel_id=1, source_target_pairs={{0,4},{4,0},{8,12},{12,8},{16,20},{20,16},{24,28},{28,24},{1,5},{5... | collective-permute-start | bytes 3932168 | tf_op jit(solution)/shard_map/ppermute | solution.py:378
  207.8 94.0 %collective-permute-start.38 = (bf16[256,1024]{1,0:T(8,128)(2,1)S(1)}, bf16[256,1024]{1,0:T(8,128)(2,1)S(1)}, u32[]{:S(2)}, u32[]{:S(2)}) collective-permute-start(bf16[256,1024]{1,0:T(8,128)(2,1)S(1)} %shard_map.301), channel_id=1, source_target_pairs={{0,4},{4,0},{8,12},{12,8},{16,20},{20,16},{24,28},{28,24},{1,5},{5... | collective-permute-start | bytes 1572872 | tf_op jit(solution)/shard_map/ppermute | solution.py:378
  213.4 94.7 %collective-permute-start.28 = (bf16[128,2048]{1,0:T(8,128)(2,1)}, bf16[128,2048]{1,0:T(8,128)(2,1)}, u32[]{:S(2)}, u32[]{:S(2)}) collective-permute-start(bf16[128,2048]{1,0:T(8,128)(2,1)} %get-tuple-element.129.refs_0_), channel_id=1, source_target_pairs={{0,2},{1,3},{2,0},{3,1},{4,6},{5,7},{6,4},{7,5},{8,10},{9,11},{10,... | collective-permute-start | bytes 1572872 | tf_op jit(solution)/shard_map/ppermute | solution.py:378
  316.7 53.2 %collective-permute-start.44 = (bf16[512,512]{1,0:T(8,128)(2,1)}, bf16[512,512]{1,0:T(8,128)(2,1)}, u32[]{:S(2)}, u32[]{:S(2)}) collective-permute-start(bf16[512,512]{1,0:T(8,128)(2,1)} %copy.141.g_ref), channel_id=1, source_target_pairs={{0,4},{4,0},{8,12},{12,8},{16,20},{20,16},{24,28},{28,24},{1,5},{5... | collective-permute-start | bytes 1572872 | tf_op jit(solution)/shard_map/ppermute | solution.py:378
  318.4 56.0 %collective-permute-start.36 = (bf16[256,1024]{1,0:T(8,128)(2,1)}, bf16[256,1024]{1,0:T(8,128)(2,1)}, u32[]{:S(2)}, u32[]{:S(2)}) collective-permute-start(bf16[256,1024]{1,0:T(8,128)(2,1)} %shard_map.300), channel_id=1, source_target_pairs={{0,4},{4,0},{8,12},{12,8},{16,20},{20,16},{24,28},{28,24},{1,5},{5... | collective-permute-start | bytes 1572872 | tf_op jit(solution)/shard_map/ppermute | solution.py:378
  369.9 72.3 %collective-permute-start.35 = (bf16[1024,512]{1,0:T(8,128)(2,1)}, bf16[1024,512]{1,0:T(8,128)(2,1)}, u32[]{:S(2)}, u32[]{:S(2)}) collective-permute-start(bf16[1024,512]{1,0:T(8,128)(2,1)} %copy.143.g_ref), channel_id=1, source_target_pairs={{0,4},{4,0},{8,12},{12,8},{16,20},{20,16},{24,28},{28,24},{1,5},{5... | collective-permute-start | bytes 3145736 | tf_op jit(solution)/shard_map/ppermute | solution.py:378
  374.4 74.5 %collective-permute-start.34 = (bf16[1024,512]{1,0:T(8,128)(2,1)}, bf16[1024,512]{1,0:T(8,128)(2,1)S(1)}, u32[]{:S(2)}, u32[]{:S(2)}) collective-permute-start(bf16[1024,512]{1,0:T(8,128)(2,1)} %copy.142.g_ref), channel_id=1, source_target_pairs={{0,4},{4,0},{8,12},{12,8},{16,20},{20,16},{24,28},{28,24},{1,5},{5... | collective-permute-start | bytes 3145736 | tf_op jit(solution)/shard_map/ppermute | solution.py:378
  383.3 53.1 %collective-permute-start.41 = (bf16[512,512]{1,0:T(8,128)(2,1)S(1)}, bf16[512,512]{1,0:T(8,128)(2,1)S(1)}, u32[]{:S(2)}, u32[]{:S(2)}) collective-permute-start(bf16[512,512]{1,0:T(8,128)(2,1)S(1)} %copy-done.54), channel_id=1, source_target_pairs={{0,4},{4,0},{8,12},{12,8},{16,20},{20,16},{24,28},{28,24},{1,5},{5... | collective-permute-start | bytes 1572872 | tf_op jit(solution)/shard_map/ppermute | solution.py:378
  387.7 67.3 %collective-permute-start.49 = (bf16[128,2048]{1,0:T(8,128)(2,1)S(1)}, bf16[128,2048]{1,0:T(8,128)(2,1)S(1)}, u32[]{:S(2)}, u32[]{:S(2)}) collective-permute-start(bf16[128,2048]{1,0:T(8,128)(2,1)S(1)} %copy-done.138), channel_id=1, source_target_pairs={{0,1},{1,0},{2,3},{3,2},{4,5},{5,4},{6,7},{7,6},{8,9},{9,8},{10,11... | collective-permute-start | bytes 1572872 | tf_op jit(solution)/shard_map/ppermute | solution.py:378
  388.0 67.1 %collective-permute-start.51 = (bf16[128,2048]{1,0:T(8,128)(2,1)S(1)}, bf16[128,2048]{1,0:T(8,128)(2,1)S(1)}, u32[]{:S(2)}, u32[]{:S(2)}) collective-permute-start(bf16[128,2048]{1,0:T(8,128)(2,1)S(1)} %add_convert_fusion.7), channel_id=1, source_target_pairs={{0,2},{1,3},{2,0},{3,1},{4,6},{5,7},{6,4},{7,5},{8,10},{9,11},{10,... | collective-permute-start | bytes 1572872 | tf_op jit(solution)/shard_map/ppermute | solution.py:378
  436.4 45.8 %collective-permute-start.62 = (bf16[3,256,1280]{2,1,0:T(8,128)(2,1)S(1)}, bf16[3,256,1280]{2,1,0:T(8,128)(2,1)S(1)}, u32[]{:S(2)}, u32[]{:S(2)}) collective-permute-start(bf16[3,256,1280]{2,1,0:T(8,128)(2,1)S(1)} %copy-done.117), channel_id=1, source_target_pairs={{0,8},{4,12},{8,0},{12,4},{16,24},{20,28},{24,16},{28,20},{1,9},{5... | collective-permute-start | bytes 5898248 | tf_op jit(solution)/shard_map/ppermute | solution.py:378
  442.2 82.1 %collective-permute-start.60 = (bf16[3,256,1280]{2,1,0:T(8,128)(2,1)S(1)}, bf16[3,256,1280]{2,1,0:T(8,128)(2,1)S(1)}, u32[]{:S(2)}, u32[]{:S(2)}) collective-permute-start(bf16[3,256,1280]{2,1,0:T(8,128)(2,1)S(1)} %copy-done.116), channel_id=1, source_target_pairs={{0,8},{4,12},{8,0},{12,4},{16,24},{20,28},{24,16},{28,20},{1,9},{5... | collective-permute-start | bytes 5898248 | tf_op jit(solution)/shard_map/ppermute | solution.py:378
  449.0 115.8 %collective-permute-start.58 = (bf16[3,256,1280]{2,1,0:T(8,128)(2,1)S(1)}, bf16[3,256,1280]{2,1,0:T(8,128)(2,1)S(1)}, u32[]{:S(2)}, u32[]{:S(2)}) collective-permute-start(bf16[3,256,1280]{2,1,0:T(8,128)(2,1)S(1)} %copy-done.115), channel_id=1, source_target_pairs={{0,8},{4,12},{8,0},{12,4},{16,24},{20,28},{24,16},{28,20},{1,9},{5... | collective-permute-start | bytes 5898248 | tf_op jit(solution)/shard_map/ppermute | solution.py:378
  455.1 113.3 %collective-permute-start.72 = (bf16[1024,512]{1,0:T(8,128)(2,1)S(1)}, bf16[1024,512]{1,0:T(8,128)(2,1)S(1)}, u32[]{:S(2)}, u32[]{:S(2)}) collective-permute-start(bf16[1024,512]{1,0:T(8,128)(2,1)S(1)} %shard_map.322), channel_id=1, source_target_pairs={{0,2},{1,3},{2,0},{3,1},{4,6},{5,7},{6,4},{7,5},{8,10},{9,11},{10,... | collective-permute-start | bytes 3145736 | tf_op jit(solution)/shard_map/ppermute | solution.py:378
  462.5 104.3 %collective-permute-start.47 = (bf16[128,2048]{1,0:T(8,128)(2,1)S(1)}, bf16[128,2048]{1,0:T(8,128)(2,1)S(1)}, u32[]{:S(2)}, u32[]{:S(2)}) collective-permute-start(bf16[128,2048]{1,0:T(8,128)(2,1)S(1)} %get-tuple-element.151), channel_id=1, source_target_pairs={{0,1},{1,0},{2,3},{3,2},{4,5},{5,4},{6,7},{7,6},{8,9},{9,8},{10,11... | collective-permute-start | bytes 1572872 | tf_op jit(solution)/shard_map/ppermute | solution.py:378
  482.2 86.1 %collective-permute-start.52 = (bf16[128,2048]{1,0:T(8,128)(2,1)S(1)}, bf16[128,2048]{1,0:T(8,128)(2,1)S(1)}, u32[]{:S(2)}, u32[]{:S(2)}) collective-permute-start(bf16[128,2048]{1,0:T(8,128)(2,1)S(1)} %get-tuple-element.127.refs_0_), channel_id=1, source_target_pairs={{0,2},{1,3},{2,0},{3,1},{4,6},{5,7},{6,4},{7,5},{8,10},{9,11},{10,... | collective-permute-start | bytes 1572872 | tf_op jit(solution)/shard_map/ppermute | solution.py:378
  524.3 48.0 %collective-permute-start.53 = (bf16[128,2048]{1,0:T(8,128)(2,1)S(1)}, bf16[128,2048]{1,0:T(8,128)(2,1)S(1)}, u32[]{:S(2)}, u32[]{:S(2)}) collective-permute-start(bf16[128,2048]{1,0:T(8,128)(2,1)S(1)} %get-tuple-element.127.refs_0_), channel_id=1, source_target_pairs={{0,1},{1,0},{2,3},{3,2},{4,5},{5,4},{6,7},{7,6},{8,9},{9,8},{10,11... | collective-permute-start | bytes 1572872 | tf_op jit(solution)/shard_map/ppermute | solution.py:378
  568.3 39.2 %collective-permute-start.61 = (bf16[2,256,1280]{2,1,0:T(8,128)(2,1)}, bf16[2,256,1280]{2,1,0:T(8,128)(2,1)}, u32[]{:S(2)}, u32[]{:S(2)}) collective-permute-start(bf16[2,256,1280]{2,1,0:T(8,128)(2,1)} %slice.167), channel_id=1, source_target_pairs={{0,1},{1,0},{2,3},{3,2},{4,5},{5,4},{6,7},{7,6},{8,16},{9,17},{10,... | collective-permute-start | bytes 3932168 | tf_op jit(solution)/shard_map/ppermute | solution.py:418
  607.5 41.1 %collective-permute-start.66 = (bf16[512,512]{1,0:T(8,128)(2,1)}, bf16[512,512]{1,0:T(8,128)(2,1)}, u32[]{:S(2)}, u32[]{:S(2)}) collective-permute-start(bf16[512,512]{1,0:T(8,128)(2,1)} %copy.140.g_ref), channel_id=1, source_target_pairs={{0,4},{4,0},{8,12},{12,8},{16,20},{20,16},{24,28},{28,24},{1,5},{5... | collective-permute-start | bytes 1572872 | tf_op jit(solution)/shard_map/ppermute | solution.py:378
  611.5 44.3 %collective-permute-start.67 = (bf16[512,512]{1,0:T(8,128)(2,1)}, bf16[512,512]{1,0:T(8,128)(2,1)}, u32[]{:S(2)}, u32[]{:S(2)}) collective-permute-start(bf16[512,512]{1,0:T(8,128)(2,1)} %copy.145.g_ref), channel_id=1, source_target_pairs={{0,4},{4,0},{8,12},{12,8},{16,20},{20,16},{24,28},{28,24},{1,5},{5... | collective-permute-start | bytes 1572872 | tf_op jit(solution)/shard_map/ppermute | solution.py:378
  (214 other events, 2809.2 us)
Sparse Core Ops, SparseCore 0:
  648.7 166.9 reduce-scatter.3

commit v4 on v3

v4 whole, which is shorter than its diff:
```python
import functools

import jax
import jax.numpy as jnp
from jax import lax
from jax.experimental import pallas as pl
from jax.experimental.pallas import tpu as pltpu
from jax.sharding import PartitionSpec as P

HEAD_DIM = 128
SEGS = 4
EPSILON = 1e-06
MASKED = -1000000000.0
F32 = jnp.float32
BF16 = jnp.bfloat16


def matmul(left, right):
    return jnp.dot(left, right, preferred_element_type=F32)


def product(spec, left, right):
    return jnp.einsum(spec, left, right, preferred_element_type=F32)


def rows_dot(left, right):
    return lax.dot_general(left, right, (((0,), (0,)), ((), ())), preferred_element_type=F32)


def cols_dot(left, right):
    return lax.dot_general(left, right, (((1,), (1,)), ((), ())), preferred_element_type=F32)


def tie(value, after):
    return lax.optimization_barrier((value, after))[0]


def inverse_rms(rows):
    return lax.rsqrt(jnp.mean(rows * rows, axis=-1, keepdims=True) + EPSILON)


def norm_rows(rows, gain):
    return (rows * inverse_rms(rows) * gain).astype(BF16)


def norm_back(rows, gain, grad):
    inv = inverse_rms(rows)
    weighted = gain * grad
    inner = jnp.mean(rows * weighted, axis=-1, keepdims=True)
    grad_rows = inv * weighted - rows * (inv * inv * inv) * inner
    return grad_rows, jnp.sum(grad * rows * inv, axis=0)


VMEM_LIMIT = 20 * 2**20
ANY = pl.BlockSpec(memory_space=pl.ANY)


def params(grid_rank):
    return pltpu.CompilerParams(
        dimension_semantics=("arbitrary",) * grid_rank, vmem_limit_bytes=VMEM_LIMIT
    )


def cost(flops, size):
    return pl.CostEstimate(flops=flops, bytes_accessed=size, transcendentals=0)


def masked_scores(q_ref, k_ref, row_ref, col_ref, causal):
    scores = cols_dot(q_ref[...], k_ref[...]) * (HEAD_DIM ** (-0.5))
    allowed = row_ref[:, 0:1] == col_ref[0:1, :]
    if causal:
        allowed = allowed & (col_ref[1:2, :] <= row_ref[:, 1:2])
    return jnp.where(allowed, scores, MASKED)


def attend_kernel(causal, q_ref, k_ref, v_ref, row_ref, col_ref, out_ref):
    scores = masked_scores(q_ref, k_ref, row_ref, col_ref, causal)
    exponent = jnp.exp(scores - jnp.max(scores, axis=-1, keepdims=True))
    total = jnp.sum(exponent, axis=-1, keepdims=True)
    weights = (exponent * (1.0 / total)).astype(BF16)
    out_ref[...] = matmul(weights, v_ref[...]).astype(BF16)


def attend(queries, keys, values, rows, cols, causal):
    length, width = queries.shape
    spots = keys.shape[0]
    head = lambda size: pl.BlockSpec((size, HEAD_DIM), lambda h: (0, h))
    whole = lambda arr: pl.BlockSpec(arr.shape, lambda h: (0, 0))
    return pl.pallas_call(
        functools.partial(attend_kernel, causal),
        grid=(width // HEAD_DIM,),
        in_specs=[head(length), head(spots), head(spots), whole(rows), whole(cols)],
        out_specs=head(length),
        out_shape=jax.ShapeDtypeStruct((length, width), BF16),
        compiler_params=params(1),
        cost_estimate=pl.CostEstimate(
            flops=4 * length * spots * width,
            bytes_accessed=4 * (length + spots) * width,
            transcendentals=length * spots * width // HEAD_DIM,
        ),
    )(queries, keys, values, rows, cols)


def attend_back_kernel(causal, q_ref, k_ref, v_ref, row_ref, col_ref, do_ref, dq_ref, dk_ref, dv_ref):
    scale = HEAD_DIM ** (-0.5)
    scores = masked_scores(q_ref, k_ref, row_ref, col_ref, causal)
    exponent = jnp.exp(scores - jnp.max(scores, axis=-1, keepdims=True))
    weights = exponent * (1.0 / jnp.sum(exponent, axis=-1, keepdims=True))
    grad_weights = cols_dot(do_ref[...], v_ref[...])
    inner = jnp.sum(weights * grad_weights, axis=-1, keepdims=True)
    grad_scores = (weights * (grad_weights - inner)).astype(BF16)
    dq_ref[...] = (matmul(grad_scores, k_ref[...]) * scale).astype(BF16)
    dk_ref[...] = (rows_dot(grad_scores, q_ref[...]) * scale).astype(BF16)
    dv_ref[...] = rows_dot(weights.astype(BF16), do_ref[...]).astype(BF16)


def self_back_kernel(q_ref, k_ref, v_ref, row_ref, col_ref, do_ref, *outs):
    attend_back_kernel(
        True, q_ref, k_ref, v_ref, row_ref, col_ref, do_ref,
        *outs,
    )


def cross_back_kernel(q_ref, k_ref, v_ref, row_ref, col_ref, do_ref, *outs):
    attend_back_kernel(
        False, q_ref, k_ref, v_ref, row_ref, col_ref, do_ref,
        *outs,
    )


def attend_back(queries, keys, values, rows, cols, grad_out, causal):
    length, width = queries.shape
    spots = keys.shape[0]
    head = lambda size: pl.BlockSpec((size, HEAD_DIM), lambda h: (0, h))
    whole = lambda arr: pl.BlockSpec(arr.shape, lambda h: (0, 0))
    sizes = (length, spots, spots)
    out_specs = tuple(head(size) for size in sizes)
    out_shape = tuple(jax.ShapeDtypeStruct((size, width), BF16) for size in sizes)
    return pl.pallas_call(
        self_back_kernel if causal else cross_back_kernel,
        grid=(width // HEAD_DIM,),
        in_specs=[
            head(length), head(spots), head(spots), whole(rows), whole(cols), head(length),
        ],
        out_specs=out_specs,
        out_shape=out_shape,
        compiler_params=params(1),
        cost_estimate=pl.CostEstimate(
            flops=10 * length * spots * width,
            bytes_accessed=8 * (length + spots) * width,
            transcendentals=length * spots * width // HEAD_DIM,
        ),
    )(queries, keys, values, rows, cols, grad_out)


def assemble_kernel(*refs):
    *blocks, out_ref = refs
    step = blocks[0].shape[0]
    for k, block in enumerate(blocks):
        out_ref[k * step : (k + 1) * step] = block[...]


def assemble(blocks):
    step, width = blocks[0].shape
    columns = 512
    return pl.pallas_call(
        assemble_kernel,
        grid=(width // columns,),
        in_specs=[pl.BlockSpec((step, columns), lambda j: (0, j))] * len(blocks),
        out_specs=pl.BlockSpec((len(blocks) * step, columns), lambda j: (0, j)),
        out_shape=jax.ShapeDtypeStruct((len(blocks) * step, width), blocks[0].dtype),
        compiler_params=params(1),
        cost_estimate=cost(0, 4 * len(blocks) * step * width),
    )(*blocks)


def copy_kernel(at_ref, in_ref, out_ref):
    out_ref[...] = in_ref[...]


def pick_rows(at, arr, step):
    count, width = at.shape[0], arr.shape[1]
    return pl.pallas_call(
        copy_kernel,
        grid_spec=pltpu.PrefetchScalarGridSpec(
            num_scalar_prefetch=1,
            grid=(count,),
            in_specs=[pl.BlockSpec((step, width), lambda k, at: (at[k], 0))],
            out_specs=pl.BlockSpec((step, width), lambda k, at: (k, 0)),
        ),
        out_shape=jax.ShapeDtypeStruct((count * step, width), arr.dtype),
        compiler_params=params(1),
        cost_estimate=cost(0, 4 * count * step * width),
    )(at, arr)


def pick_columns(at, arr, rows, width):
    count = at.shape[0]
    return pl.pallas_call(
        copy_kernel,
        grid_spec=pltpu.PrefetchScalarGridSpec(
            num_scalar_prefetch=1,
            grid=(count,),
            in_specs=[pl.BlockSpec((rows, width), lambda k, at: (0, at[k]))],
            out_specs=pl.BlockSpec((rows, width), lambda k, at: (0, k)),
        ),
        out_shape=jax.ShapeDtypeStruct((rows, count * width), arr.dtype),
        compiler_params=params(1),
        cost_estimate=cost(0, 4 * count * rows * width),
    )(at, arr)


def pair_kernel(at_ref, a_ref, lo_ref, hi_ref, g_ref, far_ref, *rest):
    half = lo_ref.shape[0]
    total = rows_dot(a_ref[...], g_ref[...])
    total += rows_dot(lo_ref[...], far_ref[:half])
    total += rows_dot(hi_ref[...], far_ref[half:])
    first_ref, rest_ref = rest[-2:]

    @pl.when(pl.program_id(0) == 0)
    def _():
        first_ref[0] = total.astype(BF16)

    @pl.when(pl.program_id(0) > 0)
    def _():
        rest_ref[0] = total.astype(BF16)


def pair_grad(at, own, low, high, grad, grad_far, after):
    length, units = grad.shape
    width = own.shape[1] // 8
    whole = pl.BlockSpec((length, units), lambda k, at: (0, 0))
    side = pl.BlockSpec((length // 2, width), lambda k, at: (0, k))
    return pl.pallas_call(
        pair_kernel,
        grid_spec=pltpu.PrefetchScalarGridSpec(
            num_scalar_prefetch=1,
            grid=(4,),
            in_specs=[
                pl.BlockSpec((length, width), lambda k, at: (0, at[k])), side, side, whole, whole,
            ] + [ANY] * len(after),
            out_specs=(
                pl.BlockSpec((1, width, units), lambda k, at: (0, 0, 0)),
                pl.BlockSpec((1, width, units), lambda k, at: (jnp.maximum(k - 1, 0), 0, 0)),
            ),
        ),
        out_shape=tuple(jax.ShapeDtypeStruct((n, width, units), BF16) for n in (1, 3)),
        compiler_params=params(1),
        cost_estimate=cost(
            16 * length * width * units, 2 * units * (2 * length + 4 * width) + 16 * length * width
        ),
    )(at, own, low, high, grad, grad_far, *after)


def merge_kernel(left_ref, right_ref, *rest):
    rest[-1][...] = (left_ref[...].astype(F32) + right_ref[...].astype(F32)).astype(BF16)


def merge(left, right, after):
    spec = pl.BlockSpec((1,) + left.shape[1:], lambda k: (k, 0, 0))
    return pl.pallas_call(
        merge_kernel,
        grid=(left.shape[0],),
        in_specs=[spec, spec] + [ANY] * len(after),
        out_specs=spec,
        out_shape=jax.ShapeDtypeStruct(left.shape, BF16),
        compiler_params=params(1),
        cost_estimate=cost(left.size, 6 * left.size),
    )(left, right, *after)


def cross_kernel(at_ref, first_ref, rest_ref, in_ref, out_ref):
    part = jnp.where(pl.program_id(0) == 0, first_ref[...], rest_ref[...]).astype(F32)
    keep = jnp.where(at_ref[0] == 1, in_ref[...].astype(F32), 0.0)
    out_ref[...] = (part + keep).astype(BF16)


def cross_add(inner, first, rest, crossed):
    block = (1,) + rest.shape[1:]
    here = pl.BlockSpec(block, lambda k, at: (0, 0, 0))
    return pl.pallas_call(
        cross_kernel,
        grid_spec=pltpu.PrefetchScalarGridSpec(
            num_scalar_prefetch=1,
            grid=(2,),
            in_specs=[here, here, pl.BlockSpec(block, lambda k, at: (1 - k, 0, 0))],
            out_specs=pl.BlockSpec(block, lambda k, at: (k, 0, 0)),
        ),
        out_shape=jax.ShapeDtypeStruct((2,) + rest.shape[1:], BF16),
        compiler_params=params(1),
        cost_estimate=cost(crossed.size, 6 * crossed.size),
    )(inner, first, rest, crossed)


def add_rows(target, *sources):
    step = 32

    def body(i, carry):
        rows = pl.ds(pl.multiple_of(i * step, step), step)
        total = sources[0][rows].astype(F32)
        for source in sources[1:]:
            total = total + source[rows].astype(F32)
        target[rows] = total.astype(target.dtype)
        return carry

    lax.fori_loop(0, target.shape[0] // step, body, 0)


def line_kernel(ready, merged, count, pairs, *refs):
    refs = list(refs)
    take = lambda size: [refs.pop(0) for unused in range(size)]
    total = count + pairs
    first = take(count)
    rest = dict(zip(range(ready, count), take(count - ready)))
    grads, [own, low, high] = take(pairs), take(3)
    outs = take(total)
    late = range(ready + merged, total)
    open_ends = range(ready, total)
    first += take(pairs)
    rest.update(zip(range(count, total), take(pairs)))
    far = take(pairs)
    from_outer = dict(zip(late, take(len(late))))
    from_inner = dict(zip(open_ends, take(len(open_ends))))
    last = take(total)
    send_out, got_out, send_in, got_in, send_last, got_last, send_x, got_x = refs
    dp, mp = lax.axis_index("dp"), lax.axis_index("mp")
    z, x = dp // 2, dp % 2
    beside = ((z + 1 - 2 * (z % 2)) * 2 + x, mp)
    across = ((3 - z) * 2 + x, mp)
    partner = (z * 2 + 1 - x, mp)
    flip = z // 2
    inner = (z == 1) | (z == 2)
    outer = (z == 0) | (z == 3)
    mesh_id = pl.DeviceIdType.MESH
    barrier = pltpu.get_barrier_semaphore()
    for device in (beside, partner):
        pl.semaphore_signal(barrier, inc=1, device_id=device, device_id_type=mesh_id)

    def copy(source, target, sent, got, device):
        return pltpu.make_async_remote_copy(
            src_ref=source, dst_ref=target, send_sem=sent, recv_sem=got,
            device_id=device, device_id_type=mesh_id,
        )

    def copy_out(g):
        return copy(rest[g], from_outer[g], send_out.at[g], got_out.at[g], beside)

    def copy_in(g):
        source = (from_outer if g in late else rest)[g].at[pl.ds(1, 2)]
        return copy(source, from_inner[g], send_in.at[g], got_in.at[g], across)

    def copy_last(g):
        source = first[g].at[0] if g < ready else from_inner[g].at[1]
        return copy(source, last[g], send_last.at[g], got_last.at[g], beside)

    def copy_grad(p):
        return copy(grads[p], far[p], send_x.at[p], got_x.at[p], partner)

    def multiply(p):
        copy_grad(p).wait_recv()
        half, width = low.shape[0], first[count + p].shape[1]

        def body(k, carry):
            lane = k + flip * (3 - 2 * k)
            at = pl.ds(pl.multiple_of((2 * lane + x) * width, width), width)
            side = pl.ds(pl.multiple_of(k * width, width), width)
            value = rows_dot(own[:, at], grads[p][...])
            value += rows_dot(low[:, side], far[p][:half])
            value += rows_dot(high[:, side], far[p][half:])

            @pl.when(k == 0)
            def _():
                first[count + p][0] = value.astype(BF16)

            @pl.when(k > 0)
            def _():
                rest[count + p][jnp.maximum(k - 1, 0)] = value.astype(BF16)

            return carry

        lax.fori_loop(0, 4, body, 0)

    large = [g for g in late if g < count and first[g].shape[1] >= 256]
    small = [g for g in late if g < count and first[g].shape[1] < 256]
    sequence = large + list(range(count, total)) + small

    @pl.when(outer)
    def _():
        pl.semaphore_wait(barrier, 2)
        for p in range(pairs):
            copy_grad(p).start()
        for g in sequence:
            if g >= count:
                multiply(g - count)
            copy_out(g).start()
        for g in list(range(ready + merged)) + sequence:
            copy_last(g).wait_recv()
            add_rows(outs[g], first[g].at[0], last[g])
        for g in late:
            copy_out(g).wait_send()

    @pl.when(inner)
    def _():
        pl.semaphore_signal(barrier, inc=1, device_id=across, device_id_type=mesh_id)
        pl.semaphore_wait(barrier, 3)
        for p in range(pairs):
            copy_grad(p).start()
        for g in range(ready):
            copy_last(g).start()
        for g in range(ready, ready + merged):
            copy_in(g).start()

        def begin(g):
            copy_out(g).wait_recv()
            for k in (1, 2):
                add_rows(from_outer[g].at[k], rest[g].at[k], from_outer[g].at[k])
            copy_in(g).start()

        def finish(g):
            copy_in(g).wait_recv()
            add_rows(from_inner[g].at[1], first[g].at[0], from_inner[g].at[1])
            copy_last(g).start()
            near = [from_outer[g].at[0]] if g in late else []
            add_rows(outs[g], rest[g].at[0], from_inner[g].at[0], *near)

        for g in range(ready):
            add_rows(outs[g], first[g].at[1])
        waiting = list(range(ready, ready + merged))
        for g in sequence:
            if g >= count:
                multiply(g - count)
            begin(g)
            waiting.append(g)
            if len(waiting) > 1:
                finish(waiting.pop(0))
        for g in waiting:
            finish(g)
        for g in open_ends:
            copy_in(g).wait_send()
        for g in range(total):
            copy_last(g).wait_send()

    for p in range(pairs):
        copy_grad(p).wait_send()


def line_sums(ready_parts, merged_parts, late_parts, grads, own, low, high):
    open_parts = list(merged_parts) + list(late_parts)
    parts = list(ready_parts) + [first for first, unused in open_parts]
    rests = [rest for unused, rest in open_parts]
    ready, merged, count, pairs = len(ready_parts), len(merged_parts), len(parts), len(grads)
    width = own.shape[1] // 8
    shapes = [p.shape[1:] for p in parts] + [(width, g.shape[1]) for g in grads]
    total, late = count + pairs, shapes[ready + merged :]
    assert ready + merged <= count and merged <= 1
    vmem = pl.BlockSpec(memory_space=pltpu.VMEM)
    sizes = [r * k for r, k in shapes]
    return pl.pallas_call(
        functools.partial(line_kernel, ready, merged, count, pairs),
        in_specs=[vmem] * (count + len(rests) + pairs + 3),
        out_specs=[vmem] * total,
        out_shape=[jax.ShapeDtypeStruct(shape, F32) for shape in shapes],
        scratch_shapes=[pltpu.VMEM((n,) + shape, BF16) for n in (1, 3) for shape in shapes[count:]]
        + [pltpu.VMEM(g.shape, BF16) for g in grads]
        + [pltpu.VMEM((3,) + shape, BF16) for shape in late]
        + [pltpu.VMEM((2,) + shape, BF16) for shape in shapes[ready:]]
        + [pltpu.VMEM(shape, BF16) for shape in shapes]
        + [pltpu.SemaphoreType.DMA((total,))] * 6
        + [pltpu.SemaphoreType.DMA((pairs,))] * 2,
        compiler_params=pltpu.CompilerParams(
            collective_id=0, has_side_effects=True, vmem_limit_bytes=56 * 2**20
        ),
        cost_estimate=cost(4 * sum(sizes), 40 * sum(sizes)),
    )(*parts, *rests, *grads, own, low, high)


CHUNKS = 4


def boundary_kernel(mode, jobs, plain, partial, rows, kept, gain, *refs):
    refs = list(refs)
    take = lambda size: [refs.pop(0) for unused in range(size)]
    wanted = take(jobs)
    [sums] = take(1) if mode != "first" else [None]
    [gathered] = take(1) if mode not in ("last", "sum") else [None]
    [gain_out] = take(1) if mode in ("backward", "last") else [None]
    [kept_out] = take(1) if mode == "sum" else [None]
    low_out, high_out = take(jobs), take(0 if plain else jobs)
    from_core, far_sum, from_chip, whole = take(4)
    low, high = take(jobs), take(0 if plain else jobs)
    sends, gots = take(2)
    if jobs:
        send_jobs, got_jobs = take(2)
    if mode == "sum":
        running, others, send_kept, got_kept = take(4)
    dp, mp = lax.axis_index("dp"), lax.axis_index("mp")
    core = (dp, mp + 1 - 2 * (mp % 2))
    chip = (dp, (mp + 2) % 4)
    mesh_id = pl.DeviceIdType.MESH
    step = rows.shape[0]
    size = step // CHUNKS
    barrier = pltpu.get_barrier_semaphore()
    beside = (dp + 1 - 2 * (dp % 2), mp)
    near = (core, chip, beside) if jobs or mode == "sum" else (core, chip)
    for device in near:
        pl.semaphore_signal(barrier, inc=1, device_id=device, device_id_type=mesh_id)
    pl.semaphore_wait(barrier, len(near))

    def job(hop, k):
        source, target = ((wanted, low), (low, high))[hop]
        return pltpu.make_async_remote_copy(
            src_ref=source[k], dst_ref=target[k], send_sem=send_jobs.at[hop, k],
            recv_sem=got_jobs.at[hop, k], device_id=(beside, core)[hop], device_id_type=mesh_id,
        )

    for k in range(jobs):
        job(0, k).start()

    def copy(kind, c, source, target, device):
        return pltpu.make_async_remote_copy(
            src_ref=source, dst_ref=target, send_sem=sends.at[kind, c], recv_sem=gots.at[kind, c],
            device_id=device, device_id_type=mesh_id,
        )

    def part(block, c):
        return pl.ds(block * step + c * size, size)

    def core_sum(block, c):
        return copy(
            block, c, partial.at[part(2 + block, c)], from_core.at[part(block, c)], core
        )

    def chip_sum(c):
        return copy(2, c, far_sum.at[part(0, c)], from_chip.at[part(0, c)], chip)

    def chip_row(c):
        return copy(3, c, whole.at[part(0, c)], whole.at[part(1, c)], chip)

    def core_row(block, c):
        return copy(
            4 + block, c, whole.at[part(block, c)], whole.at[part(2 + block, c)], core
        )

    every = range(CHUNKS)
    wide = lambda value: value.astype(F32)
    if mode != "first":
        for block in (1, 0):
            for c in every:
                core_sum(block, c).start()
        for c in every:
            core_sum(1, c).wait_recv()
            total = wide(partial[part(1, c)]) + wide(from_core[part(1, c)])
            far_sum[part(0, c)] = total.astype(BF16)
            chip_sum(c).start()
    if gain_out is not None:
        gain_out[...] = jnp.zeros_like(gain_out)
    for c in every:
        here = part(0, c)
        if mode == "first":
            value = wide(rows[here])
        else:
            core_sum(0, c).wait_recv()
            chip_sum(c).wait_recv()
            total = wide(partial[here]) + wide(from_core[here]) + wide(from_chip[here])
            if mode in ("forward", "sum"):
                value = wide(rows[here]) + total
                sums[here] = value
            else:
                old = kept[here]
                inv = inverse_rms(old)
                weighted = gain[...] * total
                inner = jnp.mean(old * weighted, axis=-1, keepdims=True)
                value = wide(rows[here]) + inv * weighted - old * (inv * inv * inv) * inner
                gain_out[...] += jnp.sum(total * old * inv, axis=0, keepdims=True)
                sums[here] = value
        if gathered is not None:
            if mode != "backward":
                value = value * inverse_rms(value) * gain[...]
            whole[here] = value.astype(BF16)
            chip_row(c).start()
            core_row(0, c).start()
    if gathered is not None:
        for c in every:
            chip_row(c).wait_recv()
            core_row(1, c).start()
        for c in every:
            for block in range(2):
                core_row(block, c).wait_recv()
        gathered[...] = whole[...]
    if mode == "sum":
        running[...] = kept[...]
        hops = []
        for k, device in enumerate((core, chip, beside)):
            hop = pltpu.make_async_remote_copy(
                src_ref=running, dst_ref=others.at[k], send_sem=send_kept.at[k],
                recv_sem=got_kept.at[k], device_id=device, device_id_type=mesh_id,
            )
            hop.start()
            hop.wait()
            running[...] = running[...] + others[k]
        kept_out[...] = running[...]
    for k in range(jobs):
        job(0, k).wait_recv()
        if not plain:
            job(1, k).start()
        low_out[k][...] = low[k][...]
    for k in range(jobs):
        job(0, k).wait_send()
        if not plain:
            job(1, k).wait_recv()
            high_out[k][...] = high[k][...]
            job(1, k).wait_send()
    for c in every:
        if mode != "first":
            core_sum(0, c).wait_send()
            core_sum(1, c).wait_send()
            chip_sum(c).wait_send()
        if gathered is not None:
            chip_row(c).wait_send()
            core_row(0, c).wait_send()
            core_row(1, c).wait_send()


def boundary(mode, number, partial, rows, kept, gain, wanted=(), plain=False):
    step, width = rows.shape
    vmem = pl.BlockSpec(memory_space=pltpu.VMEM)
    shapes = []
    if mode != "first":
        shapes.append(jax.ShapeDtypeStruct((step, width), F32))
    if mode not in ("last", "sum"):
        shapes.append(jax.ShapeDtypeStruct((4 * step, width), BF16))
    if mode in ("backward", "last"):
        shapes.append(jax.ShapeDtypeStruct((1, width), F32))
    if mode == "sum":
        shapes.append(jax.ShapeDtypeStruct(kept.shape, F32))
    jobs = len(wanted)
    hops = 1 if plain else 2
    shapes += [jax.ShapeDtypeStruct(w.shape, BF16) for w in wanted] * hops
    scratch = [pltpu.VMEM(w.shape, BF16) for w in wanted] * hops
    outs = pl.pallas_call(
        functools.partial(boundary_kernel, mode, jobs, plain),
        in_specs=[vmem] * (4 + jobs),
        out_specs=[vmem] * len(shapes),
        out_shape=shapes,
        scratch_shapes=[
            pltpu.VMEM((2 * step, width), BF16),
            pltpu.VMEM((step, width), BF16),
            pltpu.VMEM((step, width), BF16),
            pltpu.VMEM((4 * step, width), BF16),
        ]
        + scratch
        + [pltpu.SemaphoreType.DMA((6, CHUNKS))] * 2
        + ([pltpu.SemaphoreType.DMA((2, jobs))] * 2 if jobs else [])
        + (
            [pltpu.VMEM(kept.shape, F32), pltpu.VMEM((3,) + kept.shape, F32)]
            + [pltpu.SemaphoreType.DMA((3,))] * 2
            if mode == "sum"
            else []
        ),
        compiler_params=pltpu.CompilerParams(
            collective_id=number, has_side_effects=True, vmem_limit_bytes=2 * VMEM_LIMIT
        ),
        cost_estimate=cost(10 * step * width, 60 * 2**20),
    )(partial, rows, kept, gain, *wanted)
    if not jobs or plain:
        return outs
    halves = list(zip(outs[-2 * jobs : -jobs], outs[-jobs:]))
    return list(outs[: -2 * jobs]) + halves


def gated_unit(gate_arg, up_arg):
    return jax.nn.gelu(gate_arg, approximate=True) * up_arg


def layer(n_dp, n_mp):
    lanes = n_dp // 2
    paired = n_dp == 8

    def swap(value, axis, size, bit):
        return lax.ppermute(value, axis, [(i, i ^ bit) for i in range(size)])

    def core(value):
        return swap(value, "mp", n_mp, 1)

    def chip(value):
        return swap(value, "mp", n_mp, 2)

    def beside(value):
        return swap(value, "dp", n_dp, 1)

    def gather(mine):
        far = chip(mine)
        return assemble([mine, far, core(mine), core(far)])

    def gather_after(mine, after):
        return gather(tie(mine, after))

    def scatter_rows(partial):
        step = partial.shape[0] // 4
        block = [partial[k * step : (k + 1) * step] for k in range(4)]
        far = (block[1].astype(F32) + core(block[3]).astype(F32)).astype(BF16)
        far_in = chip(far)
        return block[0].astype(F32) + core(block[2]).astype(F32) + far_in.astype(F32)

    def line_place():
        z = lax.axis_index("dp") // 2
        number = lambda value: jnp.asarray(value).astype(jnp.int32)
        return lax.axis_index("dp") % 2, number(z >= 2), number((z == 1) | (z == 2))

    def outer_swap(value):
        return swap(value, "dp", n_dp, 2)

    def inner_swap(value):
        pairs = []
        for d in range(n_dp):
            for m in range(n_mp):
                inner = d // 2 in (1, 2)
                to = (d ^ 6) * n_mp + m if inner else d * n_mp + (m ^ 1)
                pairs.append((d * n_mp + m, to))
        return lax.ppermute(value, ("dp", "mp"), pairs)

    def lane_columns(parity):
        flip = line_place()[1]
        k = jnp.arange(4, dtype=jnp.int32)
        return 2 * (k + flip * (3 - 2 * k)) + parity

    def wanted_of(value, half=None):
        rows = value.shape[0] // 2
        if half is not None:
            value = pick_rows(jnp.stack([half]).astype(jnp.int32), value, rows)
        x = line_place()[0]
        return pick_columns(lane_columns(1 - x), value, rows, value.shape[1] // n_dp)

    def shards(
        tokens, norm_gains, w_query, w_key, w_value, w_out, c_query, c_key, c_value, c_out,
        patch_proj, w_gate, w_up, w_down, patches, segment_ids, image_index, cotangent,
    ):
        length = segment_ids.shape[1]
        model = tokens.shape[2]
        patch_rows = patches.shape[0] * patches.shape[1]
        m = lax.axis_index("mp")
        order = [m, m ^ 2, m ^ 1, m ^ 3]

        def blocks(arr, axis=0):
            step = arr.shape[axis] // 4
            return jnp.concatenate(
                [lax.dynamic_slice_in_dim(arr, k * step, step, axis) for k in order], axis=axis
            )

        places = blocks(jnp.arange(length, dtype=jnp.int32))
        segment_row = blocks(segment_ids[0])
        slots = jnp.arange(SEGS, dtype=jnp.int32)
        token_image = jnp.sum(
            jnp.where(segment_row[:, None] == slots, image_index[0][None, :], 0), axis=-1
        )
        patch_image = jnp.arange(patch_rows, dtype=jnp.int32) // patches.shape[1]

        far_of = beside if paired else (lambda value: value)
        core_bit = m % 2

        def exchange(*values):
            return [wanted_of(*value) for value in values] if paired else []

        def split(value, halves):
            return (value, *halves) if paired else (value,)

        def split_now(value):
            if not paired:
                return (value,)
            wanted = wanted_of(value)
            low = beside(wanted)
            return value, low, core(low)

        self_rows = jnp.stack([segment_row, places], axis=1)
        self_cols = self_rows.T
        cross_rows, cross_cols = token_image[:, None], patch_image[None, :]
        residual = tokens[0].astype(F32)
        gain_rows = [norm_gains[k : k + 1] for k in range(3)]
        nothing = jnp.zeros((16, 128), BF16)
        none = [None] * 4
        [normed_one] = boundary("first", 1, nothing, tokens[0], nothing, gain_rows[0])
        patch_own = patches.reshape(patch_rows, patches.shape[2])
        projected = matmul(patch_own, patch_proj).astype(BF16)
        queries = matmul(normed_one, w_query).astype(BF16)
        key_rows = matmul(normed_one, w_key).astype(BF16)
        value_rows = matmul(normed_one, w_value).astype(BF16)
        self_mixed = attend(queries, key_rows, value_rows, self_rows, self_cols, True)
        self_far = far_of(self_mixed)
        grad_three = gather_after(cotangent[0], normed_one)
        split_one = split_now(normed_one)
        self_mixed = tie(self_mixed, (grad_three, split_one))
        partial = matmul(self_mixed, w_out).astype(BF16)
        after_self, normed_two, *halves = boundary(
            "forward", 2, partial, tokens[0], nothing, gain_rows[1], exchange((projected, core_bit), (grad_three,))
        )
        patch_low, patch_high = halves[0] if paired else (None, None)
        [split_cotangent] = map(split, (grad_three,), halves[1:] or none)
        normed_two = tie(normed_two, self_far)
        cross_keys = matmul(projected, c_key).astype(BF16)
        cross_values = matmul(projected, c_value).astype(BF16)
        cross_queries = matmul(normed_two, c_query).astype(BF16)
        cross_mixed = attend(
            cross_queries, cross_keys, cross_values, cross_rows, cross_cols, False
        )
        mixed_far = far_of(cross_mixed)
        partial = matmul(cross_mixed, c_out).astype(BF16)
        after_cross, normed_three, *halves = boundary(
            "forward", 3, partial, after_self, nothing, gain_rows[2],
            exchange((normed_two,)),
        )
        [split_two] = map(split, (normed_two,), halves or none)
        grad_hidden = tie(product("sd,fd->sf", grad_three, w_down), ())
        if paired:
            wanted = wanted_of(normed_three)
            low_three = beside(wanted)
            split_three = normed_three, low_three, core(low_three)
            normed_three = tie(normed_three, (grad_hidden, mixed_far, wanted))
        else:
            split_three, low_three = (normed_three,), normed_three
        gate_pre, up_pre = matmul(normed_three, w_gate), matmul(normed_three, w_up)
        hidden, pull = jax.vjp(gated_unit, gate_pre, up_pre)
        hidden = hidden.astype(BF16)
        grad_gate, grad_up = [g.astype(BF16) for g in pull(grad_hidden)]

        results, turned = {}, {}

        def line(name, split, grad, grad_far, rows_first, after=()):
            turned[name] = not rows_first
            if not paired:
                partial = product("td,te->de", split[0], grad).astype(BF16)
                total = lax.psum_scatter(partial, "dp", scatter_dimension=0, tiled=True)
                results[name] = total.astype(F32)
                return ()
            results[name] = pair_grad(
                lane_columns(line_place()[0]), *split, grad, grad_far, after
            )
            return results[name]

        def line_out(name):
            return outer_swap(results[name][1]) if paired else None

        def line_merge(name, incoming, after):
            if paired:
                first, rest = results[name]
                results[name] = first, merge(rest, incoming, after)

        def line_across(name):
            if paired:
                inner = line_place()[2]
                first, rest = results[name]
                results[name] = cross_add(inner.reshape(1), first, rest, inner_swap(rest[1:]))

        hidden_far = far_of(tie(hidden, low_three))
        partial = (
            product("sf,df->sd", grad_gate, w_gate) + product("sf,df->sd", grad_up, w_up)
        ).astype(BF16)
        gate_far, up_far = [far_of(v) for v in tie((grad_gate, grad_up), partial)]
        sent = line("down", split_cotangent, hidden, hidden_far, False, (partial,))
        incoming_down = line_out("down")
        grad_rows, grad_two, gain_three = boundary(
            "backward", 4, tie(partial, sent), cotangent[0], after_cross, gain_rows[2]
        )
        sent = line("gate", split_three, grad_gate, gate_far, True, (grad_two,))
        incoming_gate = line_out("gate")
        grad_two = tie(grad_two, sent)

        grad_mixed = product("sd,ed->se", grad_two, c_out).astype(BF16)
        grad_cq, grad_ck, grad_cv = attend_back(
            cross_queries, cross_keys, cross_values, cross_rows, cross_cols, grad_mixed, False
        )
        cq_far, ck_far, cv_far = far_of(grad_cq), far_of(grad_ck), far_of(grad_cv)
        partial = product("se,de->sd", grad_cq, c_query).astype(BF16)
        sent = line("up", split_three, grad_up, up_far, True, (partial,))
        incoming_up = line_out("up")
        line_merge("down", incoming_down, (partial,))
        grad_rows, grad_one, gain_two = boundary(
            "backward", 5, tie(partial, (sent, results["down"])), grad_rows, after_self, gain_rows[1]
        )
        line_across("down")

        grad_mixed = product("sd,ed->se", grad_one, w_out).astype(BF16)
        grad_sq, grad_sk, grad_sv = attend_back(
            queries, key_rows, value_rows, self_rows, self_cols, grad_mixed, True
        )
        partial = (
            product("se,de->sd", grad_sq, w_query)
            + product("se,de->sd", grad_sk, w_key)
            + product("se,de->sd", grad_sv, w_value)
        ).astype(BF16)
        width = model // (n_dp * n_mp)

        def projected_block(k):
            def rows_of(weight):
                cut = weight.reshape(n_dp, n_mp, width, weight.shape[1])
                return lax.dynamic_index_in_dim(cut, k, 1, keepdims=False).reshape(
                    n_dp * width, weight.shape[1]
                )

            return (cols_dot(late_ck, rows_of(c_key)) + cols_dot(late_cv, rows_of(c_value))).astype(
                BF16
            )

        late_ck, late_cv = tie((grad_ck, grad_cv), grad_one)
        block = [projected_block(k) for k in order]
        far = (block[1].astype(F32) + core(block[3]).astype(F32)).astype(BF16)
        near = (block[0].astype(F32) + core(block[2]).astype(F32)).astype(BF16)
        far_in = chip(far)
        line_merge("gate", incoming_gate, (partial,))
        line("c_query", split_two, grad_cq, cq_far, True, (partial,))
        split_patch = (projected,)
        if paired:
            swapped = core_bit == 1
            split_patch = (
                projected,
                jnp.where(swapped, patch_high, patch_low),
                jnp.where(swapped, patch_low, patch_high),
            )
        sent = line("c_key", split_patch, grad_ck, ck_far, True, (partial,))
        grad_rows, gain_one, *halves = boundary(
            "last", 6, tie(partial, (sent, far, near, results["gate"], results["down"])), grad_rows,
            residual, gain_rows[0], exchange((grad_two,), (grad_one,)),
        )
        line_across("gate")
        split_grad_two, split_grad_one = map(split, (grad_two, grad_one), halves or none)
        grad_projected = (near.astype(F32) + far_in.astype(F32)).astype(BF16)
        patch_partial = rows_dot(grad_projected, patch_own).astype(BF16)
        x, flip, unused = line_place()
        patch_parts = patch_partial.reshape(n_dp // 2, 2, width, patches.shape[2])
        patch_sent = lax.dynamic_index_in_dim(patch_parts, 1 - x, 1, keepdims=False)
        partial = matmul(tie(hidden, grad_rows), w_down).astype(BF16)
        gains = jnp.concatenate([gain_one, gain_two, gain_three], axis=0)
        gains_wide = jnp.pad(gains, ((0, 5), (0, 0)))
        output, gains_near, *patch_got = boundary(
            "sum", 7, partial, after_cross, gains_wide, gain_rows[0],
            [patch_sent.reshape(-1, patches.shape[2])] if paired else [], True,
        )
        line("c_value", split_patch, grad_cv, cv_far, True, (grad_rows,))
        line("c_out", split_grad_two, cross_mixed, mixed_far, False, (grad_rows,))
        line("w_out", split_grad_one, self_mixed, self_far, False, (grad_rows,))
        line_merge("up", incoming_up, (grad_rows,))
        if paired:
            kept = lax.dynamic_index_in_dim(patch_parts, x, 1, keepdims=False)
            summed = kept.astype(F32) + patch_got[0].reshape(kept.shape).astype(F32)
            summed = jnp.where(flip == 1, summed[::-1], summed).astype(BF16)
            results["patch"] = summed[:1], summed[1:]
            mine = lax.dynamic_index_in_dim(
                gains_near[:3].reshape(3, 4, 2, n_mp, width), x, 2, keepdims=False
            )
            mine = lax.dynamic_index_in_dim(mine, m, 2, keepdims=False).transpose(1, 0, 2)
            mine = jnp.where(flip == 1, mine[::-1], mine)
            mine = jnp.pad(mine, ((0, 0), (0, 29), (0, 128 - width))).astype(BF16)
            results["gains"] = mine[:1], mine[1:]
            early, late = ["down", "gate", "up"], ["c_out", "c_query", "c_key", "c_value", "w_out"]
            late += ["patch", "gains"]
            names = early + late + ["w_query", "w_key", "w_value"]
            sums = line_sums(
                [results["down"], results["gate"]], [results["up"]], [results[n] for n in late],
                [grad_sq, grad_sk, grad_sv], *split_one,
            )
            results.update(zip(names, sums))
        else:
            results["patch"] = lax.psum_scatter(
                patch_partial, "dp", scatter_dimension=0, tiled=True
            ).astype(F32)
            line("w_query", split_one, grad_sq, grad_sq, True)
            line("w_key", split_one, grad_sk, grad_sk, True)
            line("w_value", split_one, grad_sv, grad_sv, True)
        turned["patch"] = True
        results = {n: v.T if turned.get(n) else v for n, v in results.items()}
        patch_total = results["patch"]
        if paired:
            gain_total = results["gains"][:3, :width]
        else:
            gain_total = lax.psum_scatter(
                gains, ("dp", "mp"), scatter_dimension=1, tiled=True,
            )
        sum_query, sum_key, sum_value = results["w_query"], results["w_key"], results["w_value"]
        sum_cquery, sum_ckey, sum_cvalue = results["c_query"], results["c_key"], results["c_value"]
        sum_out, sum_cout, sum_down = results["w_out"], results["c_out"], results["down"]
        sum_gate, sum_up = results["gate"], results["up"]
        return (
            output.astype(BF16)[None], grad_rows[None], gain_total,
            sum_query, sum_key, sum_value, sum_out,
            sum_cquery, sum_ckey, sum_cvalue, sum_cout,
            patch_total, sum_gate, sum_up, sum_down,
        )

    return shards


def solution(mesh):
    columns, rows = P(None, "mp"), P("mp", None)
    return jax.shard_map(
        layer(mesh.shape["dp"], mesh.shape["mp"]),
        mesh=mesh,
        in_specs=(
            P("dp", "mp", None), P(), columns, columns, columns, rows, columns, columns, columns,
            rows, P(), columns, columns, rows, P("dp", None, None), P("dp", None), P("dp", None),
            P("dp", "mp", None),
        ),
        out_specs=(
            P("dp", "mp", None), P("dp", "mp", None), P(None, ("dp", "mp")),
            P("dp", "mp"), P("dp", "mp"), P("dp", "mp"), P("mp", "dp"),
            P("dp", "mp"), P("dp", "mp"), P("dp", "mp"), P("mp", "dp"),
            P(None, ("dp", "mp")), P("dp", "mp"), P("dp", "mp"), P("mp", "dp"),
        ),
        check_vma=False,
    )
```

time: 908 us -> 672 us (0.74)
  waiting for transfers between devices: 347 us -> 23.3 us
  Pallas kernels: 278 us -> 479 us
  starting transfers between devices: 56.3 us -> 18.3 us
  other arithmetic: 28.3 us -> 3.95 us
  local copies, waits for them, and re-layouts: 82.1 us -> 60.7 us
  matrix products: 89.1 us -> 75.2 us
  between operations: 16.6 us -> 2.76 us
    ppermute x71 -> x21, waiting for transfers between devices: 347 us -> 23.3 us  [swap(): return lax.ppermute(value, axis, [(i, i ^ bit) for i in range(size)])]
    pallas_call x7 -> x15, Pallas kernels: 198 us -> 425 us  [the longest x7 207 us: boundary(): pl.pallas_call(functools.partial(boundary_kernel, mode, jobs, plain), in_...]
    ppermute x71 -> x21, starting transfers between devices: 55.3 us -> 17.8 us  [swap(): return lax.ppermute(value, axis, [(i, i ^ bit) for i in range(size)])]
    dot_general x21 -> x9, matrix products: 44.5 us -> 23.4 us  [product(): return jnp.einsum(spec, left, right, preferred_element_type=F32)]
    convert_element_type x8 -> x0, local copies, waits for them, and re-layouts: 15.1 us -> none  [flat_heads(): return arr.reshape(arr.shape[0], -1).astype(BF16)]
    convert_element_type x14 -> x2, other arithmetic: 13.4 us -> 1.28 us  [the longest x1 1.13 us: shards(): residual = tokens[0].astype(F32)]
    pallas_call x11 -> x8, Pallas kernels: 54.1 us -> 42 us  [pair_grad(): pl.pallas_call(pair_kernel, grid_spec=pltpu.PrefetchScalarGridSpec(num_sc...]
    pallas_call x7 -> x1, Pallas kernels: 12 us -> 2.55 us  [assemble(): pl.pallas_call(assemble_kernel, grid=(width // columns,), in_specs=[pl.Bl...]
  transfers between devices with their start and end apart: 75 -> 23, of which waited for: 20 -> 1; matrix products, arithmetic and copies ran while one was open for 14% -> 12% of each run, Pallas kernels for 31% -> 38%
where the time goes in v4:
time: 672 us; the launch traced here: 663 us
  Pallas kernels  479 us (71%)
  matrix products  75.2 us (11%)
  local copies, waits for them, and re-layouts  60.7 us (9%)
  waiting for transfers between devices  23.3 us (3%)
  starting transfers between devices  18.3 us (3%)
    pallas_call x7, Pallas kernels, boundary(): pl.pallas_call(functools.partial(boundary_kernel, mode, jobs, plain), in_...  207 us
    pallas_call x1, Pallas kernels, line_sums(): pl.pallas_call(functools.partial(line_kernel, ready, merged, count, pairs...  178 us
    unnamed x282, local copies, waits for them, and re-layouts  50 us
    pallas_call x8, Pallas kernels, pair_grad(): pl.pallas_call(pair_kernel, grid_spec=pltpu.PrefetchScalarGridSpec(num_sc...  42 us
    dot_general x12, matrix products, matmul(): return jnp.dot(left, right, preferred_element_type=F32)  39.5 us
    dot_general x9, matrix products, product(): return jnp.einsum(spec, left, right, preferred_element_type=F32)  23.4 us
    ppermute x21, waiting for transfers between devices, swap(): return lax.ppermute(value, axis, [(i, i ^ bit) for i in range(size)])  23.3 us
    ppermute x21, starting transfers between devices, swap(): return lax.ppermute(value, axis, [(i, i ^ bit) for i in range(size)])  17.8 us
  transfers between devices with their start and end apart: 23, of which 1 were waited for; matrix products, arithmetic and copies ran while one was open for 12% of the time, Pallas kernels for 38%

profile of v4, /device:TPU:0, one launch (start us, length us, event | category | flops | bytes accessed | tf_op | source)
XLA Modules:
  0.0 663.0 jit_solution(7811627641466305854)
XLA Ops:
  2.8 17.1 %shard_map.289.in_ref.refs_21_ = bf16[512,2048]{1,0:T(8,128)(2,1)S(1)} custom-call(bf16[16,128]{1,0:T(8,128)(2,1)S(1)} %broadcast_in_dim.29.partial.kept, bf16[128,2048]{1,0:T(8,128)(2,1)S(1)} %bitcast.113, bf16[16,128]{1,0:T(8,128)(2,1)S(1)} %broadcast_in_dim.29.partial.kept, f32[1,2048]{1,0:T(1,128)S(1)} %get-tuple-element.222.gain), custom_call_target="tpu_custom_call" | custom-call | flops 2621440 | bytes 62914560 | tf_op jit(solution)/shard_map/pallas_call | solution.py:640
  35.8 5.7 shard_map.290.g_ref
  42.1 7.9 %convolution_convert_fusion.in_ref.a_ref = bf16[1024,2048]{1,0:T(8,128)(2,1)S(1)} fusion(bf16[1024,1664]{1,0:T(8,128)(2,1)S(1)} %bitcast.110, bf16[1664,2048]{1,0:T(8,128)(2,1)S(1)} %bitcast.139), kind=kOutput, calls=%fused_computation.2 | convolution fusion | flops 6981419008 | bytes 14417920 | tf_op jit(solution)/shard_map/dot_general | solution.py:19
  69.8 38.9 %shard_map.296 = (f32[128,2048]{1,0:T(8,128)S(1)}, bf16[512,2048]{1,0:T(8,128)(2,1)S(1)}, bf16[512,1024]{1,0:T(8,128)(2,1)S(1)}, bf16[256,1024]{1,0:T(8,128)(2,1...) custom-call(bf16[512,2048]{1,0:T(8,128)(2,1)S(1)} %convolution_convert_fusion.5.partial, ...), custom_call_target="tpu_custom_call" | custom-call | flops 2621440 | bytes 62914560 | tf_op jit(solution)/shard_map/pallas_call | solution.py:640
  115.3 7.3 %shard_map.297.g_ref = bf16[512,512]{1,0:T(8,128)(2,1)S(1)} custom-call(bf16[512,512]{1,0:T(8,128)(2,1)S(1)} %convolution_convert_fusion.10.q_ref, bf16[1024,512]{1,0:T(8,128)(2,1)S(1)} %copy-done.86, bf16[1024,512]{1,0:T(8,128)(2,1)S(1)} %copy-done.84, s32[512,1]{1,0:T(8,128)S(1)} %copy-done.73, s32[1,1024]{1,0:T(1,128)S(1)} %and_select_fusion.col_ref), custom_call_target="tpu_custom_call" | custom-call | flops 1073741824 | bytes 3145728 | tf_op jit(solution)/shard_map/pallas_call | solution.py:89
  125.1 30.2 %shard_map.299 = (f32[128,2048]{1,0:T(8,128)S(1)}, bf16[512,2048]{1,0:T(8,128)(2,1)S(1)}, bf16[256,1024]{1,0:T(8,128)(2,1)S(1)}, bf16[256,1024]{1,0:T(8,128)(2,1)S(1)}) custom-call(bf16[512,2048]{1,0:T(8,128)(2,1)S(1)} %convolution_convert_fusion.4.partial, f32[128,2048]{1,0:T(8,128)S(1)} %get-tuple-element.93.rows.kept, ...), custom_call_target="tpu_custom_call" | custom-call | flops 2621440 | bytes 62914560 | tf_op jit(solution)/shard_map/pallas_call | solution.py:640
  163.2 6.6 multiply_convert_fusion
  169.8 4.2 fusion.17
  175.1 5.5 add_convert_fusion.1.rest_0_.partial
  182.8 23.3 %collective-permute-done.8.far_ref = bf16[512,1280]{1,0:T(8,128)(2,1)} collective-permute-done((bf16[512,1280]{1,0:T(8,128)(2,1)}, bf16[512,1280]{1,0:T(8,128)(2,1)}, u32[]{:S(2)}, u32[]{:S(2)}) %collective-permute-start.8) | collective-permute-done | bytes 1310752 | tf_op jit(solution)/shard_map/ppermute | solution.py:680
  211.3 6.6 shard_map.301
  224.7 29.1 %shard_map.302 = (f32[128,2048]{1,0:T(8,128)S(1)}, bf16[512,2048]{1,0:T(8,128)(2,1)S(1)}, f32[1,2048]{1,0:T(1,128)S(1)}) custom-call(bf16[512,2048]{1,0:T(8,128)(2,1)S(1)} %copy-done.30, bf16[128,2048]{1,0:T(8,128)(2,1)} %bitcast.8.refs_0_.rows, f32[128,2048]{1,0:T(8,128)S(1)} %copy-done.23, f32[1,2048]{1,0:T(1,128)S(1)} %get-tuple-element.221.gain), custom_call_target="tpu_custom_call" | custom-call | flops 2621440 | bytes 62914560 | tf_op jit(solution)/shard_map/pallas_call | solution.py:640
  253.9 7.2 %shard_map.303 = (bf16[1,256,1280]{2,1,0:T(8,128)(2,1)S(1)}, bf16[3,256,1280]{2,1,0:T(8,128)(2,1)}) custom-call(s32[4]{0:T(128)S(1)} %broadcast_add_fusion.at_ref, bf16[512,2048]{1,0:T(8,128)(2,1)S(1)} %copy-done.32, bf16[256,1024]{1,0:T(8,128)(2,1)S(1)} %copy-done.76, bf16[256,1024]{1,0:T(8,128)(2,1)S(1)} %collective-permute-done.9.hi_ref, ...), custom_call_target="tpu_custom_call" | custom-call | flops 2684354560 | bytes 7340032 | tf_op jit(solution)/shard_map/pallas_call | solution.py:234
  264.9 9.8 %shard_map.304 = (bf16[512,512]{1,0:T(8,128)(2,1)S(1)}, bf16[1024,512]{1,0:T(8,128)(2,1)S(1)}, bf16[1024,512]{1,0:T(8,128)(2,1)S(1)}) custom-call(bf16[512,512]{1,0:T(8,128)(2,1)S(1)} %copy-done.89, bf16[1024,512]{1,0:T(8,128)(2,1)S(1)} %copy-done.87, bf16[1024,512]{1,0:T(8,128)(2,1)S(1)} %copy-done.85, s32[512,1]{1,0:T(8,128)S(1)} %copy-done.74, ...), custom_call_target="tpu_custom_call" | custom-call | flops 2684354560 | bytes 6291456 | tf_op jit(solution)/shard_map/pallas_call | solution.py:139
  278.2 7.2 %shard_map.305 = (bf16[1,256,1280]{2,1,0:T(8,128)(2,1)S(1)}, bf16[3,256,1280]{2,1,0:T(8,128)(2,1)}) custom-call(s32[4]{0:T(128)S(1)} %broadcast_add_fusion.at_ref, bf16[512,2048]{1,0:T(8,128)(2,1)S(1)} %copy-done.32, bf16[256,1024]{1,0:T(8,128)(2,1)S(1)} %copy-done.77, bf16[256,1024]{1,0:T(8,128)(2,1)S(1)} %copy-done.83, ...), custom_call_target="tpu_custom_call" | custom-call | flops 2684354560 | bytes 7340032 | tf_op jit(solution)/shard_map/pallas_call | solution.py:234
  289.7 28.2 %shard_map.307 = (f32[128,2048]{1,0:T(8,128)S(1)}, bf16[512,2048]{1,0:T(8,128)(2,1)S(1)}, f32[1,2048]{1,0:T(1,128)S(1)}) custom-call(bf16[512,2048]{1,0:T(8,128)(2,1)S(1)} %convolution_convert_fusion.3.rest_0_.partial, f32[128,2048]{1,0:T(8,128)S(1)} %get-tuple-element.113.rows, f32[128,2048]{1,0:T(8,128)S(1)} %copy-done.25, ...), custom_call_target="tpu_custom_call" | custom-call | flops 2621440 | bytes 62914560 | tf_op jit(solution)/shard_map/pallas_call | solution.py:640
  322.0 7.5 %shard_map.308 = (bf16[512,512]{1,0:T(8,128)(2,1)S(1)}, bf16[512,512]{1,0:T(8,128)(2,1)S(1)}, bf16[512,512]{1,0:T(8,128)(2,1)S(1)}) custom-call(bf16[512,512]{1,0:T(8,128)(2,1)S(1)} %copy-done.61, bf16[512,512]{1,0:T(8,128)(2,1)S(1)} %copy-done.59, bf16[512,512]{1,0:T(8,128)(2,1)S(1)} %copy-done.57, s32[512,2]{1,0:T(8,128)S(1)} %copy-done.42, ...), custom_call_target="tpu_custom_call" | custom-call | flops 1342177280 | bytes 4194304 | tf_op jit(solution)/shard_map/pallas_call | solution.py:139
  346.2 4.3 shard_map.309
  365.8 39.6 %shard_map.314 = (f32[128,2048]{1,0:T(8,128)S(1)}, f32[1,2048]{1,0:T(1,128)S(1)}, bf16[256,1024]{1,0:T(8,128)(2,1)S(1)}, bf16[256,1024]{1,0:T(8,128)(2,1)S(1)}, ...) custom-call(bf16[512,2048]{1,0:T(8,128)(2,1)S(1)} %add_convert_fusion.rest_0_.partial, ...), custom_call_target="tpu_custom_call" | custom-call | flops 2621440 | bytes 62914560 | tf_op jit(solution)/shard_map/pallas_call | solution.py:640
  409.6 5.5 shard_map.319
  419.1 4.5 shard_map.320
  429.7 4.5 convolution_convert_fusion.2.partial
  437.8 24.0 %shard_map.315 = (f32[128,2048]{1,0:T(8,128)S(1)}, f32[8,2048]{1,0:T(8,128)S(1)}, bf16[256,1664]{1,0:T(8,128)(2,1)S(1)}) custom-call(bf16[512,2048]{1,0:T(8,128)(2,1)S(1)} %convolution_convert_fusion.2.partial, f32[128,2048]{1,0:T(8,128)S(1)} %copy-done.23, f32[8,2048]{1,0:T(8,128)S(1)} %select_maximum_fusion.kept, f32[1,2048]{1,0:T(1,128)S(1)} %get-tuple-element.222.gain, ...), custom_call_target="tpu_custom_call" | custom-call | flops 2621440 | bytes 62914560 | tf_op jit(solution)/shard_map/pallas_call | solution.py:640
  465.8 177.8 %shard_map.322 = (f32[256,1280]{1,0:T(8,128)}, f32[256,1280]{1,0:T(8,128)}, f32[256,1280]{1,0:T(8,128)}, f32[256,512]{1,0:T(8,128)}, f32[256,512]{1,0:T(8,128)},...) custom-call(bf16[2,256,1280]{2,1,0:T(8,128)(2,1)} %copy-done.16, ...), custom_call_target="tpu_custom_call" | custom-call | flops 8568832 | bytes 85688320 | tf_op jit(solution)/shard_map/pallas_call | solution.py:458
  (411 shorter events, 157.7 us)
Async XLA Ops:
  21.3 32.1 %collective-permute-start = (bf16[128,2048]{1,0:T(8,128)(2,1)}, bf16[128,2048]{1,0:T(8,128)(2,1)}, u32[]{:S(2)}, u32[]{:S(2)}) collective-permute-start(bf16[128,2048]{1,0:T(8,128)(2,1)} %bitcast.8.refs_0_.rows), channel_id=1, source_target_pairs={{0,2},{1,3},{2,0},{3,1},{4,6},{5,7},{6,4},{7,5},{8,10},{9,11},{10,... | collective-permute-start | bytes 1572872 | tf_op jit(solution)/shard_map/ppermute | solution.py:680
  22.3 40.2 %collective-permute-start.1 = (bf16[128,2048]{1,0:T(8,128)(2,1)}, bf16[128,2048]{1,0:T(8,128)(2,1)}, u32[]{:S(2)}, u32[]{:S(2)}) collective-permute-start(bf16[128,2048]{1,0:T(8,128)(2,1)} %bitcast.8.refs_0_.rows), channel_id=1, source_target_pairs={{0,1},{1,0},{2,3},{3,2},{4,5},{5,4},{6,7},{7,6},{8,9},{9,8},{10,11... | collective-permute-start | bytes 1572872 | tf_op jit(solution)/shard_map/ppermute | solution.py:680
  26.2 27.2 %collective-permute-start.3 = (bf16[256,1024]{1,0:T(8,128)(2,1)}, bf16[256,1024]{1,0:T(8,128)(2,1)}, u32[]{:S(2)}, u32[]{:S(2)}) collective-permute-start(bf16[256,1024]{1,0:T(8,128)(2,1)} %shard_map.292), channel_id=1, source_target_pairs={{0,4},{4,0},{8,12},{12,8},{16,20},{20,16},{24,28},{28,24},{1,5},{5... | collective-permute-start | bytes 1572872 | tf_op jit(solution)/shard_map/ppermute | solution.py:680
  41.5 68.9 %collective-permute-start.5 = (bf16[512,512]{1,0:T(8,128)(2,1)}, bf16[512,512]{1,0:T(8,128)(2,1)}, u32[]{:S(2)}, u32[]{:S(2)}) collective-permute-start(bf16[512,512]{1,0:T(8,128)(2,1)} %shard_map.290.g_ref), channel_id=1, source_target_pairs={{0,4},{4,0},{8,12},{12,8},{16,20},{20,16},{24,28},{28,24},{1,5},{5... | collective-permute-start | bytes 1572872 | tf_op jit(solution)/shard_map/ppermute | solution.py:680
  53.4 12.7 %collective-permute-start.4 = (bf16[256,1024]{1,0:T(8,128)(2,1)}, bf16[256,1024]{1,0:T(8,128)(2,1)}, u32[]{:S(2)}, u32[]{:S(2)}) collective-permute-start(bf16[256,1024]{1,0:T(8,128)(2,1)} %collective-permute-done.3.refs_22_), channel_id=1, source_target_pairs={{0,1},{1,0},{2,3},{3,2},{4,5},{5,4},{6,7},{7,6},{8,9},{9,8},{10,11... | collective-permute-start | bytes 1572872 | tf_op jit(solution)/shard_map/ppermute | solution.py:680
  53.4 9.1 %collective-permute-start.2 = (bf16[128,2048]{1,0:T(8,128)(2,1)}, bf16[128,2048]{1,0:T(8,128)(2,1)}, u32[]{:S(2)}, u32[]{:S(2)}) collective-permute-start(bf16[128,2048]{1,0:T(8,128)(2,1)} %collective-permute-done.refs_1_), channel_id=1, source_target_pairs={{0,1},{1,0},{2,3},{3,2},{4,5},{5,4},{6,7},{7,6},{8,9},{9,8},{10,11... | collective-permute-start | bytes 1572872 | tf_op jit(solution)/shard_map/ppermute | solution.py:680
  65.1 91.1 %copy-start.13 = (bf16[512,2048]{1,0:T(8,128)(2,1)}, bf16[512,2048]{1,0:T(8,128)(2,1)S(1)}, u32[]{:S(2)}) copy-start(bf16[512,2048]{1,0:T(8,128)(2,1)S(1)} %shard_map.291.in_ref.a_ref) | copy-start | bytes 6291460
  122.6 37.6 %collective-permute-start.6 = (bf16[512,512]{1,0:T(8,128)(2,1)S(1)}, bf16[512,512]{1,0:T(8,128)(2,1)S(1)}, u32[]{:S(2)}, u32[]{:S(2)}) collective-permute-start(bf16[512,512]{1,0:T(8,128)(2,1)S(1)} %shard_map.297.g_ref), channel_id=1, source_target_pairs={{0,4},{4,0},{8,12},{12,8},{16,20},{20,16},{24,28},{28,24},{1,5},{5... | collective-permute-start | bytes 1572872 | tf_op jit(solution)/shard_map/ppermute | solution.py:680
  159.2 14.8 %collective-permute-start.7 = (bf16[256,1024]{1,0:T(8,128)(2,1)S(1)}, bf16[256,1024]{1,0:T(8,128)(2,1)S(1)}, u32[]{:S(2)}, u32[]{:S(2)}) collective-permute-start(bf16[256,1024]{1,0:T(8,128)(2,1)S(1)} %shard_map.300), channel_id=1, source_target_pairs={{0,4},{4,0},{8,12},{12,8},{16,20},{20,16},{24,28},{28,24},{1,5},{5... | collective-permute-start | bytes 1572872 | tf_op jit(solution)/shard_map/ppermute | solution.py:680
  174.0 32.1 %collective-permute-start.8 = (bf16[512,1280]{1,0:T(8,128)(2,1)}, bf16[512,1280]{1,0:T(8,128)(2,1)}, u32[]{:S(2)}, u32[]{:S(2)}) collective-permute-start(bf16[512,1280]{1,0:T(8,128)(2,1)} %get-tuple-element.129.g_ref), channel_id=1, source_target_pairs={{0,4},{4,0},{8,12},{12,8},{16,20},{20,16},{24,28},{28,24},{1,5},{5... | collective-permute-start | bytes 3932168 | tf_op jit(solution)/shard_map/ppermute | solution.py:680
  180.6 73.2 %collective-permute-start.10 = (bf16[512,1280]{1,0:T(8,128)(2,1)}, bf16[512,1280]{1,0:T(8,128)(2,1)}, u32[]{:S(2)}, u32[]{:S(2)}) collective-permute-start(bf16[512,1280]{1,0:T(8,128)(2,1)} %get-tuple-element.104.g_ref), channel_id=1, source_target_pairs={{0,4},{4,0},{8,12},{12,8},{16,20},{20,16},{24,28},{28,24},{1,5},{5... | collective-permute-start | bytes 3932168 | tf_op jit(solution)/shard_map/ppermute | solution.py:680
  182.7 71.1 %collective-permute-start.9 = (bf16[256,1024]{1,0:T(8,128)(2,1)}, bf16[256,1024]{1,0:T(8,128)(2,1)S(1)}, u32[]{:S(2)}, u32[]{:S(2)}) collective-permute-start(bf16[256,1024]{1,0:T(8,128)(2,1)} %copy-done.75), channel_id=1, source_target_pairs={{0,1},{1,0},{2,3},{3,2},{4,5},{5,4},{6,7},{7,6},{8,9},{9,8},{10,11... | collective-permute-start | bytes 1572872 | tf_op jit(solution)/shard_map/ppermute | solution.py:680
  218.0 69.0 %collective-permute-start.12 = (bf16[3,256,1280]{2,1,0:T(8,128)(2,1)S(1)}, bf16[3,256,1280]{2,1,0:T(8,128)(2,1)}, u32[]{:S(2)}, u32[]{:S(2)}) collective-permute-start(bf16[3,256,1280]{2,1,0:T(8,128)(2,1)S(1)} %get-tuple-element.100.left_ref), channel_id=1, source_target_pairs={{0,8},{4,12},{8,0},{12,4},{16,24},{20,28},{24,16},{28,20},{1,9},{5... | collective-permute-start | bytes 5898248 | tf_op jit(solution)/shard_map/ppermute | solution.py:680
  221.7 56.4 %collective-permute-start.11 = (bf16[512,1280]{1,0:T(8,128)(2,1)}, bf16[512,1280]{1,0:T(8,128)(2,1)}, u32[]{:S(2)}, u32[]{:S(2)}) collective-permute-start(bf16[512,1280]{1,0:T(8,128)(2,1)} %get-tuple-element.109.g_ref), channel_id=1, source_target_pairs={{0,4},{4,0},{8,12},{12,8},{16,20},{20,16},{24,28},{28,24},{1,5},{5... | collective-permute-start | bytes 3932168 | tf_op jit(solution)/shard_map/ppermute | solution.py:680
  261.1 78.2 %collective-permute-start.16 = (bf16[3,256,1280]{2,1,0:T(8,128)(2,1)}, bf16[3,256,1280]{2,1,0:T(8,128)(2,1)}, u32[]{:S(2)}, u32[]{:S(2)}) collective-permute-start(bf16[3,256,1280]{2,1,0:T(8,128)(2,1)} %get-tuple-element.106.left_ref), channel_id=1, source_target_pairs={{0,8},{4,12},{8,0},{12,4},{16,24},{20,28},{24,16},{28,20},{1,9},{5... | collective-permute-start | bytes 5898248 | tf_op jit(solution)/shard_map/ppermute | solution.py:680
  274.7 71.2 %collective-permute-start.13 = (bf16[1024,512]{1,0:T(8,128)(2,1)S(1)}, bf16[1024,512]{1,0:T(8,128)(2,1)S(1)}, u32[]{:S(2)}, u32[]{:S(2)}) collective-permute-start(bf16[1024,512]{1,0:T(8,128)(2,1)S(1)} %get-tuple-element.124.g_ref), channel_id=1, source_target_pairs={{0,4},{4,0},{8,12},{12,8},{16,20},{20,16},{24,28},{28,24},{1,5},{5... | collective-permute-start | bytes 3145736 | tf_op jit(solution)/shard_map/ppermute | solution.py:680
  275.9 75.5 %collective-permute-start.20 = (bf16[512,512]{1,0:T(8,128)(2,1)S(1)}, bf16[512,512]{1,0:T(8,128)(2,1)}, u32[]{:S(2)}, u32[]{:S(2)}) collective-permute-start(bf16[512,512]{1,0:T(8,128)(2,1)S(1)} %get-tuple-element.108.g_ref), channel_id=1, source_target_pairs={{0,4},{4,0},{8,12},{12,8},{16,20},{20,16},{24,28},{28,24},{1,5},{5... | collective-permute-start | bytes 1572872 | tf_op jit(solution)/shard_map/ppermute | solution.py:680
  285.4 120.9 %collective-permute-start.22 = (bf16[3,256,1280]{2,1,0:T(8,128)(2,1)}, bf16[3,256,1280]{2,1,0:T(8,128)(2,1)}, u32[]{:S(2)}, u32[]{:S(2)}) collective-permute-start(bf16[3,256,1280]{2,1,0:T(8,128)(2,1)} %get-tuple-element.111.left_ref), channel_id=1, source_target_pairs={{0,8},{4,12},{8,0},{12,4},{16,24},{20,28},{24,16},{28,20},{1,9},{5... | collective-permute-start | bytes 5898248 | tf_op jit(solution)/shard_map/ppermute | solution.py:680
  332.7 22.9 %collective-permute-start.14 = (bf16[1024,512]{1,0:T(8,128)(2,1)}, bf16[1024,512]{1,0:T(8,128)(2,1)S(1)}, u32[]{:S(2)}, u32[]{:S(2)}) collective-permute-start(bf16[1024,512]{1,0:T(8,128)(2,1)} %add_convert_fusion.7), channel_id=1, source_target_pairs={{0,1},{1,0},{2,3},{3,2},{4,5},{5,4},{6,7},{7,6},{8,9},{9,8},{10,11... | collective-permute-start | bytes 3145736 | tf_op jit(solution)/shard_map/ppermute | solution.py:680
  339.3 19.8 %collective-permute-start.15 = (bf16[1024,512]{1,0:T(8,128)(2,1)S(1)}, bf16[1024,512]{1,0:T(8,128)(2,1)S(1)}, u32[]{:S(2)}, u32[]{:S(2)}) collective-permute-start(bf16[1024,512]{1,0:T(8,128)(2,1)S(1)} %add_convert_fusion.4), channel_id=1, source_target_pairs={{0,1},{1,0},{2,3},{3,2},{4,5},{5,4},{6,7},{7,6},{8,9},{9,8},{10,11... | collective-permute-start | bytes 3145736 | tf_op jit(solution)/shard_map/ppermute | solution.py:680
  345.9 16.1 %collective-permute-start.17 = (bf16[2,256,1280]{2,1,0:T(8,128)(2,1)S(1)}, bf16[2,256,1280]{2,1,0:T(8,128)(2,1)S(1)}, u32[]{:S(2)}, u32[]{:S(2)}) collective-permute-start(bf16[2,256,1280]{2,1,0:T(8,128)(2,1)S(1)} %slice.44), channel_id=1, source_target_pairs={{0,1},{1,0},{2,3},{3,2},{4,5},{5,4},{6,7},{7,6},{8,16},{9,17},{10,... | collective-permute-start | bytes 3932168 | tf_op jit(solution)/shard_map/ppermute | solution.py:720
  351.4 64.8 %collective-permute-start.19 = (bf16[2,256,1280]{2,1,0:T(8,128)(2,1)}, bf16[2,256,1280]{2,1,0:T(8,128)(2,1)}, u32[]{:S(2)}, u32[]{:S(2)}) collective-permute-start(bf16[2,256,1280]{2,1,0:T(8,128)(2,1)} %slice.45), channel_id=1, source_target_pairs={{0,1},{1,0},{2,3},{3,2},{4,5},{5,4},{6,7},{7,6},{8,16},{9,17},{10,... | collective-permute-start | bytes 3932168 | tf_op jit(solution)/shard_map/ppermute | solution.py:720
  355.6 54.0 %collective-permute-start.21 = (bf16[1024,512]{1,0:T(8,128)(2,1)S(1)}, bf16[1024,512]{1,0:T(8,128)(2,1)}, u32[]{:S(2)}, u32[]{:S(2)}) collective-permute-start(bf16[1024,512]{1,0:T(8,128)(2,1)S(1)} %get-tuple-element.125.g_ref), channel_id=1, source_target_pairs={{0,4},{4,0},{8,12},{12,8},{16,20},{20,16},{24,28},{28,24},{1,5},{5... | collective-permute-start | bytes 3145736 | tf_op jit(solution)/shard_map/ppermute | solution.py:680
  359.1 75.2 %collective-permute-start.18 = (bf16[1024,512]{1,0:T(8,128)(2,1)}, bf16[1024,512]{1,0:T(8,128)(2,1)}, u32[]{:S(2)}, u32[]{:S(2)}) collective-permute-start(bf16[1024,512]{1,0:T(8,128)(2,1)} %add_convert_fusion.6), channel_id=1, source_target_pairs={{0,2},{1,3},{2,0},{3,1},{4,6},{5,7},{6,4},{7,5},{8,10},{9,11},{10,... | collective-permute-start | bytes 3145736 | tf_op jit(solution)/shard_map/ppermute | solution.py:680
  (133 other events, 699.1 us)

commit v5 on v4

--- a/solution.py
+++ b/solution.py
@@ -121,10 +121,10 @@
     )
 
 
-def cross_back_kernel(q_ref, k_ref, v_ref, row_ref, col_ref, do_ref, *outs):
+def cross_back_kernel(q_ref, k_ref, v_ref, row_ref, col_ref, do_ref, dq_ref, out_ref):
     attend_back_kernel(
         False, q_ref, k_ref, v_ref, row_ref, col_ref, do_ref,
-        *outs,
+        dq_ref, out_ref.at[0], out_ref.at[1],
     )
 
 
@@ -133,9 +133,12 @@
     spots = keys.shape[0]
     head = lambda size: pl.BlockSpec((size, HEAD_DIM), lambda h: (0, h))
     whole = lambda arr: pl.BlockSpec(arr.shape, lambda h: (0, 0))
-    sizes = (length, spots, spots)
-    out_specs = tuple(head(size) for size in sizes)
-    out_shape = tuple(jax.ShapeDtypeStruct((size, width), BF16) for size in sizes)
+    shape = lambda *dims: jax.ShapeDtypeStruct(dims, BF16)
+    if causal:
+        out_specs, out_shape = (head(length),) * 3, (shape(length, width),) * 3
+    else:
+        out_specs = (head(length), pl.BlockSpec((2, spots, HEAD_DIM), lambda h: (0, 0, h)))
+        out_shape = (shape(length, width), shape(2, spots, width))
     return pl.pallas_call(
         self_back_kernel if causal else cross_back_kernel,
         grid=(width // HEAD_DIM,),
@@ -212,6 +215,8 @@
 
 def pair_kernel(at_ref, a_ref, lo_ref, hi_ref, g_ref, far_ref, *rest):
     half = lo_ref.shape[0]
+    if len(g_ref.shape) == 3:
+        g_ref, far_ref = g_ref.at[0], far_ref.at[0]
     total = rows_dot(a_ref[...], g_ref[...])
     total += rows_dot(lo_ref[...], far_ref[:half])
     total += rows_dot(hi_ref[...], far_ref[half:])
@@ -226,10 +231,12 @@
         rest_ref[0] = total.astype(BF16)
 
 
-def pair_grad(at, own, low, high, grad, grad_far, after):
-    length, units = grad.shape
+def pair_grad(at, own, low, high, grad, grad_far, after, pick=None):
+    length, units = grad.shape[-2:]
     width = own.shape[1] // 8
     whole = pl.BlockSpec((length, units), lambda k, at: (0, 0))
+    if pick is not None:
+        whole = pl.BlockSpec((1, length, units), lambda k, at: (pick, 0, 0))
     side = pl.BlockSpec((length // 2, width), lambda k, at: (0, k))
     return pl.pallas_call(
         pair_kernel,
@@ -309,16 +316,17 @@
 def line_kernel(ready, merged, count, pairs, *refs):
     refs = list(refs)
     take = lambda size: [refs.pop(0) for unused in range(size)]
-    total = count + pairs
+    total = count + pairs + 1
     first = take(count)
     rest = dict(zip(range(ready, count), take(count - ready)))
-    grads, [own, low, high] = take(pairs), take(3)
+    grads, [own, low, high, kept, sent] = take(pairs), take(5)
     outs = take(total)
     late = range(ready + merged, total)
     open_ends = range(ready, total)
-    first += take(pairs)
-    rest.update(zip(range(count, total), take(pairs)))
+    first += take(pairs + 1)
+    rest.update(zip(range(count, total), take(pairs + 1)))
     far = take(pairs)
+    [got] = take(1)
     from_outer = dict(zip(late, take(len(late))))
     from_inner = dict(zip(open_ends, take(len(open_ends))))
     last = take(total)
@@ -354,10 +362,16 @@
         return copy(source, last[g], send_last.at[g], got_last.at[g], beside)
 
     def copy_grad(p):
-        return copy(grads[p], far[p], send_x.at[p], got_x.at[p], partner)
+        source, target = (grads[p], far[p]) if p < pairs else (sent, got)
+        return copy(source, target, send_x.at[p], got_x.at[p], partner)
 
     def multiply(p):
         copy_grad(p).wait_recv()
+        if p == pairs:
+            add_rows(first[total - 1].at[0], kept.at[0], got.at[0])
+            for k in range(3):
+                add_rows(rest[total - 1].at[k], kept.at[k + 1], got.at[k + 1])
+            return
         half, width = low.shape[0], first[count + p].shape[1]
 
         def body(k, carry):
@@ -387,7 +401,7 @@
     @pl.when(outer)
     def _():
         pl.semaphore_wait(barrier, 2)
-        for p in range(pairs):
+        for p in range(pairs + 1):
             copy_grad(p).start()
         for g in sequence:
             if g >= count:
@@ -403,7 +417,7 @@
     def _():
         pl.semaphore_signal(barrier, inc=1, device_id=across, device_id_type=mesh_id)
         pl.semaphore_wait(barrier, 3)
-        for p in range(pairs):
+        for p in range(pairs + 1):
             copy_grad(p).start()
         for g in range(ready):
             copy_last(g).start()
@@ -431,7 +445,7 @@
                 multiply(g - count)
             begin(g)
             waiting.append(g)
-            if len(waiting) > 1:
+            if len(waiting) > 2:
                 finish(waiting.pop(0))
         for g in waiting:
             finish(g)
@@ -440,59 +454,60 @@
         for g in range(total):
             copy_last(g).wait_send()
 
-    for p in range(pairs):
+    for p in range(pairs + 1):
         copy_grad(p).wait_send()
 
 
-def line_sums(ready_parts, merged_parts, late_parts, grads, own, low, high):
+def line_sums(ready_parts, merged_parts, late_parts, grads, own, low, high, kept, sent):
     open_parts = list(merged_parts) + list(late_parts)
     parts = list(ready_parts) + [first for first, unused in open_parts]
     rests = [rest for unused, rest in open_parts]
     ready, merged, count, pairs = len(ready_parts), len(merged_parts), len(parts), len(grads)
     width = own.shape[1] // 8
-    shapes = [p.shape[1:] for p in parts] + [(width, g.shape[1]) for g in grads]
-    total, late = count + pairs, shapes[ready + merged :]
-    assert ready + merged <= count and merged <= 1
+    shapes = [p.shape[1:] for p in parts] + [(width, g.shape[1]) for g in grads] + [kept.shape[1:]]
+    total, late = count + pairs + 1, shapes[ready + merged :]
     vmem = pl.BlockSpec(memory_space=pltpu.VMEM)
     sizes = [r * k for r, k in shapes]
     return pl.pallas_call(
         functools.partial(line_kernel, ready, merged, count, pairs),
-        in_specs=[vmem] * (count + len(rests) + pairs + 3),
+        in_specs=[vmem] * (count + len(rests) + pairs + 5),
         out_specs=[vmem] * total,
         out_shape=[jax.ShapeDtypeStruct(shape, F32) for shape in shapes],
         scratch_shapes=[pltpu.VMEM((n,) + shape, BF16) for n in (1, 3) for shape in shapes[count:]]
-        + [pltpu.VMEM(g.shape, BF16) for g in grads]
+        + [pltpu.VMEM(g.shape, BF16) for g in grads + [kept]]
         + [pltpu.VMEM((3,) + shape, BF16) for shape in late]
         + [pltpu.VMEM((2,) + shape, BF16) for shape in shapes[ready:]]
         + [pltpu.VMEM(shape, BF16) for shape in shapes]
         + [pltpu.SemaphoreType.DMA((total,))] * 6
-        + [pltpu.SemaphoreType.DMA((pairs,))] * 2,
+        + [pltpu.SemaphoreType.DMA((pairs + 1,))] * 2,
         compiler_params=pltpu.CompilerParams(
             collective_id=0, has_side_effects=True, vmem_limit_bytes=56 * 2**20
         ),
         cost_estimate=cost(4 * sum(sizes), 40 * sum(sizes)),
-    )(*parts, *rests, *grads, own, low, high)
+    )(*parts, *rests, *grads, own, low, high, kept, sent)
 
 
 CHUNKS = 4
 
 
-def boundary_kernel(mode, jobs, plain, partial, rows, kept, gain, *refs):
+def boundary_kernel(mode, jobs, early, partial, rows, kept, gain, *refs):
     refs = list(refs)
     take = lambda size: [refs.pop(0) for unused in range(size)]
-    wanted = take(jobs)
+    [gains] = take(1) if mode == "last" else [None]
+    wanted, along = take(jobs), take(early)
     [sums] = take(1) if mode != "first" else [None]
     [gathered] = take(1) if mode not in ("last", "sum") else [None]
     [gain_out] = take(1) if mode in ("backward", "last") else [None]
-    [kept_out] = take(1) if mode == "sum" else [None]
-    low_out, high_out = take(jobs), take(0 if plain else jobs)
+    low_out, high_out, along_out = take(jobs), take(jobs), take(early)
     from_core, far_sum, from_chip, whole = take(4)
-    low, high = take(jobs), take(0 if plain else jobs)
+    low, high, from_lane = take(jobs), take(jobs), take(early)
     sends, gots = take(2)
     if jobs:
         send_jobs, got_jobs = take(2)
-    if mode == "sum":
-        running, others, send_kept, got_kept = take(4)
+    if early:
+        send_along, got_along = take(2)
+    if mode == "last":
+        others, send_gains, got_gains = take(3)
     dp, mp = lax.axis_index("dp"), lax.axis_index("mp")
     core = (dp, mp + 1 - 2 * (mp % 2))
     chip = (dp, (mp + 2) % 4)
@@ -501,10 +516,22 @@
     size = step // CHUNKS
     barrier = pltpu.get_barrier_semaphore()
     beside = (dp + 1 - 2 * (dp % 2), mp)
-    near = (core, chip, beside) if jobs or mode == "sum" else (core, chip)
-    for device in near:
+    lane = dp // 2
+    next_lane = ((lane + 1 - 2 * (lane % 2)) * 2 + dp % 2, mp)
+    near = (core, chip, beside) if jobs else (core, chip)
+    greeted = near + ((next_lane,) if early else ())
+    for device in greeted:
         pl.semaphore_signal(barrier, inc=1, device_id=device, device_id_type=mesh_id)
-    pl.semaphore_wait(barrier, len(near))
+    pl.semaphore_wait(barrier, len(greeted))
+
+    def along_copy(k):
+        return pltpu.make_async_remote_copy(
+            src_ref=along[k], dst_ref=from_lane[k], send_sem=send_along.at[k],
+            recv_sem=got_along.at[k], device_id=next_lane, device_id_type=mesh_id,
+        )
+
+    for k in range(early):
+        along_copy(k).start()
 
     def job(hop, k):
         source, target = ((wanted, low), (low, high))[hop]
@@ -553,7 +580,7 @@
             far_sum[part(0, c)] = total.astype(BF16)
             chip_sum(c).start()
     if gain_out is not None:
-        gain_out[...] = jnp.zeros_like(gain_out)
+        gain_out[...] = jnp.zeros_like(gain_out) if mode != "last" else gains[...]
     for c in every:
         here = part(0, c)
         if mode == "first":
@@ -571,7 +598,7 @@
                 weighted = gain[...] * total
                 inner = jnp.mean(old * weighted, axis=-1, keepdims=True)
                 value = wide(rows[here]) + inv * weighted - old * (inv * inv * inv) * inner
-                gain_out[...] += jnp.sum(total * old * inv, axis=0, keepdims=True)
+                gain_out[0:1] += jnp.sum(total * old * inv, axis=0, keepdims=True)
                 sums[here] = value
         if gathered is not None:
             if mode != "backward":
@@ -587,29 +614,28 @@
             for block in range(2):
                 core_row(block, c).wait_recv()
         gathered[...] = whole[...]
-    if mode == "sum":
-        running[...] = kept[...]
-        hops = []
-        for k, device in enumerate((core, chip, beside)):
+    if mode == "last":
+        for k, device in enumerate(near):
+            others[0] = gain_out[...]
             hop = pltpu.make_async_remote_copy(
-                src_ref=running, dst_ref=others.at[k], send_sem=send_kept.at[k],
-                recv_sem=got_kept.at[k], device_id=device, device_id_type=mesh_id,
+                src_ref=others.at[0], dst_ref=others.at[k + 1], send_sem=send_gains.at[k],
+                recv_sem=got_gains.at[k], device_id=device, device_id_type=mesh_id,
             )
             hop.start()
             hop.wait()
-            running[...] = running[...] + others[k]
-        kept_out[...] = running[...]
+            gain_out[...] += others[k + 1]
     for k in range(jobs):
         job(0, k).wait_recv()
-        if not plain:
-            job(1, k).start()
+        job(1, k).start()
         low_out[k][...] = low[k][...]
     for k in range(jobs):
         job(0, k).wait_send()
-        if not plain:
-            job(1, k).wait_recv()
-            high_out[k][...] = high[k][...]
-            job(1, k).wait_send()
+        job(1, k).wait_recv()
+        high_out[k][...] = high[k][...]
+        job(1, k).wait_send()
+    for k in range(early):
+        along_copy(k).wait()
+        along_out[k][...] = from_lane[k][...]
     for c in every:
         if mode != "first":
             core_sum(0, c).wait_send()
@@ -621,7 +647,7 @@
             core_row(1, c).wait_send()
 
 
-def boundary(mode, number, partial, rows, kept, gain, wanted=(), plain=False):
+def boundary(mode, number, partial, rows, kept, gain, wanted=(), gains=None, along=()):
     step, width = rows.shape
     vmem = pl.BlockSpec(memory_space=pltpu.VMEM)
     shapes = []
@@ -630,16 +656,15 @@
     if mode not in ("last", "sum"):
         shapes.append(jax.ShapeDtypeStruct((4 * step, width), BF16))
     if mode in ("backward", "last"):
-        shapes.append(jax.ShapeDtypeStruct((1, width), F32))
-    if mode == "sum":
-        shapes.append(jax.ShapeDtypeStruct(kept.shape, F32))
-    jobs = len(wanted)
-    hops = 1 if plain else 2
-    shapes += [jax.ShapeDtypeStruct(w.shape, BF16) for w in wanted] * hops
-    scratch = [pltpu.VMEM(w.shape, BF16) for w in wanted] * hops
+        shapes.append(jax.ShapeDtypeStruct((1 if mode == "backward" else 8, width), F32))
+    given = [gains] if mode == "last" else []
+    jobs, early = len(wanted), len(along)
+    moved = list(wanted) * 2 + list(along)
+    shapes += [jax.ShapeDtypeStruct(w.shape, BF16) for w in moved]
+    scratch = [pltpu.VMEM(w.shape, BF16) for w in moved]
     outs = pl.pallas_call(
-        functools.partial(boundary_kernel, mode, jobs, plain),
-        in_specs=[vmem] * (4 + jobs),
+        functools.partial(boundary_kernel, mode, jobs, early),
+        in_specs=[vmem] * (4 + len(given) + jobs + early),
         out_specs=[vmem] * len(shapes),
         out_shape=shapes,
         scratch_shapes=[
@@ -651,21 +676,23 @@
         + scratch
         + [pltpu.SemaphoreType.DMA((6, CHUNKS))] * 2
         + ([pltpu.SemaphoreType.DMA((2, jobs))] * 2 if jobs else [])
+        + ([pltpu.SemaphoreType.DMA((early,))] * 2 if early else [])
         + (
-            [pltpu.VMEM(kept.shape, F32), pltpu.VMEM((3,) + kept.shape, F32)]
-            + [pltpu.SemaphoreType.DMA((3,))] * 2
-            if mode == "sum"
+            [pltpu.VMEM((4, 8, width), F32)] + [pltpu.SemaphoreType.DMA((3,))] * 2
+            if mode == "last"
             else []
         ),
         compiler_params=pltpu.CompilerParams(
             collective_id=number, has_side_effects=True, vmem_limit_bytes=2 * VMEM_LIMIT
         ),
         cost_estimate=cost(10 * step * width, 60 * 2**20),
-    )(partial, rows, kept, gain, *wanted)
-    if not jobs or plain:
+    )(partial, rows, kept, gain, *given, *wanted, *along)
+    if not jobs:
         return outs
-    halves = list(zip(outs[-2 * jobs : -jobs], outs[-jobs:]))
-    return list(outs[: -2 * jobs]) + halves
+    outs = list(outs)
+    plain = len(outs) - 2 * jobs - early
+    halves = list(zip(outs[plain : plain + jobs], outs[plain + jobs :]))
+    return outs[:plain] + halves + outs[plain + 2 * jobs :]
 
 
 def gated_unit(gate_arg, up_arg):
@@ -791,10 +818,9 @@
         self_mixed = tie(self_mixed, (grad_three, split_one))
         partial = matmul(self_mixed, w_out).astype(BF16)
         after_self, normed_two, *halves = boundary(
-            "forward", 2, partial, tokens[0], nothing, gain_rows[1], exchange((projected, core_bit), (grad_three,))
+            "forward", 2, partial, tokens[0], nothing, gain_rows[1], exchange((projected, core_bit))
         )
         patch_low, patch_high = halves[0] if paired else (None, None)
-        [split_cotangent] = map(split, (grad_three,), halves[1:] or none)
         normed_two = tie(normed_two, self_far)
         cross_keys = matmul(projected, c_key).astype(BF16)
         cross_values = matmul(projected, c_value).astype(BF16)
@@ -802,19 +828,18 @@
         cross_mixed = attend(
             cross_queries, cross_keys, cross_values, cross_rows, cross_cols, False
         )
-        mixed_far = far_of(cross_mixed)
         partial = matmul(cross_mixed, c_out).astype(BF16)
         after_cross, normed_three, *halves = boundary(
             "forward", 3, partial, after_self, nothing, gain_rows[2],
-            exchange((normed_two,)),
-        )
-        [split_two] = map(split, (normed_two,), halves or none)
+            exchange((grad_three,), (normed_two,)),
+        )
+        split_cotangent, split_two = map(split, (grad_three, normed_two), halves or none)
         grad_hidden = tie(product("sd,fd->sf", grad_three, w_down), ())
         if paired:
             wanted = wanted_of(normed_three)
             low_three = beside(wanted)
             split_three = normed_three, low_three, core(low_three)
-            normed_three = tie(normed_three, (grad_hidden, mixed_far, wanted))
+            normed_three = tie(normed_three, (grad_hidden, wanted))
         else:
             split_three, low_three = (normed_three,), normed_three
         gate_pre, up_pre = matmul(normed_three, w_gate), matmul(normed_three, w_up)
@@ -824,15 +849,16 @@
 
         results, turned = {}, {}
 
-        def line(name, split, grad, grad_far, rows_first, after=()):
+        def line(name, split, grad, grad_far, rows_first, after=(), pick=None):
             turned[name] = not rows_first
             if not paired:
+                grad = grad if pick is None else grad[pick]
                 partial = product("td,te->de", split[0], grad).astype(BF16)
                 total = lax.psum_scatter(partial, "dp", scatter_dimension=0, tiled=True)
                 results[name] = total.astype(F32)
                 return ()
             results[name] = pair_grad(
-                lane_columns(line_place()[0]), *split, grad, grad_far, after
+                lane_columns(line_place()[0]), *split, grad, grad_far, after, pick
             )
             return results[name]
 
@@ -855,7 +881,9 @@
             product("sf,df->sd", grad_gate, w_gate) + product("sf,df->sd", grad_up, w_up)
         ).astype(BF16)
         gate_far, up_far = [far_of(v) for v in tie((grad_gate, grad_up), partial)]
-        sent = line("down", split_cotangent, hidden, hidden_far, False, (partial,))
+        partial_out = matmul(tie(hidden, partial), w_down).astype(BF16)
+        [output] = boundary("sum", 7, partial_out, after_cross, nothing, gain_rows[0])
+        sent = line("down", split_cotangent, hidden, hidden_far, False, (output,))
         incoming_down = line_out("down")
         grad_rows, grad_two, gain_three = boundary(
             "backward", 4, tie(partial, sent), cotangent[0], after_cross, gain_rows[2]
@@ -865,10 +893,10 @@
         grad_two = tie(grad_two, sent)
 
         grad_mixed = product("sd,ed->se", grad_two, c_out).astype(BF16)
-        grad_cq, grad_ck, grad_cv = attend_back(
+        grad_cq, grad_ckv = attend_back(
             cross_queries, cross_keys, cross_values, cross_rows, cross_cols, grad_mixed, False
         )
-        cq_far, ck_far, cv_far = far_of(grad_cq), far_of(grad_ck), far_of(grad_cv)
+        cq_far, ckv_far = far_of(grad_cq), far_of(grad_ckv)
         partial = product("se,de->sd", grad_cq, c_query).astype(BF16)
         sent = line("up", split_three, grad_up, up_far, True, (partial,))
         incoming_up = line_out("up")
@@ -878,15 +906,6 @@
         )
         line_across("down")
 
-        grad_mixed = product("sd,ed->se", grad_one, w_out).astype(BF16)
-        grad_sq, grad_sk, grad_sv = attend_back(
-            queries, key_rows, value_rows, self_rows, self_cols, grad_mixed, True
-        )
-        partial = (
-            product("se,de->sd", grad_sq, w_query)
-            + product("se,de->sd", grad_sk, w_key)
-            + product("se,de->sd", grad_sv, w_value)
-        ).astype(BF16)
         width = model // (n_dp * n_mp)
 
         def projected_block(k):
@@ -896,15 +915,32 @@
                     n_dp * width, weight.shape[1]
                 )
 
-            return (cols_dot(late_ck, rows_of(c_key)) + cols_dot(late_cv, rows_of(c_value))).astype(
+            return (
+                cols_dot(grad_ckv_late[0], rows_of(c_key))
+                + cols_dot(grad_ckv_late[1], rows_of(c_value))
+            ).astype(
                 BF16
             )
 
-        late_ck, late_cv = tie((grad_ck, grad_cv), grad_one)
+        grad_ckv_late = tie(grad_ckv, grad_one)
         block = [projected_block(k) for k in order]
-        far = (block[1].astype(F32) + core(block[3]).astype(F32)).astype(BF16)
+        far_core = core(block[3])
+
+        grad_mixed = product(
+            "sd,ed->se", tie(grad_one, (block[1], block[3])), w_out
+        ).astype(BF16)
+        grad_sq, grad_sk, grad_sv = attend_back(
+            queries, key_rows, value_rows, self_rows, self_cols, grad_mixed, True
+        )
+        far = (block[1].astype(F32) + far_core.astype(F32)).astype(BF16)
+        grad_sq, grad_sk, grad_sv = tie((grad_sq, grad_sk, grad_sv), far)
+        far_in = chip(far)
         near = (block[0].astype(F32) + core(block[2]).astype(F32)).astype(BF16)
-        far_in = chip(far)
+        partial = (
+            product("se,de->sd", grad_sq, w_query)
+            + product("se,de->sd", grad_sk, w_key)
+            + product("se,de->sd", grad_sv, w_value)
+        ).astype(BF16)
         line_merge("gate", incoming_gate, (partial,))
         line("c_query", split_two, grad_cq, cq_far, True, (partial,))
         split_patch = (projected,)
@@ -915,34 +951,34 @@
                 jnp.where(swapped, patch_high, patch_low),
                 jnp.where(swapped, patch_low, patch_high),
             )
-        sent = line("c_key", split_patch, grad_ck, ck_far, True, (partial,))
-        grad_rows, gain_one, *halves = boundary(
+        sent = line("c_key", split_patch, grad_ckv, ckv_far, True, (partial,), 0)
+        gains = jnp.pad(jnp.concatenate([gain_two, gain_three], axis=0), ((1, 5), (0, 0)))
+        along = [results["c_query"][1], results["c_key"][1]] if paired else []
+        grad_rows, gains_near, *halves = boundary(
             "last", 6, tie(partial, (sent, far, near, results["gate"], results["down"])), grad_rows,
-            residual, gain_rows[0], exchange((grad_two,), (grad_one,)),
-        )
+            residual, gain_rows[0], exchange((grad_two,), (grad_one,)), gains, along,
+        )
+        if paired:
+            line_merge("c_query", halves[2], ())
+            line_merge("c_key", halves[3], ())
+        mixed_far = far_of(tie(cross_mixed, grad_rows))
         line_across("gate")
-        split_grad_two, split_grad_one = map(split, (grad_two, grad_one), halves or none)
+        split_grad_two, split_grad_one = map(split, (grad_two, grad_one), halves[:2] or none)
         grad_projected = (near.astype(F32) + far_in.astype(F32)).astype(BF16)
         patch_partial = rows_dot(grad_projected, patch_own).astype(BF16)
         x, flip, unused = line_place()
         patch_parts = patch_partial.reshape(n_dp // 2, 2, width, patches.shape[2])
         patch_sent = lax.dynamic_index_in_dim(patch_parts, 1 - x, 1, keepdims=False)
-        partial = matmul(tie(hidden, grad_rows), w_down).astype(BF16)
-        gains = jnp.concatenate([gain_one, gain_two, gain_three], axis=0)
-        gains_wide = jnp.pad(gains, ((0, 5), (0, 0)))
-        output, gains_near, *patch_got = boundary(
-            "sum", 7, partial, after_cross, gains_wide, gain_rows[0],
-            [patch_sent.reshape(-1, patches.shape[2])] if paired else [], True,
-        )
-        line("c_value", split_patch, grad_cv, cv_far, True, (grad_rows,))
+        line("c_value", split_patch, grad_ckv, ckv_far, True, (grad_rows,), 1)
         line("c_out", split_grad_two, cross_mixed, mixed_far, False, (grad_rows,))
         line("w_out", split_grad_one, self_mixed, self_far, False, (grad_rows,))
         line_merge("up", incoming_up, (grad_rows,))
         if paired:
-            kept = lax.dynamic_index_in_dim(patch_parts, x, 1, keepdims=False)
-            summed = kept.astype(F32) + patch_got[0].reshape(kept.shape).astype(F32)
-            summed = jnp.where(flip == 1, summed[::-1], summed).astype(BF16)
-            results["patch"] = summed[:1], summed[1:]
+            patch_kept = lax.dynamic_index_in_dim(patch_parts, x, 1, keepdims=False)
+            patch_kept, patch_sent = [
+                jnp.where(flip == 1, v.astype(F32)[::-1], v.astype(F32)).astype(BF16)
+                for v in (patch_kept, patch_sent)
+            ]
             mine = lax.dynamic_index_in_dim(
                 gains_near[:3].reshape(3, 4, 2, n_mp, width), x, 2, keepdims=False
             )
@@ -950,12 +986,13 @@
             mine = jnp.where(flip == 1, mine[::-1], mine)
             mine = jnp.pad(mine, ((0, 0), (0, 29), (0, 128 - width))).astype(BF16)
             results["gains"] = mine[:1], mine[1:]
-            early, late = ["down", "gate", "up"], ["c_out", "c_query", "c_key", "c_value", "w_out"]
-            late += ["patch", "gains"]
-            names = early + late + ["w_query", "w_key", "w_value"]
+            early, late = ["down", "gate"], ["c_value", "w_out", "c_out"]
+            merged = ["up", "c_query", "c_key"]
+            late.append("gains")
+            names = early + merged + late + ["w_query", "w_key", "w_value", "patch"]
             sums = line_sums(
-                [results["down"], results["gate"]], [results["up"]], [results[n] for n in late],
-                [grad_sq, grad_sk, grad_sv], *split_one,
+                *[[results[n] for n in group] for group in (early, merged, late)],
+                [grad_sq, grad_sk, grad_sv], *split_one, patch_kept, patch_sent,
             )
             results.update(zip(names, sums))
         else:
@@ -971,8 +1008,11 @@
         if paired:
             gain_total = results["gains"][:3, :width]
         else:
+            gain_total = lax.dynamic_index_in_dim(
+                gains_near[:3].reshape(3, n_dp, n_mp, width), m, 2, keepdims=False
+            )
             gain_total = lax.psum_scatter(
-                gains, ("dp", "mp"), scatter_dimension=1, tiled=True,
+                gain_total.reshape(3, n_dp * width), "dp", scatter_dimension=1, tiled=True
             )
         sum_query, sum_key, sum_value = results["w_query"], results["w_key"], results["w_value"]
         sum_cquery, sum_ckey, sum_cvalue = results["c_query"], results["c_key"], results["c_value"]

time: 672 us -> 625 us (0.930)
  Pallas kernels: 479 us -> 432 us
  waiting for transfers between devices: 23.3 us -> 2.01 us
  matrix products: 75.2 us -> 92.3 us
    pallas_call x1, Pallas kernels: 178 us -> 148 us  [line_sums(): pl.pallas_call(functools.partial(line_kernel, ready, merged, count, pairs...]
    ppermute x21 -> x20, waiting for transfers between devices: 23.3 us -> 2.01 us  [swap(): return lax.ppermute(value, axis, [(i, i ^ bit) for i in range(size)])]
    pallas_call x7, Pallas kernels: 207 us -> 191 us  [boundary(): pl.pallas_call(functools.partial(boundary_kernel, mode, jobs, early), in_...]
    dot_general x12, matrix products: 39.5 us -> 49.4 us  [matmul(): return jnp.dot(left, right, preferred_element_type=F32)]
    unnamed x282 -> x258, local copies, waits for them, and re-layouts: 50 us -> 52.3 us
    ppermute x21 -> x20, starting transfers between devices: 17.8 us -> 16.1 us  [swap(): return lax.ppermute(value, axis, [(i, i ^ bit) for i in range(size)])]
  transfers between devices with their start and end apart: 23 -> 22, of which waited for: 1 -> 2; matrix products, arithmetic and copies ran while one was open for 12% -> 17% of each run, Pallas kernels for 38% -> 37%
where the time goes in v5:
time: 625 us; the launch traced here: 615 us
  Pallas kernels  432 us (69%)
  matrix products  92.3 us (15%)
  local copies, waits for them, and re-layouts  64.9 us (10%)
  starting transfers between devices  16.4 us (3%)
    pallas_call x7, Pallas kernels, boundary(): pl.pallas_call(functools.partial(boundary_kernel, mode, jobs, early), in_...  191 us
    pallas_call x1, Pallas kernels, line_sums(): pl.pallas_call(functools.partial(line_kernel, ready, merged, count, pairs...  148 us
    unnamed x258, local copies, waits for them, and re-layouts  52.3 us
    dot_general x12, matrix products, matmul(): return jnp.dot(left, right, preferred_element_type=F32)  49.4 us
    pallas_call x8, Pallas kernels, pair_grad(): pl.pallas_call(pair_kernel, grid_spec=pltpu.PrefetchScalarGridSpec(num_sc...  40.4 us
    dot_general x9, matrix products, product(): return jnp.einsum(spec, left, right, preferred_element_type=F32)  29.2 us
    pallas_call x2, Pallas kernels, attend_back(): pl.pallas_call(self_back_kernel if causal else cross_back_kernel, grid=(w...  17.2 us
    ppermute x20, starting transfers between devices, swap(): return lax.ppermute(value, axis, [(i, i ^ bit) for i in range(size)])  16.1 us
  transfers between devices with their start and end apart: 22, of which 2 were waited for; matrix products, arithmetic and copies ran while one was open for 17% of the time, Pallas kernels for 37%

profile of v5, /device:TPU:0, one launch (start us, length us, event | category | flops | bytes accessed | tf_op | source)
XLA Modules:
  0.0 614.7 jit_solution(14902056525727685613)
XLA Ops:
  2.8 17.1 %shard_map.289.in_ref.refs_19_ = bf16[512,2048]{1,0:T(8,128)(2,1)S(1)} custom-call(bf16[16,128]{1,0:T(8,128)(2,1)S(1)} %broadcast_in_dim.29.partial.kept, bf16[128,2048]{1,0:T(8,128)(2,1)S(1)} %bitcast.127, bf16[16,128]{1,0:T(8,128)(2,1)S(1)} %broadcast_in_dim.29.partial.kept, f32[1,2048]{1,0:T(1,128)S(1)} %get-tuple-element.228.gain), custom_call_target="tpu_custom_call" | custom-call | flops 2621440 | bytes 62914560 | tf_op jit(solution)/shard_map/pallas_call | solution.py:665
  27.6 4.4 convolution_convert_fusion.13.q_ref
  41.4 5.7 shard_map.290.g_ref
  47.8 10.1 %convolution_convert_fusion.in_ref.a_ref = bf16[1024,2048]{1,0:T(8,128)(2,1)S(1)} fusion(bf16[1024,1664]{1,0:T(8,128)(2,1)S(1)} %bitcast.124, bf16[1664,2048]{1,0:T(8,128)(2,1)} %param.28), kind=kOutput, calls=%fused_computation.2 | convolution fusion | flops 6981419008 | bytes 14417920 | tf_op jit(solution)/shard_map/dot_general | solution.py:19
  63.2 4.5 constant_dynamic-slice_fusion.3
  81.8 6.9 %fusion.37 = f32[512,1280]{1,0:T(8,128)} fusion(bf16[512,2048]{1,0:T(8,128)(2,1)S(1)} %shard_map.291.in_ref.a_ref, bf16[1280,2048]{1,0:T(8,128)(2,1)} %param.31), kind=kOutput, calls=%fused_computation.105 | convolution fusion | flops 2684354560 | bytes 9961472 | tf_op jit(solution)/shard_map/sd,fd->sf/dot_general | solution.py:23
  92.8 31.3 %shard_map.295 = (f32[128,2048]{1,0:T(8,128)S(1)}, bf16[512,2048]{1,0:T(8,128)(2,1)S(1)}, bf16[512,1024]{1,0:T(8,128)(2,1)S(1)}, bf16[512,1024]{1,0:T(8,128)(2,1)S(1)}) custom-call(bf16[512,2048]{1,0:T(8,128)(2,1)S(1)} %convolution_convert_fusion.5.partial, bf16[128,2048]{1,0:T(8,128)(2,1)S(1)} %bitcast.128, ...), custom_call_target="tpu_custom_call" | custom-call | flops 2621440 | bytes 62914560 | tf_op jit(solution)/shard_map/pallas_call | solution.py:665
  127.3 8.0 %shard_map.296.g_ref = bf16[512,512]{1,0:T(8,128)(2,1)} custom-call(bf16[512,512]{1,0:T(8,128)(2,1)S(1)} %convolution_convert_fusion.10.q_ref, bf16[1024,512]{1,0:T(8,128)(2,1)S(1)} %copy-done.78, bf16[1024,512]{1,0:T(8,128)(2,1)S(1)} %copy-done.80, s32[512,1]{1,0:T(8,128)S(1)} %copy-done.73, s32[1,1024]{1,0:T(1,128)S(1)} %and_select_fusion.col_ref), custom_call_target="tpu_custom_call" | custom-call | flops 1073741824 | bytes 3145728 | tf_op jit(solution)/shard_map/pallas_call | solution.py:89
  137.6 31.0 %shard_map.299 = (f32[128,2048]{1,0:T(8,128)S(1)}, bf16[512,2048]{1,0:T(8,128)(2,1)S(1)}, bf16[256,1024]{1,0:T(8,128)(2,1)S(1)}, bf16[256,1024]{1,0:T(8,128)(2,1...) custom-call(bf16[512,2048]{1,0:T(8,128)(2,1)S(1)} %convolution_convert_fusion.4.partial, ...), custom_call_target="tpu_custom_call" | custom-call | flops 2621440 | bytes 62914560 | tf_op jit(solution)/shard_map/pallas_call | solution.py:665
  170.6 6.1 fusion.38
  176.9 6.4 %multiply_convert_fusion = (bf16[512,1280]{1,0:T(8,128)(2,1)}, bf16[512,1280]{1,0:T(8,128)(2,1)}, bf16[512,1280]{1,0:T(8,128)(2,1)S(1)}) fusion(f32[512,1280]{1,0:T(8,128)S(1)} %copy-done.119, f32[512,1280]{1,0:T(8,128)S(1)} %fusion.38, bf16[512,2048]{1,0:T(8,128)(2,1)S(1)} %get-tuple-element.97.in_ref.a_ref, bf16[2048,1280]{1,0:T(8,128)(2,1)S(1)} %bitcast.150), kind=kOutput, calls=%fused_computation.17 | convolution fusion | flops 2701393920 | bytes 16515072 | tf_op jit(solution)/shard_map/dot_general | solution.py:19
  183.2 5.8 fusion.39
  190.0 7.0 %add_convert_fusion.1.partial = bf16[512,2048]{1,0:T(8,128)(2,1)S(1)} fusion(f32[512,2048]{1,0:T(8,128)} %fusion.39, bf16[512,1280]{1,0:T(8,128)(2,1)} %get-tuple-element.112.g_ref, bf16[2048,1280]{1,0:T(8,128)(2,1)} %param.30), kind=kOutput, calls=%fused_computation.1 | convolution fusion | flops 2686451712 | bytes 12845056 | tf_op jit(solution)/shard_map/sf,df->sd/dot_general | solution.py:23
  198.1 5.6 convolution_convert_fusion.3.partial
  203.8 15.4 %shard_map.301.rest_0_ = f32[128,2048]{1,0:T(8,128)S(1)} custom-call(bf16[512,2048]{1,0:T(8,128)(2,1)S(1)} %convolution_convert_fusion.3.partial, f32[128,2048]{1,0:T(8,128)S(1)} %get-tuple-element.99.rows.kept, bf16[16,128]{1,0:T(8,128)(2,1)S(1)} %broadcast_in_dim.29.partial.kept, f32[1,2048]{1,0:T(1,128)S(1)} %get-tuple-element.228.gain), custom_call_target="tpu_custom_call" | custom-call | flops 2621440 | bytes 62914560 | tf_op jit(solution)/shard_map/pallas_call | solution.py:665
  222.8 5.5 shard_map.302
  231.9 29.6 %shard_map.303 = (f32[128,2048]{1,0:T(8,128)S(1)}, bf16[512,2048]{1,0:T(8,128)(2,1)S(1)}, f32[1,2048]{1,0:T(1,128)S(1)}) custom-call(bf16[512,2048]{1,0:T(8,128)(2,1)S(1)} %add_convert_fusion.1.partial, bf16[128,2048]{1,0:T(8,128)(2,1)} %bitcast.8.refs_0_.rows, f32[128,2048]{1,0:T(8,128)S(1)} %get-tuple-element.99.rows.kept, ...), custom_call_target="tpu_custom_call" | custom-call | flops 2621440 | bytes 62914560 | tf_op jit(solution)/shard_map/pallas_call | solution.py:665
  261.4 7.5 %shard_map.304 = (bf16[1,256,1280]{2,1,0:T(8,128)(2,1)S(1)}, bf16[3,256,1280]{2,1,0:T(8,128)(2,1)}) custom-call(s32[4]{0:T(128)S(1)} %broadcast_add_fusion.at_ref, bf16[512,2048]{1,0:T(8,128)(2,1)S(1)} %get-tuple-element.97.in_ref.a_ref, bf16[256,1024]{1,0:T(8,128)(2,1)} %collective-permute-done.6.lo_ref, bf16[256,1024]{1,0:T(8,128)(2,1)} %collective-permute-done.8.hi_ref, ...), custom_call_target="tpu_custom_call" | custom-call | flops 2684354560 | bytes 7340032 | tf_op jit(solution)/shard_map/pallas_call | solution.py:241
  272.5 9.8 %shard_map.305 = (bf16[512,512]{1,0:T(8,128)(2,1)S(1)}, bf16[2,1024,512]{2,1,0:T(8,128)(2,1)S(1)}) custom-call(bf16[512,512]{1,0:T(8,128)(2,1)S(1)} %copy-done.83, bf16[1024,512]{1,0:T(8,128)(2,1)S(1)} %copy-done.79, bf16[1024,512]{1,0:T(8,128)(2,1)S(1)} %copy-done.81, s32[512,1]{1,0:T(8,128)S(1)} %copy-done.73, s32[1,1024]{1,0:T(1,128)S(1)} %and_select_fusion.col_ref, ...), custom_call_target="tpu_custom_call" | custom-call | flops 2684354560 | bytes 6291456 | tf_op jit(solution)/shard_map/pallas_call | solution.py:142
  284.6 7.4 %shard_map.306 = (bf16[1,256,1280]{2,1,0:T(8,128)(2,1)S(1)}, bf16[3,256,1280]{2,1,0:T(8,128)(2,1)}) custom-call(s32[4]{0:T(128)S(1)} %broadcast_add_fusion.at_ref, bf16[512,2048]{1,0:T(8,128)(2,1)S(1)} %get-tuple-element.97.in_ref.a_ref, bf16[256,1024]{1,0:T(8,128)(2,1)} %collective-permute-done.6.lo_ref, bf16[256,1024]{1,0:T(8,128)(2,1)} %collective-permute-done.8.hi_ref, ...), custom_call_target="tpu_custom_call" | custom-call | flops 2684354560 | bytes 7340032 | tf_op jit(solution)/shard_map/pallas_call | solution.py:241
  297.2 28.1 %shard_map.308 = (f32[128,2048]{1,0:T(8,128)S(1)}, bf16[512,2048]{1,0:T(8,128)(2,1)S(1)}, f32[1,2048]{1,0:T(1,128)S(1)}) custom-call(bf16[512,2048]{1,0:T(8,128)(2,1)S(1)} %convolution_convert_fusion.2.rest_0_.partial, f32[128,2048]{1,0:T(8,128)S(1)} %get-tuple-element.116.rows, f32[128,2048]{1,0:T(8,128)S(1)} %get-tuple-element.95.rows.kept, ...), custom_call_target="tpu_custom_call" | custom-call | flops 2621440 | bytes 62914560 | tf_op jit(solution)/shard_map/pallas_call | solution.py:665
  337.8 7.5 %shard_map.309 = (bf16[512,512]{1,0:T(8,128)(2,1)S(1)}, bf16[512,512]{1,0:T(8,128)(2,1)S(1)}, bf16[512,512]{1,0:T(8,128)(2,1)S(1)}) custom-call(bf16[512,512]{1,0:T(8,128)(2,1)S(1)} %copy-done.55, bf16[512,512]{1,0:T(8,128)(2,1)S(1)} %copy-done.57, bf16[512,512]{1,0:T(8,128)(2,1)S(1)} %copy-done.59, s32[512,2]{1,0:T(8,128)S(1)} %copy-done.39, ...), custom_call_target="tpu_custom_call" | custom-call | flops 1342177280 | bytes 4194304 | tf_op jit(solution)/shard_map/pallas_call | solution.py:142
  370.7 38.3 %shard_map.316 = (f32[128,2048]{1,0:T(8,128)S(1)}, f32[8,2048]{1,0:T(8,128)S(1)}, bf16[256,1024]{1,0:T(8,128)(2,1)S(1)}, bf16[256,1024]{1,0:T(8,128)(2,1)S(1)}, ...) custom-call(bf16[512,2048]{1,0:T(8,128)(2,1)S(1)} %add_convert_fusio, ...), custom_call_target="tpu_custom_call" | custom-call | flops 2621440 | bytes 62914560 | tf_op jit(solution)/shard_map/pallas_call | solution.py:665
  448.5 147.6 %shard_map.324 = (f32[256,1280]{1,0:T(8,128)}, f32[256,1280]{1,0:T(8,128)}, f32[256,1280]{1,0:T(8,128)}, f32[256,512]{1,0:T(8,128)}, f32[256,512]{1,0:T(8,128)},...) custom-call(bf16[2,256,1280]{2,1,0:T(8,128)(2,1)} %copy-done.27, ...), custom_call_target="tpu_custom_call" | custom-call | flops 8568832 | bytes 85688320 | tf_op jit(solution)/shard_map/pallas_call | solution.py:471
  (381 shorter events, 165.7 us)
Async XLA Ops:
  21.2 50.9 %collective-permute-start = (bf16[128,2048]{1,0:T(8,128)(2,1)}, bf16[128,2048]{1,0:T(8,128)(2,1)}, u32[]{:S(2)}, u32[]{:S(2)}) collective-permute-start(bf16[128,2048]{1,0:T(8,128)(2,1)} %bitcast.8.refs_0_.rows), channel_id=1, source_target_pairs={{0,2},{1,3},{2,0},{3,1},{4,6},{5,7},{6,4},{7,5},{8,10},{9,11},{10,... | collective-permute-start | bytes 1572872 | tf_op jit(solution)/shard_map/ppermute | solution.py:707
  22.3 56.7 %collective-permute-start.1 = (bf16[128,2048]{1,0:T(8,128)(2,1)}, bf16[128,2048]{1,0:T(8,128)(2,1)}, u32[]{:S(2)}, u32[]{:S(2)}) collective-permute-start(bf16[128,2048]{1,0:T(8,128)(2,1)} %bitcast.8.refs_0_.rows), channel_id=1, source_target_pairs={{0,1},{1,0},{2,3},{3,2},{4,5},{5,4},{6,7},{7,6},{8,9},{9,8},{10,11... | collective-permute-start | bytes 1572872 | tf_op jit(solution)/shard_map/ppermute | solution.py:707
  26.1 52.3 %collective-permute-start.3 = (bf16[256,1024]{1,0:T(8,128)(2,1)}, bf16[256,1024]{1,0:T(8,128)(2,1)}, u32[]{:S(2)}, u32[]{:S(2)}) collective-permute-start(bf16[256,1024]{1,0:T(8,128)(2,1)} %shard_map.292), channel_id=1, source_target_pairs={{0,4},{4,0},{8,12},{12,8},{16,20},{20,16},{24,28},{28,24},{1,5},{5... | collective-permute-start | bytes 1572872 | tf_op jit(solution)/shard_map/ppermute | solution.py:707
  47.2 76.9 %collective-permute-start.5 = (bf16[512,512]{1,0:T(8,128)(2,1)}, bf16[512,512]{1,0:T(8,128)(2,1)}, u32[]{:S(2)}, u32[]{:S(2)}) collective-permute-start(bf16[512,512]{1,0:T(8,128)(2,1)} %shard_map.290.g_ref), channel_id=1, source_target_pairs={{0,4},{4,0},{8,12},{12,8},{16,20},{20,16},{24,28},{28,24},{1,5},{5... | collective-permute-start | bytes 1572872 | tf_op jit(solution)/shard_map/ppermute | solution.py:707
  72.1 6.9 %collective-permute-start.2 = (bf16[128,2048]{1,0:T(8,128)(2,1)}, bf16[128,2048]{1,0:T(8,128)(2,1)}, u32[]{:S(2)}, u32[]{:S(2)}) collective-permute-start(bf16[128,2048]{1,0:T(8,128)(2,1)} %collective-permute-done.refs_1_), channel_id=1, source_target_pairs={{0,1},{1,0},{2,3},{3,2},{4,5},{5,4},{6,7},{7,6},{8,9},{9,8},{10,11... | collective-permute-start | bytes 1572872 | tf_op jit(solution)/shard_map/ppermute | solution.py:707
  78.5 11.0 %collective-permute-start.4 = (bf16[256,1024]{1,0:T(8,128)(2,1)}, bf16[256,1024]{1,0:T(8,128)(2,1)S(1)}, u32[]{:S(2)}, u32[]{:S(2)}) collective-permute-start(bf16[256,1024]{1,0:T(8,128)(2,1)} %collective-permute-done.3.refs_20_), channel_id=1, source_target_pairs={{0,1},{1,0},{2,3},{3,2},{4,5},{5,4},{6,7},{7,6},{8,9},{9,8},{10,11... | collective-permute-start | bytes 1572872 | tf_op jit(solution)/shard_map/ppermute | solution.py:707
  169.5 19.5 %collective-permute-start.6 = (bf16[256,1024]{1,0:T(8,128)(2,1)S(1)}, bf16[256,1024]{1,0:T(8,128)(2,1)}, u32[]{:S(2)}, u32[]{:S(2)}) collective-permute-start(bf16[256,1024]{1,0:T(8,128)(2,1)S(1)} %shard_map.300), channel_id=1, source_target_pairs={{0,4},{4,0},{8,12},{12,8},{16,20},{20,16},{24,28},{28,24},{1,5},{5... | collective-permute-start | bytes 1572872 | tf_op jit(solution)/shard_map/ppermute | solution.py:707
  189.0 31.7 %collective-permute-start.7 = (bf16[512,1280]{1,0:T(8,128)(2,1)S(1)}, bf16[512,1280]{1,0:T(8,128)(2,1)S(1)}, u32[]{:S(2)}, u32[]{:S(2)}) collective-permute-start(bf16[512,1280]{1,0:T(8,128)(2,1)S(1)} %get-tuple-element.102.g_ref), channel_id=1, source_target_pairs={{0,4},{4,0},{8,12},{12,8},{16,20},{20,16},{24,28},{28,24},{1,5},{5... | collective-permute-start | bytes 3932168 | tf_op jit(solution)/shard_map/ppermute | solution.py:707
  197.0 64.4 %collective-permute-start.9 = (bf16[512,1280]{1,0:T(8,128)(2,1)}, bf16[512,1280]{1,0:T(8,128)(2,1)}, u32[]{:S(2)}, u32[]{:S(2)}) collective-permute-start(bf16[512,1280]{1,0:T(8,128)(2,1)} %get-tuple-element.107.g_ref), channel_id=1, source_target_pairs={{0,4},{4,0},{8,12},{12,8},{16,20},{20,16},{24,28},{28,24},{1,5},{5... | collective-permute-start | bytes 3932168 | tf_op jit(solution)/shard_map/ppermute | solution.py:707
  219.2 42.3 %collective-permute-start.8 = (bf16[256,1024]{1,0:T(8,128)(2,1)}, bf16[256,1024]{1,0:T(8,128)(2,1)}, u32[]{:S(2)}, u32[]{:S(2)}) collective-permute-start(bf16[256,1024]{1,0:T(8,128)(2,1)} %collective-permute-done.6.lo_ref), channel_id=1, source_target_pairs={{0,1},{1,0},{2,3},{3,2},{4,5},{5,4},{6,7},{7,6},{8,9},{9,8},{10,11... | collective-permute-start | bytes 1572872 | tf_op jit(solution)/shard_map/ppermute | solution.py:707
  228.3 64.8 %collective-permute-start.11 = (bf16[3,256,1280]{2,1,0:T(8,128)(2,1)}, bf16[3,256,1280]{2,1,0:T(8,128)(2,1)}, u32[]{:S(2)}, u32[]{:S(2)}) collective-permute-start(bf16[3,256,1280]{2,1,0:T(8,128)(2,1)} %get-tuple-element.104.left_ref), channel_id=1, source_target_pairs={{0,8},{4,12},{8,0},{12,4},{16,24},{20,28},{24,16},{28,20},{1,9},{5... | collective-permute-start | bytes 5898248 | tf_op jit(solution)/shard_map/ppermute | solution.py:707
  230.7 53.9 %collective-permute-start.10 = (bf16[512,1280]{1,0:T(8,128)(2,1)}, bf16[512,1280]{1,0:T(8,128)(2,1)}, u32[]{:S(2)}, u32[]{:S(2)}) collective-permute-start(bf16[512,1280]{1,0:T(8,128)(2,1)} %get-tuple-element.112.g_ref), channel_id=1, source_target_pairs={{0,4},{4,0},{8,12},{12,8},{16,20},{20,16},{24,28},{28,24},{1,5},{5... | collective-permute-start | bytes 3932168 | tf_op jit(solution)/shard_map/ppermute | solution.py:707
  231.8 127.1 %copy-start.16 = (bf16[512,1024]{1,0:T(8,128)(2,1)}, bf16[512,1024]{1,0:T(8,128)(2,1)S(1)}, u32[]{:S(2)}) copy-start(bf16[512,1024]{1,0:T(8,128)(2,1)S(1)} %get-tuple-element.223.hi_ref) | copy-start | bytes 3145732
  231.8 127.1 %copy-start.18 = (bf16[512,1024]{1,0:T(8,128)(2,1)}, bf16[512,1024]{1,0:T(8,128)(2,1)S(1)}, u32[]{:S(2)}) copy-start(bf16[512,1024]{1,0:T(8,128)(2,1)S(1)} %get-tuple-element.224.lo_ref) | copy-start | bytes 3145732
  269.0 82.9 %collective-permute-start.15 = (bf16[3,256,1280]{2,1,0:T(8,128)(2,1)}, bf16[3,256,1280]{2,1,0:T(8,128)(2,1)}, u32[]{:S(2)}, u32[]{:S(2)}) collective-permute-start(bf16[3,256,1280]{2,1,0:T(8,128)(2,1)} %get-tuple-element.109.left_ref), channel_id=1, source_target_pairs={{0,8},{4,12},{8,0},{12,4},{16,24},{20,28},{24,16},{28,20},{1,9},{5... | collective-permute-start | bytes 5898248 | tf_op jit(solution)/shard_map/ppermute | solution.py:707
  282.3 75.1 %collective-permute-start.13 = (bf16[2,1024,512]{2,1,0:T(8,128)(2,1)S(1)}, bf16[2,1024,512]{2,1,0:T(8,128)(2,1)S(1)}, u32[]{:S(2)}, u32[]{:S(2)}) collective-permute-start(bf16[2,1024,512]{2,1,0:T(8,128)(2,1)S(1)} %get-tuple-element.119.g_ref), channel_id=1, source_target_pairs={{0,4},{4,0},{8,12},{12,8},{16,20},{20,16},{24,28},{28,24},{1,5},{5... | collective-permute-start | bytes 6291464 | tf_op jit(solution)/shard_map/ppermute | solution.py:707
  292.0 121.9 %collective-permute-start.20 = (bf16[3,256,1280]{2,1,0:T(8,128)(2,1)}, bf16[3,256,1280]{2,1,0:T(8,128)(2,1)}, u32[]{:S(2)}, u32[]{:S(2)}) collective-permute-start(bf16[3,256,1280]{2,1,0:T(8,128)(2,1)} %get-tuple-element.114.left_ref), channel_id=1, source_target_pairs={{0,8},{4,12},{8,0},{12,4},{16,24},{20,28},{24,16},{28,20},{1,9},{5... | collective-permute-start | bytes 5898248 | tf_op jit(solution)/shard_map/ppermute | solution.py:707
  328.3 6.0 collective-permute-start.12
  331.1 32.1 %collective-permute-start.14 = (bf16[1024,512]{1,0:T(8,128)(2,1)}, bf16[1024,512]{1,0:T(8,128)(2,1)S(1)}, u32[]{:S(2)}, u32[]{:S(2)}) collective-permute-start(bf16[1024,512]{1,0:T(8,128)(2,1)} %add_convert_fusion.4), channel_id=1, source_target_pairs={{0,1},{1,0},{2,3},{3,2},{4,5},{5,4},{6,7},{7,6},{8,9},{9,8},{10,11... | collective-permute-start | bytes 3145736 | tf_op jit(solution)/shard_map/ppermute | solution.py:707
  334.3 34.6 %collective-permute-start.16 = (bf16[2,256,1280]{2,1,0:T(8,128)(2,1)S(1)}, bf16[2,256,1280]{2,1,0:T(8,128)(2,1)S(1)}, u32[]{:S(2)}, u32[]{:S(2)}) collective-permute-start(bf16[2,256,1280]{2,1,0:T(8,128)(2,1)S(1)} %copy-done.99), channel_id=1, source_target_pairs={{0,1},{1,0},{2,3},{3,2},{4,5},{5,4},{6,7},{7,6},{8,16},{9,17},{10,... | collective-permute-start | bytes 3932168 | tf_op jit(solution)/shard_map/ppermute | solution.py:747
  351.8 14.2 %collective-permute-start.17 = (bf16[512,512]{1,0:T(8,128)(2,1)S(1)}, bf16[512,512]{1,0:T(8,128)(2,1)S(1)}, u32[]{:S(2)}, u32[]{:S(2)}) collective-permute-start(bf16[512,512]{1,0:T(8,128)(2,1)S(1)} %copy-done.53), channel_id=1, source_target_pairs={{0,4},{4,0},{8,12},{12,8},{16,20},{20,16},{24,28},{28,24},{1,5},{5... | collective-permute-start | bytes 1572872 | tf_op jit(solution)/shard_map/ppermute | solution.py:707
  357.8 82.3 %collective-permute-start.21 = (bf16[1024,512]{1,0:T(8,128)(2,1)}, bf16[1024,512]{1,0:T(8,128)(2,1)}, u32[]{:S(2)}, u32[]{:S(2)}) collective-permute-start(bf16[1024,512]{1,0:T(8,128)(2,1)} %add_convert_fusion.6), channel_id=1, source_target_pairs={{0,2},{1,3},{2,0},{3,1},{4,6},{5,7},{6,4},{7,5},{8,10},{9,11},{10,... | collective-permute-start | bytes 3145736 | tf_op jit(solution)/shard_map/ppermute | solution.py:707
  363.2 82.6 %collective-permute-start.18 = (bf16[2,256,1280]{2,1,0:T(8,128)(2,1)}, bf16[2,256,1280]{2,1,0:T(8,128)(2,1)}, u32[]{:S(2)}, u32[]{:S(2)}) collective-permute-start(bf16[2,256,1280]{2,1,0:T(8,128)(2,1)} %slice.51), channel_id=1, source_target_pairs={{0,1},{1,0},{2,3},{3,2},{4,5},{5,4},{6,7},{7,6},{8,16},{9,17},{10,... | collective-permute-start | bytes 3932168 | tf_op jit(solution)/shard_map/ppermute | solution.py:747
  410.6 24.3 %collective-permute-start.19 = (bf16[512,512]{1,0:T(8,128)(2,1)}, bf16[512,512]{1,0:T(8,128)(2,1)}, u32[]{:S(2)}, u32[]{:S(2)}) collective-permute-start(bf16[512,512]{1,0:T(8,128)(2,1)} %shard_map.296.g_ref), channel_id=1, source_target_pairs={{0,4},{4,0},{8,12},{12,8},{16,20},{20,16},{24,28},{28,24},{1,5},{5... | collective-permute-start | bytes 1572872 | tf_op jit(solution)/shard_map/ppermute | solution.py:707
  (120 other events, 545.8 us)

commit v6 on v5

--- a/solution.py
+++ b/solution.py
@@ -51,13 +51,21 @@
     return grad_rows, jnp.sum(grad * rows * inv, axis=0)
 
 
-VMEM_LIMIT = 20 * 2**20
+VMEM_LIMIT = 17 * 2**20
+GELU_SCALE = 0.7978845608028654
+GELU_CUBE = 0.044715
 ANY = pl.BlockSpec(memory_space=pl.ANY)
 
 
 def params(grid_rank):
     return pltpu.CompilerParams(
         dimension_semantics=("arbitrary",) * grid_rank, vmem_limit_bytes=VMEM_LIMIT
+    )
+
+
+def wide_params(grid_rank, size=28):
+    return pltpu.CompilerParams(
+        dimension_semantics=("arbitrary",) * grid_rank, vmem_limit_bytes=size * 2**20
     )
 
 
@@ -485,6 +493,94 @@
         ),
         cost_estimate=cost(4 * sum(sizes), 40 * sum(sizes)),
     )(*parts, *rests, *grads, own, low, high, kept, sent)
+
+
+def feed_kernel(n_ref, g_ref, u_ref, three_ref, down_ref, hid_ref, gate_ref, up_ref):
+    gate = matmul(n_ref[...], g_ref[...])
+    up = matmul(n_ref[...], u_ref[...])
+    grad = cols_dot(three_ref[...], down_ref[...])
+    square = gate * gate
+    tanh = jnp.tanh(GELU_SCALE * (gate + GELU_CUBE * (gate * square)))
+    half = 0.5 * (1.0 + tanh)
+    gelu = gate * half
+    slope = half + 0.5 * gate * (1.0 - tanh * tanh) * (
+        GELU_SCALE * (1.0 + 3.0 * GELU_CUBE * square)
+    )
+    hid_ref[...] = (gelu * up).astype(BF16)
+    gate_ref[...] = (grad * up * slope).astype(BF16)
+    up_ref[...] = (grad * gelu).astype(BF16)
+
+
+def feed(normed, w_gate, w_up, grad_three, w_down):
+    length, model = normed.shape
+    units = w_gate.shape[1]
+    tile = 256
+    column = lambda rows: pl.BlockSpec((rows, tile), lambda j: (0, j))
+    whole = pl.BlockSpec((length, model), lambda j: (0, 0))
+    return pl.pallas_call(
+        feed_kernel,
+        grid=(units // tile,),
+        in_specs=[
+            whole, column(model), column(model), whole,
+            pl.BlockSpec((tile, model), lambda j: (j, 0)),
+        ],
+        out_specs=(column(length),) * 3,
+        out_shape=(jax.ShapeDtypeStruct((length, units), BF16),) * 3,
+        compiler_params=wide_params(1),
+        cost_estimate=cost(6 * length * model * units, 6 * model * units + 6 * length * units),
+    )(normed, w_gate, w_up, grad_three, w_down)
+
+
+def feed_back_kernel(gate_ref, up_ref, g_ref, u_ref, out_ref):
+    total = cols_dot(gate_ref[...], g_ref[...]) + cols_dot(up_ref[...], u_ref[...])
+    out_ref[...] = total.astype(BF16)
+
+
+def feed_back(grad_gate, grad_up, w_gate, w_up):
+    length, units = grad_gate.shape
+    model = w_gate.shape[0]
+    tile = 512
+    whole = pl.BlockSpec((length, units), lambda j: (0, 0))
+    row = pl.BlockSpec((tile, units), lambda j: (j, 0))
+    return pl.pallas_call(
+        feed_back_kernel,
+        grid=(model // tile,),
+        in_specs=[whole, whole, row, row],
+        out_specs=pl.BlockSpec((length, tile), lambda j: (0, j)),
+        out_shape=jax.ShapeDtypeStruct((length, model), BF16),
+        compiler_params=wide_params(1),
+        cost_estimate=cost(4 * length * model * units, 4 * model * units + 4 * length * units),
+    )(grad_gate, grad_up, w_gate, w_up)
+
+
+def finish_kernel(turned, *refs):
+    for turn, source, target in zip(turned, refs[: len(turned)], refs[len(turned) :]):
+        target[...] = source[...].T if turn else source[...]
+
+
+def finish(arrays, turned):
+    steps = 2
+    in_specs, out_specs, shapes = [], [], []
+    for arr, turn in zip(arrays, turned):
+        rows, width = arr.shape
+        cut = rows // steps if rows // steps >= 128 else rows
+        at = (lambda i: i) if cut < rows else (lambda i: 0)
+        in_specs.append(pl.BlockSpec((cut, width), lambda i, at=at: (at(i), 0)))
+        if turn:
+            out_specs.append(pl.BlockSpec((width, cut), lambda i, at=at: (0, at(i))))
+            shapes.append(jax.ShapeDtypeStruct((width, rows), F32))
+        else:
+            out_specs.append(pl.BlockSpec((cut, width), lambda i, at=at: (at(i), 0)))
+            shapes.append(jax.ShapeDtypeStruct((rows, width), F32))
+    return pl.pallas_call(
+        functools.partial(finish_kernel, turned),
+        grid=(steps,),
+        in_specs=in_specs,
+        out_specs=out_specs,
+        out_shape=shapes,
+        compiler_params=wide_params(1, 60),
+        cost_estimate=cost(0, 8 * sum(a.size for a in arrays)),
+    )(*arrays)
 
 
 CHUNKS = 4
@@ -683,7 +779,7 @@
             else []
         ),
         compiler_params=pltpu.CompilerParams(
-            collective_id=number, has_side_effects=True, vmem_limit_bytes=2 * VMEM_LIMIT
+            collective_id=number, has_side_effects=True, vmem_limit_bytes=22 * 2**20
         ),
         cost_estimate=cost(10 * step * width, 60 * 2**20),
     )(partial, rows, kept, gain, *given, *wanted, *along)
@@ -693,10 +789,6 @@
     plain = len(outs) - 2 * jobs - early
     halves = list(zip(outs[plain : plain + jobs], outs[plain + jobs :]))
     return outs[:plain] + halves + outs[plain + 2 * jobs :]
-
-
-def gated_unit(gate_arg, up_arg):
-    return jax.nn.gelu(gate_arg, approximate=True) * up_arg
 
 
 def layer(n_dp, n_mp):
@@ -834,18 +926,14 @@
             exchange((grad_three,), (normed_two,)),
         )
         split_cotangent, split_two = map(split, (grad_three, normed_two), halves or none)
-        grad_hidden = tie(product("sd,fd->sf", grad_three, w_down), ())
         if paired:
             wanted = wanted_of(normed_three)
             low_three = beside(wanted)
             split_three = normed_three, low_three, core(low_three)
-            normed_three = tie(normed_three, (grad_hidden, wanted))
+            normed_three = tie(normed_three, wanted)
         else:
             split_three, low_three = (normed_three,), normed_three
-        gate_pre, up_pre = matmul(normed_three, w_gate), matmul(normed_three, w_up)
-        hidden, pull = jax.vjp(gated_unit, gate_pre, up_pre)
-        hidden = hidden.astype(BF16)
-        grad_gate, grad_up = [g.astype(BF16) for g in pull(grad_hidden)]
+        hidden, grad_gate, grad_up = feed(normed_three, w_gate, w_up, grad_three, w_down)
 
         results, turned = {}, {}
 
@@ -877,9 +965,7 @@
                 results[name] = cross_add(inner.reshape(1), first, rest, inner_swap(rest[1:]))
 
         hidden_far = far_of(tie(hidden, low_three))
-        partial = (
-            product("sf,df->sd", grad_gate, w_gate) + product("sf,df->sd", grad_up, w_up)
-        ).astype(BF16)
+        partial = feed_back(grad_gate, grad_up, w_gate, w_up)
         gate_far, up_far = [far_of(v) for v in tie((grad_gate, grad_up), partial)]
         partial_out = matmul(tie(hidden, partial), w_down).astype(BF16)
         [output] = boundary("sum", 7, partial_out, after_cross, nothing, gain_rows[0])
@@ -1003,7 +1089,9 @@
             line("w_key", split_one, grad_sk, grad_sk, True)
             line("w_value", split_one, grad_sv, grad_sv, True)
         turned["patch"] = True
-        results = {n: v.T if turned.get(n) else v for n, v in results.items()}
+        names = [n for n in results if n != "gains"]
+        turns = tuple(bool(turned.get(n)) for n in names)
+        results.update(zip(names, finish([results[n] for n in names], turns)))
         patch_total = results["patch"]
         if paired:
             gain_total = results["gains"][:3, :width]

time: 625 us -> 597 us (0.955)
  matrix products: 92.3 us -> 63.5 us
  Pallas kernels: 432 us -> 448 us
  local copies, waits for them, and re-layouts: 64.9 us -> 49.8 us
    pallas_call x0 -> x3, Pallas kernels: none -> 24.5 us  [the longest x1 10.8 us: feed(): pl.pallas_call(feed_kernel, grid=(units // tile,), in_specs=[whole, colum...]
    dot_general x9 -> x6, matrix products: 29.2 us -> 9.37 us  [product(): return jnp.einsum(spec, left, right, preferred_element_type=F32)]
    unnamed x258 -> x225, local copies, waits for them, and re-layouts: 52.3 us -> 39.7 us
    dot_general x12 -> x10, matrix products: 49.4 us -> 39 us  [matmul(): return jnp.dot(left, right, preferred_element_type=F32)]
  transfers between devices with their start and end apart: 22 -> 22, of which waited for: 2 -> 2; matrix products, arithmetic and copies ran while one was open for 17% -> 12% of each run, Pallas kernels for 37% -> 40%
where the time goes in v6:
time: 597 us; the launch traced here: 587 us
  Pallas kernels  448 us (75%)
  matrix products  63.5 us (11%)
  local copies, waits for them, and re-layouts  49.8 us (8%)
  starting transfers between devices  16.5 us (3%)
    pallas_call x7, Pallas kernels, boundary(): pl.pallas_call(functools.partial(boundary_kernel, mode, jobs, early), in_...  191 us
    pallas_call x1, Pallas kernels, line_sums(): pl.pallas_call(functools.partial(line_kernel, ready, merged, count, pairs...  148 us
    unnamed x225, local copies, waits for them, and re-layouts  39.7 us
    dot_general x10, matrix products, matmul(): return jnp.dot(left, right, preferred_element_type=F32)  39 us
    pallas_call x8, Pallas kernels, pair_grad(): pl.pallas_call(pair_kernel, grid_spec=pltpu.PrefetchScalarGridSpec(num_sc...  38 us
    pallas_call x2, Pallas kernels, attend_back(): pl.pallas_call(self_back_kernel if causal else cross_back_kernel, grid=(w...  16.9 us
    ppermute x20, starting transfers between devices, swap(): return lax.ppermute(value, axis, [(i, i ^ bit) for i in range(size)])  16.2 us
    pallas_call x2, Pallas kernels, attend(): pl.pallas_call(functools.partial(attend_kernel, causal), grid=(width // H...  13.7 us
  transfers between devices with their start and end apart: 22, of which 2 were waited for; matrix products, arithmetic and copies ran while one was open for 12% of the time, Pallas kernels for 40%

profile of v6, /device:TPU:0, one launch (start us, length us, event | category | flops | bytes accessed | tf_op | source)
XLA Modules:
  0.0 587.2 jit_solution(4414441084976476467)
XLA Ops:
  2.8 17.1 %shard_map.289.in_ref.refs_19_ = bf16[512,2048]{1,0:T(8,128)(2,1)S(1)} custom-call(bf16[16,128]{1,0:T(8,128)(2,1)S(1)} %broadcast_in_dim.29.partial.kept, bf16[128,2048]{1,0:T(8,128)(2,1)S(1)} %bitcast.113, bf16[16,128]{1,0:T(8,128)(2,1)S(1)} %broadcast_in_dim.29.partial.kept, f32[1,2048]{1,0:T(1,128)S(1)} %get-tuple-element.255.gain), custom_call_target="tpu_custom_call" | custom-call | flops 2621440 | bytes 62914560 | tf_op jit(solution)/shard_map/pallas_call | solution.py:761
  27.6 4.4 convolution_convert_fusion.13.q_ref
  41.4 5.7 shard_map.290.g_ref
  47.7 9.9 %convolution_convert_fusion.in_ref.a_ref = bf16[1024,2048]{1,0:T(8,128)(2,1)S(1)} fusion(bf16[1024,1664]{1,0:T(8,128)(2,1)S(1)} %bitcast.110, bf16[1664,2048]{1,0:T(8,128)(2,1)} %param.28), kind=kOutput, calls=%fused_computation.1 | convolution fusion | flops 6981419008 | bytes 14417920 | tf_op jit(solution)/shard_map/dot_general | solution.py:19
  65.1 5.3 convolution_convert_fusion.6.v_ref
  79.8 31.3 %shard_map.295 = (f32[128,2048]{1,0:T(8,128)S(1)}, bf16[512,2048]{1,0:T(8,128)(2,1)S(1)}, bf16[512,1024]{1,0:T(8,128)(2,1)S(1)}, bf16[512,1024]{1,0:T(8,128)(2,1)S(1)}) custom-call(bf16[512,2048]{1,0:T(8,128)(2,1)S(1)} %convolution_convert_fusion.5.partial, bf16[128,2048]{1,0:T(8,128)(2,1)S(1)} %bitcast.114, ...), custom_call_target="tpu_custom_call" | custom-call | flops 2621440 | bytes 62914560 | tf_op jit(solution)/shard_map/pallas_call | solution.py:761
  114.5 8.0 %shard_map.296.g_ref = bf16[512,512]{1,0:T(8,128)(2,1)} custom-call(bf16[512,512]{1,0:T(8,128)(2,1)S(1)} %convolution_convert_fusion.10.q_ref, bf16[1024,512]{1,0:T(8,128)(2,1)S(1)} %copy-done.75, bf16[1024,512]{1,0:T(8,128)(2,1)S(1)} %convolution_convert_fusion.6.v_ref, s32[512,1]{1,0:T(8,128)S(1)} %copy-done.69, s32[1,1024]{1,0:T(1,128)S(1)} %and_select_fusion.col_ref), custom_call_target="tpu_custom_call" | custom-call | flops 1073741824 | bytes 3145728 | tf_op jit(solution)/shard_map/pallas_call | solution.py:97
  125.7 31.0 %shard_map.299 = (f32[128,2048]{1,0:T(8,128)S(1)}, bf16[512,2048]{1,0:T(8,128)(2,1)S(1)}, bf16[256,1024]{1,0:T(8,128)(2,1)S(1)}, bf16[256,1024]{1,0:T(8,128)(2,1...) custom-call(bf16[512,2048]{1,0:T(8,128)(2,1)S(1)} %convolution_convert_fusion.4.partial, ...), custom_call_target="tpu_custom_call" | custom-call | flops 2621440 | bytes 62914560 | tf_op jit(solution)/shard_map/pallas_call | solution.py:761
  162.8 10.8 %shard_map.301 = (bf16[512,1280]{1,0:T(8,128)(2,1)}, bf16[512,1280]{1,0:T(8,128)(2,1)S(1)}, bf16[512,1280]{1,0:T(8,128)(2,1)S(1)}) custom-call(bf16[512,2048]{1,0:T(8,128)(2,1)S(1)} %get-tuple-element.112.in_ref.n_ref.a_ref, bf16[2048,1280]{1,0:T(8,128)(2,1)S(1)} %copy-done.70, bf16[2048,1280]{1,0:T(8,128)(2,1)S(1)} %bitcast.116, ...), custom_call_target="tpu_custom_call" | custom-call | flops 8053063680 | bytes 19660800 | tf_op jit(solution)/shard_map/pallas_call | solution.py:520
  174.6 6.7 %shard_map.302.partial = bf16[512,2048]{1,0:T(8,128)(2,1)S(1)} custom-call(bf16[512,1280]{1,0:T(8,128)(2,1)S(1)} %get-tuple-element.125.gate_ref.g_ref, bf16[512,1280]{1,0:T(8,128)(2,1)S(1)} %get-tuple-element.130.up_ref.g_ref, bf16[2048,1280]{1,0:T(8,128)(2,1)S(1)} %copy-done.70, bf16[2048,1280]{1,0:T(8,128)(2,1)S(1)} %bitcast.116), custom_call_target="tpu_custom_call" | custom-call | flops 5368709120 | bytes 13107200 | tf_op jit(solution)/shard_map/pallas_call | solution.py:545
  182.4 5.8 convolution_convert_fusion.3.partial
  188.2 15.3 %shard_map.303.rest_0_ = f32[128,2048]{1,0:T(8,128)S(1)} custom-call(bf16[512,2048]{1,0:T(8,128)(2,1)S(1)} %convolution_convert_fusion.3.partial, f32[128,2048]{1,0:T(8,128)S(1)} %get-tuple-element.117.rows.kept, bf16[16,128]{1,0:T(8,128)(2,1)S(1)} %broadcast_in_dim.29.partial.kept, f32[1,2048]{1,0:T(1,128)S(1)} %get-tuple-element.255.gain), custom_call_target="tpu_custom_call" | custom-call | flops 2621440 | bytes 62914560 | tf_op jit(solution)/shard_map/pallas_call | solution.py:761
  205.5 5.9 %shard_map.304 = (bf16[1,256,1280]{2,1,0:T(8,128)(2,1)S(1)}, bf16[3,256,1280]{2,1,0:T(8,128)(2,1)S(1)}) custom-call(s32[4]{0:T(128)S(1)} %broadcast_add_fusion.at_ref, bf16[512,2048]{1,0:T(8,128)(2,1)S(1)} %shard_map.291.in_ref.three_ref.a_ref, bf16[256,1024]{1,0:T(8,128)(2,1)S(1)} %copy-done.72, bf16[256,1024]{1,0:T(8,128)(2,1)S(1)} %copy-done.74, ...), custom_call_target="tpu_custom_call" | custom-call | flops 2684354560 | bytes 7340032 | tf_op jit(solution)/shard_map/pallas_call | solution.py:249
  215.2 29.5 %shard_map.305 = (f32[128,2048]{1,0:T(8,128)S(1)}, bf16[512,2048]{1,0:T(8,128)(2,1)S(1)}, f32[1,2048]{1,0:T(1,128)S(1)}) custom-call(bf16[512,2048]{1,0:T(8,128)(2,1)S(1)} %shard_map.302.partial, bf16[128,2048]{1,0:T(8,128)(2,1)} %bitcast.8.refs_0_.rows, f32[128,2048]{1,0:T(8,128)S(1)} %get-tuple-element.117.rows.kept, f32[1,2048]{1,0:T(1,128)S(1)} %get-tuple-element.254.gain), custom_call_target="tpu_custom_call" | custom-call | flops 2621440 | bytes 62914560 | tf_op jit(solution)/shard_map/pallas_call | solution.py:761
  244.7 5.5 shard_map.306
  253.7 9.6 %shard_map.307 = (bf16[512,512]{1,0:T(8,128)(2,1)S(1)}, bf16[2,1024,512]{2,1,0:T(8,128)(2,1)S(1)}) custom-call(bf16[512,512]{1,0:T(8,128)(2,1)S(1)} %copy-done.80, bf16[1024,512]{1,0:T(8,128)(2,1)S(1)} %copy-done.76, bf16[1024,512]{1,0:T(8,128)(2,1)S(1)} %copy-done.78, s32[512,1]{1,0:T(8,128)S(1)} %copy-done.69, s32[1,1024]{1,0:T(1,128)S(1)} %and_select_fusion.col_ref, ...), custom_call_target="tpu_custom_call" | custom-call | flops 2684354560 | bytes 6291456 | tf_op jit(solution)/shard_map/pallas_call | solution.py:150
  265.7 6.6 %shard_map.308 = (bf16[1,256,1280]{2,1,0:T(8,128)(2,1)S(1)}, bf16[3,256,1280]{2,1,0:T(8,128)(2,1)}) custom-call(s32[4]{0:T(128)S(1)} %broadcast_add_fusion.at_ref, bf16[512,2048]{1,0:T(8,128)(2,1)S(1)} %get-tuple-element.112.in_ref.n_ref.a_ref, bf16[256,1024]{1,0:T(8,128)(2,1)} %collective-permute-done.6.lo_ref, ...), custom_call_target="tpu_custom_call" | custom-call | flops 2684354560 | bytes 7340032 | tf_op jit(solution)/shard_map/pallas_call | solution.py:249
  275.1 28.1 %shard_map.310 = (f32[128,2048]{1,0:T(8,128)S(1)}, bf16[512,2048]{1,0:T(8,128)(2,1)S(1)}, f32[1,2048]{1,0:T(1,128)S(1)}) custom-call(bf16[512,2048]{1,0:T(8,128)(2,1)S(1)} %convolution_convert_fusion.2.rest_0_.partial, f32[128,2048]{1,0:T(8,128)S(1)} %get-tuple-element.134.rows, f32[128,2048]{1,0:T(8,128)S(1)} %get-tuple-element.110.rows.kept, ...), custom_call_target="tpu_custom_call" | custom-call | flops 2621440 | bytes 62914560 | tf_op jit(solution)/shard_map/pallas_call | solution.py:761
  315.6 7.3 %shard_map.311 = (bf16[512,512]{1,0:T(8,128)(2,1)S(1)}, bf16[512,512]{1,0:T(8,128)(2,1)S(1)}, bf16[512,512]{1,0:T(8,128)(2,1)S(1)}) custom-call(bf16[512,512]{1,0:T(8,128)(2,1)S(1)} %copy-done.51, bf16[512,512]{1,0:T(8,128)(2,1)S(1)} %copy-done.53, bf16[512,512]{1,0:T(8,128)(2,1)S(1)} %copy-done.55, s32[512,2]{1,0:T(8,128)S(1)} %copy-done.39, ...), custom_call_target="tpu_custom_call" | custom-call | flops 1342177280 | bytes 4194304 | tf_op jit(solution)/shard_map/pallas_call | solution.py:150
  334.2 4.5 shard_map.312
  348.2 38.3 %shard_map.318 = (f32[128,2048]{1,0:T(8,128)S(1)}, f32[8,2048]{1,0:T(8,128)S(1)}, bf16[256,1024]{1,0:T(8,128)(2,1)S(1)}, bf16[256,1024]{1,0:T(8,128)(2,1)S(1)}, ...) custom-call(bf16[512,2048]{1,0:T(8,128)(2,1)S(1)} %add_convert_fusio, ...), custom_call_target="tpu_custom_call" | custom-call | flops 2621440 | bytes 62914560 | tf_op jit(solution)/shard_map/pallas_call | solution.py:761
  401.6 4.3 shard_map.321
  426.4 147.7 %shard_map.326 = (f32[256,1280]{1,0:T(8,128)}, f32[256,1280]{1,0:T(8,128)}, f32[256,1280]{1,0:T(8,128)}, f32[256,512]{1,0:T(8,128)}, f32[256,512]{1,0:T(8,128)},...) custom-call(bf16[2,256,1280]{2,1,0:T(8,128)(2,1)} %copy-done.25, ...), custom_call_target="tpu_custom_call" | custom-call | flops 8568832 | bytes 85688320 | tf_op jit(solution)/shard_map/pallas_call | solution.py:479
  575.4 7.0 %shard_map.327 = (f32[1280,256]{1,0:T(8,128)}, f32[256,1280]{1,0:T(8,128)}, f32[256,1280]{1,0:T(8,128)}, f32[256,512]{1,0:T(8,128)}, f32[256,512]{1,0:T(8,128)},...) custom-call(f32[256,1280]{1,0:T(8,128)} %get-tuple-element.173.refs_, ...), custom_call_target="tpu_custom_call" | custom-call | bytes 17104896 | tf_op jit(solution)/shard_map/pallas_call | solution.py:575
  (347 shorter events, 139.2 us)
Async XLA Ops:
  21.2 49.3 %collective-permute-start = (bf16[128,2048]{1,0:T(8,128)(2,1)}, bf16[128,2048]{1,0:T(8,128)(2,1)}, u32[]{:S(2)}, u32[]{:S(2)}) collective-permute-start(bf16[128,2048]{1,0:T(8,128)(2,1)} %bitcast.8.refs_0_.rows), channel_id=1, source_target_pairs={{0,2},{1,3},{2,0},{3,1},{4,6},{5,7},{6,4},{7,5},{8,10},{9,11},{10,... | collective-permute-start | bytes 1572872 | tf_op jit(solution)/shard_map/ppermute | solution.py:799
  22.3 51.0 %collective-permute-start.1 = (bf16[128,2048]{1,0:T(8,128)(2,1)}, bf16[128,2048]{1,0:T(8,128)(2,1)}, u32[]{:S(2)}, u32[]{:S(2)}) collective-permute-start(bf16[128,2048]{1,0:T(8,128)(2,1)} %bitcast.8.refs_0_.rows), channel_id=1, source_target_pairs={{0,1},{1,0},{2,3},{3,2},{4,5},{5,4},{6,7},{7,6},{8,9},{9,8},{10,11... | collective-permute-start | bytes 1572872 | tf_op jit(solution)/shard_map/ppermute | solution.py:799
  26.1 44.4 %collective-permute-start.3 = (bf16[256,1024]{1,0:T(8,128)(2,1)}, bf16[256,1024]{1,0:T(8,128)(2,1)}, u32[]{:S(2)}, u32[]{:S(2)}) collective-permute-start(bf16[256,1024]{1,0:T(8,128)(2,1)} %shard_map.292), channel_id=1, source_target_pairs={{0,4},{4,0},{8,12},{12,8},{16,20},{20,16},{24,28},{28,24},{1,5},{5... | collective-permute-start | bytes 1572872 | tf_op jit(solution)/shard_map/ppermute | solution.py:799
  47.1 64.1 %collective-permute-start.5 = (bf16[512,512]{1,0:T(8,128)(2,1)}, bf16[512,512]{1,0:T(8,128)(2,1)}, u32[]{:S(2)}, u32[]{:S(2)}) collective-permute-start(bf16[512,512]{1,0:T(8,128)(2,1)} %shard_map.290.g_ref), channel_id=1, source_target_pairs={{0,4},{4,0},{8,12},{12,8},{16,20},{20,16},{24,28},{28,24},{1,5},{5... | collective-permute-start | bytes 1572872 | tf_op jit(solution)/shard_map/ppermute | solution.py:799
  70.5 2.8 collective-permute-start.2
  70.5 6.2 %collective-permute-start.4 = (bf16[256,1024]{1,0:T(8,128)(2,1)}, bf16[256,1024]{1,0:T(8,128)(2,1)S(1)}, u32[]{:S(2)}, u32[]{:S(2)}) collective-permute-start(bf16[256,1024]{1,0:T(8,128)(2,1)} %collective-permute-done.3.refs_20_), channel_id=1, source_target_pairs={{0,1},{1,0},{2,3},{3,2},{4,5},{5,4},{6,7},{7,6},{8,9},{9,8},{10,11... | collective-permute-start | bytes 1572872 | tf_op jit(solution)/shard_map/ppermute | solution.py:799
  159.2 14.4 %collective-permute-start.6 = (bf16[256,1024]{1,0:T(8,128)(2,1)S(1)}, bf16[256,1024]{1,0:T(8,128)(2,1)}, u32[]{:S(2)}, u32[]{:S(2)}) collective-permute-start(bf16[256,1024]{1,0:T(8,128)(2,1)S(1)} %shard_map.300), channel_id=1, source_target_pairs={{0,4},{4,0},{8,12},{12,8},{16,20},{20,16},{24,28},{28,24},{1,5},{5... | collective-permute-start | bytes 1572872 | tf_op jit(solution)/shard_map/ppermute | solution.py:799
  173.6 31.9 %collective-permute-start.7 = (bf16[512,1280]{1,0:T(8,128)(2,1)}, bf16[512,1280]{1,0:T(8,128)(2,1)S(1)}, u32[]{:S(2)}, u32[]{:S(2)}) collective-permute-start(bf16[512,1280]{1,0:T(8,128)(2,1)} %get-tuple-element.120.g_ref), channel_id=1, source_target_pairs={{0,4},{4,0},{8,12},{12,8},{16,20},{20,16},{24,28},{28,24},{1,5},{5... | collective-permute-start | bytes 3932168 | tf_op jit(solution)/shard_map/ppermute | solution.py:799
  181.3 63.4 %collective-permute-start.9 = (bf16[512,1280]{1,0:T(8,128)(2,1)S(1)}, bf16[512,1280]{1,0:T(8,128)(2,1)S(1)}, u32[]{:S(2)}, u32[]{:S(2)}) collective-permute-start(bf16[512,1280]{1,0:T(8,128)(2,1)S(1)} %get-tuple-element.125.gate_ref.g_ref), channel_id=1, source_target_pairs={{0,4},{4,0},{8,12},{12,8},{16,20},{20,16},{24,28},{28,24},{1,5},{5... | collective-permute-start | bytes 3932168 | tf_op jit(solution)/shard_map/ppermute | solution.py:799
  203.6 41.1 %collective-permute-start.8 = (bf16[256,1024]{1,0:T(8,128)(2,1)}, bf16[256,1024]{1,0:T(8,128)(2,1)S(1)}, u32[]{:S(2)}, u32[]{:S(2)}) collective-permute-start(bf16[256,1024]{1,0:T(8,128)(2,1)} %collective-permute-done.6.lo_ref), channel_id=1, source_target_pairs={{0,1},{1,0},{2,3},{3,2},{4,5},{5,4},{6,7},{7,6},{8,9},{9,8},{10,11... | collective-permute-start | bytes 1572872 | tf_op jit(solution)/shard_map/ppermute | solution.py:799
  211.4 62.0 %collective-permute-start.11 = (bf16[3,256,1280]{2,1,0:T(8,128)(2,1)S(1)}, bf16[3,256,1280]{2,1,0:T(8,128)(2,1)S(1)}, u32[]{:S(2)}, u32[]{:S(2)}) collective-permute-start(bf16[3,256,1280]{2,1,0:T(8,128)(2,1)S(1)} %get-tuple-element.122.left_ref), channel_id=1, source_target_pairs={{0,8},{4,12},{8,0},{12,4},{16,24},{20,28},{24,16},{28,20},{1,9},{5... | collective-permute-start | bytes 5898248 | tf_op jit(solution)/shard_map/ppermute | solution.py:799
  213.9 51.7 %collective-permute-start.10 = (bf16[512,1280]{1,0:T(8,128)(2,1)S(1)}, bf16[512,1280]{1,0:T(8,128)(2,1)S(1)}, u32[]{:S(2)}, u32[]{:S(2)}) collective-permute-start(bf16[512,1280]{1,0:T(8,128)(2,1)S(1)} %get-tuple-element.130.up_ref.g_ref), channel_id=1, source_target_pairs={{0,4},{4,0},{8,12},{12,8},{16,20},{20,16},{24,28},{28,24},{1,5},{5... | collective-permute-start | bytes 3932168 | tf_op jit(solution)/shard_map/ppermute | solution.py:799
  215.2 118.5 %copy-start.14 = (bf16[512,1024]{1,0:T(8,128)(2,1)}, bf16[512,1024]{1,0:T(8,128)(2,1)S(1)}, u32[]{:S(2)}) copy-start(bf16[512,1024]{1,0:T(8,128)(2,1)S(1)} %get-tuple-element.250.hi_ref) | copy-start | bytes 3145732
  215.2 118.5 %copy-start.16 = (bf16[512,1024]{1,0:T(8,128)(2,1)}, bf16[512,1024]{1,0:T(8,128)(2,1)S(1)}, u32[]{:S(2)}) copy-start(bf16[512,1024]{1,0:T(8,128)(2,1)S(1)} %get-tuple-element.251.lo_ref) | copy-start | bytes 3145732
  250.2 79.1 %collective-permute-start.15 = (bf16[3,256,1280]{2,1,0:T(8,128)(2,1)S(1)}, bf16[3,256,1280]{2,1,0:T(8,128)(2,1)S(1)}, u32[]{:S(2)}, u32[]{:S(2)}) collective-permute-start(bf16[3,256,1280]{2,1,0:T(8,128)(2,1)S(1)} %get-tuple-element.127.left_ref), channel_id=1, source_target_pairs={{0,8},{4,12},{8,0},{12,4},{16,24},{20,28},{24,16},{28,20},{1,9},{5... | collective-permute-start | bytes 5898248 | tf_op jit(solution)/shard_map/ppermute | solution.py:799
  263.3 68.7 %collective-permute-start.13 = (bf16[2,1024,512]{2,1,0:T(8,128)(2,1)S(1)}, bf16[2,1024,512]{2,1,0:T(8,128)(2,1)S(1)}, u32[]{:S(2)}, u32[]{:S(2)}) collective-permute-start(bf16[2,1024,512]{2,1,0:T(8,128)(2,1)S(1)} %get-tuple-element.137.g_ref), channel_id=1, source_target_pairs={{0,4},{4,0},{8,12},{12,8},{16,20},{20,16},{24,28},{28,24},{1,5},{5... | collective-permute-start | bytes 6291464 | tf_op jit(solution)/shard_map/ppermute | solution.py:799
  272.2 119.3 %collective-permute-start.20 = (bf16[3,256,1280]{2,1,0:T(8,128)(2,1)}, bf16[3,256,1280]{2,1,0:T(8,128)(2,1)}, u32[]{:S(2)}, u32[]{:S(2)}) collective-permute-start(bf16[3,256,1280]{2,1,0:T(8,128)(2,1)} %get-tuple-element.132.left_ref), channel_id=1, source_target_pairs={{0,8},{4,12},{8,0},{12,4},{16,24},{20,28},{24,16},{28,20},{1,9},{5... | collective-permute-start | bytes 5898248 | tf_op jit(solution)/shard_map/ppermute | solution.py:799
  306.2 6.0 %collective-permute-start.12 = (bf16[1024,512]{1,0:T(8,128)(2,1)S(1)}, bf16[1024,512]{1,0:T(8,128)(2,1)S(1)}, u32[]{:S(2)}, u32[]{:S(2)}) collective-permute-start(bf16[1024,512]{1,0:T(8,128)(2,1)S(1)} %add_convert_fusion.6), channel_id=1, source_target_pairs={{0,1},{1,0},{2,3},{3,2},{4,5},{5,4},{6,7},{7,6},{8,9},{9,8},{10,11... | collective-permute-start | bytes 3145736 | tf_op jit(solution)/shard_map/ppermute | solution.py:799
  309.0 29.7 %collective-permute-start.14 = (bf16[1024,512]{1,0:T(8,128)(2,1)}, bf16[1024,512]{1,0:T(8,128)(2,1)}, u32[]{:S(2)}, u32[]{:S(2)}) collective-permute-start(bf16[1024,512]{1,0:T(8,128)(2,1)} %add_convert_fusion.3), channel_id=1, source_target_pairs={{0,1},{1,0},{2,3},{3,2},{4,5},{5,4},{6,7},{7,6},{8,9},{9,8},{10,11... | collective-permute-start | bytes 3145736 | tf_op jit(solution)/shard_map/ppermute | solution.py:799
  312.1 34.3 %collective-permute-start.16 = (bf16[2,256,1280]{2,1,0:T(8,128)(2,1)}, bf16[2,256,1280]{2,1,0:T(8,128)(2,1)S(1)}, u32[]{:S(2)}, u32[]{:S(2)}) collective-permute-start(bf16[2,256,1280]{2,1,0:T(8,128)(2,1)} %slice.50), channel_id=1, source_target_pairs={{0,1},{1,0},{2,3},{3,2},{4,5},{5,4},{6,7},{7,6},{8,16},{9,17},{10,... | collective-permute-start | bytes 3932168 | tf_op jit(solution)/shard_map/ppermute | solution.py:839
  329.4 14.2 %collective-permute-start.17 = (bf16[512,512]{1,0:T(8,128)(2,1)S(1)}, bf16[512,512]{1,0:T(8,128)(2,1)S(1)}, u32[]{:S(2)}, u32[]{:S(2)}) collective-permute-start(bf16[512,512]{1,0:T(8,128)(2,1)S(1)} %get-tuple-element.129.g_ref), channel_id=1, source_target_pairs={{0,4},{4,0},{8,12},{12,8},{16,20},{20,16},{24,28},{28,24},{1,5},{5... | collective-permute-start | bytes 1572872 | tf_op jit(solution)/shard_map/ppermute | solution.py:799
  332.7 85.4 %collective-permute-start.21 = (bf16[1024,512]{1,0:T(8,128)(2,1)}, bf16[1024,512]{1,0:T(8,128)(2,1)}, u32[]{:S(2)}, u32[]{:S(2)}) collective-permute-start(bf16[1024,512]{1,0:T(8,128)(2,1)} %add_convert_fusion.5), channel_id=1, source_target_pairs={{0,2},{1,3},{2,0},{3,1},{4,6},{5,7},{6,4},{7,5},{8,10},{9,11},{10,... | collective-permute-start | bytes 3145736 | tf_op jit(solution)/shard_map/ppermute | solution.py:799
  338.7 85.1 %collective-permute-start.18 = (bf16[2,256,1280]{2,1,0:T(8,128)(2,1)}, bf16[2,256,1280]{2,1,0:T(8,128)(2,1)}, u32[]{:S(2)}, u32[]{:S(2)}) collective-permute-start(bf16[2,256,1280]{2,1,0:T(8,128)(2,1)} %slice.51), channel_id=1, source_target_pairs={{0,1},{1,0},{2,3},{3,2},{4,5},{5,4},{6,7},{7,6},{8,16},{9,17},{10,... | collective-permute-start | bytes 3932168 | tf_op jit(solution)/shard_map/ppermute | solution.py:839
  388.1 24.9 %collective-permute-start.19 = (bf16[512,512]{1,0:T(8,128)(2,1)}, bf16[512,512]{1,0:T(8,128)(2,1)}, u32[]{:S(2)}, u32[]{:S(2)}) collective-permute-start(bf16[512,512]{1,0:T(8,128)(2,1)} %shard_map.296.g_ref), channel_id=1, source_target_pairs={{0,4},{4,0},{8,12},{12,8},{16,20},{20,16},{24,28},{28,24},{1,5},{5... | collective-permute-start | bytes 1572872 | tf_op jit(solution)/shard_map/ppermute | solution.py:799
  (109 other events, 671.8 us)

commit v7 on v6

--- a/solution.py
+++ b/solution.py
@@ -51,7 +51,7 @@
     return grad_rows, jnp.sum(grad * rows * inv, axis=0)
 
 
-VMEM_LIMIT = 17 * 2**20
+VMEM_LIMIT = 16 * 2**20
 GELU_SCALE = 0.7978845608028654
 GELU_CUBE = 0.044715
 ANY = pl.BlockSpec(memory_space=pl.ANY)
@@ -63,7 +63,7 @@
     )
 
 
-def wide_params(grid_rank, size=28):
+def wide_params(grid_rank, size=24):
     return pltpu.CompilerParams(
         dimension_semantics=("arbitrary",) * grid_rank, vmem_limit_bytes=size * 2**20
     )
@@ -489,7 +489,7 @@
         + [pltpu.SemaphoreType.DMA((total,))] * 6
         + [pltpu.SemaphoreType.DMA((pairs + 1,))] * 2,
         compiler_params=pltpu.CompilerParams(
-            collective_id=0, has_side_effects=True, vmem_limit_bytes=56 * 2**20
+            collective_id=0, has_side_effects=True, vmem_limit_bytes=53 * 2**20
         ),
         cost_estimate=cost(4 * sum(sizes), 40 * sum(sizes)),
     )(*parts, *rests, *grads, own, low, high, kept, sent)
@@ -779,7 +779,7 @@
             else []
         ),
         compiler_params=pltpu.CompilerParams(
-            collective_id=number, has_side_effects=True, vmem_limit_bytes=22 * 2**20
+            collective_id=number, has_side_effects=True, vmem_limit_bytes=20 * 2**20
         ),
         cost_estimate=cost(10 * step * width, 60 * 2**20),
     )(partial, rows, kept, gain, *given, *wanted, *along)
@@ -1089,10 +1089,12 @@
             line("w_key", split_one, grad_sk, grad_sk, True)
             line("w_value", split_one, grad_sv, grad_sv, True)
         turned["patch"] = True
+        results["tokens"], turned["patch"] = grad_rows, False
         names = [n for n in results if n != "gains"]
         turns = tuple(bool(turned.get(n)) for n in names)
         results.update(zip(names, finish([results[n] for n in names], turns)))
-        patch_total = results["patch"]
+        grad_rows = results["tokens"]
+        patch_total = results["patch"].T
         if paired:
             gain_total = results["gains"][:3, :width]
         else:

time: 597 us -> 591 us (0.990)
  local copies, waits for them, and re-layouts: 49.8 us -> 39.5 us
    unnamed x225 -> x219, local copies, waits for them, and re-layouts: 39.7 us -> 32.3 us
  transfers between devices with their start and end apart: 22 -> 22, of which waited for: 2 -> 2; matrix products, arithmetic and copies ran while one was open for 12% -> 12% of each run, Pallas kernels for 40% -> 41%
where the time goes in v7:
time: 591 us; the launch traced here: 581 us
  Pallas kernels  451 us (76%)
  matrix products  64.8 us (11%)
  local copies, waits for them, and re-layouts  39.5 us (7%)
  starting transfers between devices  16.7 us (3%)
    pallas_call x7, Pallas kernels, boundary(): pl.pallas_call(functools.partial(boundary_kernel, mode, jobs, early), in_...  191 us
    pallas_call x1, Pallas kernels, line_sums(): pl.pallas_call(functools.partial(line_kernel, ready, merged, count, pairs...  147 us
    pallas_call x8, Pallas kernels, pair_grad(): pl.pallas_call(pair_kernel, grid_spec=pltpu.PrefetchScalarGridSpec(num_sc...  38.6 us
    dot_general x10, matrix products, matmul(): return jnp.dot(left, right, preferred_element_type=F32)  37.8 us
    unnamed x219, local copies, waits for them, and re-layouts  32.3 us
    pallas_call x2, Pallas kernels, attend_back(): pl.pallas_call(self_back_kernel if causal else cross_back_kernel, grid=(w...  16.9 us
    ppermute x20, starting transfers between devices, swap(): return lax.ppermute(value, axis, [(i, i ^ bit) for i in range(size)])  16.7 us
    pallas_call x2, Pallas kernels, attend(): pl.pallas_call(functools.partial(attend_kernel, causal), grid=(width // H...  13.7 us
  transfers between devices with their start and end apart: 22, of which 2 were waited for; matrix products, arithmetic and copies ran while one was open for 12% of the time, Pallas kernels for 41%

profile of v7, /device:TPU:0, one launch (start us, length us, event | category | flops | bytes accessed | tf_op | source)
XLA Modules:
  0.0 581.2 jit_solution(5568836406923097006)
XLA Ops:
  2.8 17.1 %shard_map.289.in_ref.refs_19_ = bf16[512,2048]{1,0:T(8,128)(2,1)S(1)} custom-call(bf16[16,128]{1,0:T(8,128)(2,1)S(1)} %broadcast_in_dim.29.partial.kept, bf16[128,2048]{1,0:T(8,128)(2,1)S(1)} %bitcast.113, bf16[16,128]{1,0:T(8,128)(2,1)S(1)} %broadcast_in_dim.29.partial.kept, f32[1,2048]{1,0:T(1,128)S(1)} %get-tuple-element.212.gain), custom_call_target="tpu_custom_call" | custom-call | flops 2621440 | bytes 62914560 | tf_op jit(solution)/shard_map/pallas_call | solution.py:761
  27.6 4.4 convolution_convert_fusion.13.q_ref
  41.4 5.7 shard_map.290.g_ref
  47.7 9.9 %convolution_convert_fusion.in_ref.a_ref = bf16[1024,2048]{1,0:T(8,128)(2,1)S(1)} fusion(bf16[1024,1664]{1,0:T(8,128)(2,1)S(1)} %bitcast.111, bf16[1664,2048]{1,0:T(8,128)(2,1)} %param.28), kind=kOutput, calls=%fused_computation.1 | convolution fusion | flops 6981419008 | bytes 14417920 | tf_op jit(solution)/shard_map/dot_general | solution.py:19
  65.2 5.3 convolution_convert_fusion.6.v_ref
  80.0 31.4 %shard_map.295 = (f32[128,2048]{1,0:T(8,128)S(1)}, bf16[512,2048]{1,0:T(8,128)(2,1)S(1)}, bf16[512,1024]{1,0:T(8,128)(2,1)S(1)}, bf16[512,1024]{1,0:T(8,128)(2,1)S(1)}) custom-call(bf16[512,2048]{1,0:T(8,128)(2,1)S(1)} %convolution_convert_fusion.5.partial, bf16[128,2048]{1,0:T(8,128)(2,1)S(1)} %bitcast.114, ...), custom_call_target="tpu_custom_call" | custom-call | flops 2621440 | bytes 62914560 | tf_op jit(solution)/shard_map/pallas_call | solution.py:761
  114.3 8.0 %shard_map.296.g_ref = bf16[512,512]{1,0:T(8,128)(2,1)} custom-call(bf16[512,512]{1,0:T(8,128)(2,1)S(1)} %convolution_convert_fusion.10.q_ref, bf16[1024,512]{1,0:T(8,128)(2,1)S(1)} %copy-done.72, bf16[1024,512]{1,0:T(8,128)(2,1)S(1)} %convolution_convert_fusion.6.v_ref, s32[512,1]{1,0:T(8,128)S(1)} %copy-done.64, s32[1,1024]{1,0:T(1,128)S(1)} %and_select_fusion.col_ref), custom_call_target="tpu_custom_call" | custom-call | flops 1073741824 | bytes 3145728 | tf_op jit(solution)/shard_map/pallas_call | solution.py:97
  124.8 31.0 %shard_map.299 = (f32[128,2048]{1,0:T(8,128)S(1)}, bf16[512,2048]{1,0:T(8,128)(2,1)S(1)}, bf16[256,1024]{1,0:T(8,128)(2,1)S(1)}, bf16[256,1024]{1,0:T(8,128)(2,1...) custom-call(bf16[512,2048]{1,0:T(8,128)(2,1)S(1)} %convolution_convert_fusion.4.partial, ...), custom_call_target="tpu_custom_call" | custom-call | flops 2621440 | bytes 62914560 | tf_op jit(solution)/shard_map/pallas_call | solution.py:761
  160.3 10.9 %shard_map.301 = (bf16[512,1280]{1,0:T(8,128)(2,1)}, bf16[512,1280]{1,0:T(8,128)(2,1)}, bf16[512,1280]{1,0:T(8,128)(2,1)S(1)}) custom-call(bf16[512,2048]{1,0:T(8,128)(2,1)S(1)} %get-tuple-element.113.in_ref.n_ref.a_ref, bf16[2048,1280]{1,0:T(8,128)(2,1)S(1)} %copy-done.65, bf16[2048,1280]{1,0:T(8,128)(2,1)S(1)} %bitcast.116, ...), custom_call_target="tpu_custom_call" | custom-call | flops 8053063680 | bytes 19660800 | tf_op jit(solution)/shard_map/pallas_call | solution.py:520
  172.3 7.6 %shard_map.302.partial = bf16[512,2048]{1,0:T(8,128)(2,1)S(1)} custom-call(bf16[512,1280]{1,0:T(8,128)(2,1)} %get-tuple-element.126.gate_ref.g_ref, bf16[512,1280]{1,0:T(8,128)(2,1)S(1)} %get-tuple-element.131.up_ref.g_ref, bf16[2048,1280]{1,0:T(8,128)(2,1)S(1)} %copy-done.65, bf16[2048,1280]{1,0:T(8,128)(2,1)S(1)} %bitcast.116), custom_call_target="tpu_custom_call" | custom-call | flops 5368709120 | bytes 13107200 | tf_op jit(solution)/shard_map/pallas_call | solution.py:545
  181.1 4.5 convolution_convert_fusion.3.partial
  185.6 15.4 %shard_map.303.rest_0_ = f32[128,2048]{1,0:T(8,128)S(1)} custom-call(bf16[512,2048]{1,0:T(8,128)(2,1)S(1)} %convolution_convert_fusion.3.partial, f32[128,2048]{1,0:T(8,128)S(1)} %get-tuple-element.118.rows.kept, bf16[16,128]{1,0:T(8,128)(2,1)S(1)} %broadcast_in_dim.29.partial.kept, f32[1,2048]{1,0:T(1,128)S(1)} %get-tuple-element.212.gain), custom_call_target="tpu_custom_call" | custom-call | flops 2621440 | bytes 62914560 | tf_op jit(solution)/shard_map/pallas_call | solution.py:761
  203.3 6.5 %shard_map.304 = (bf16[1,256,1280]{2,1,0:T(8,128)(2,1)S(1)}, bf16[3,256,1280]{2,1,0:T(8,128)(2,1)S(1)}) custom-call(s32[4]{0:T(128)S(1)} %broadcast_add_fusion.at_ref, bf16[512,2048]{1,0:T(8,128)(2,1)S(1)} %shard_map.291.in_ref.three_ref.a_ref, bf16[256,1024]{1,0:T(8,128)(2,1)S(1)} %copy-done.69, bf16[256,1024]{1,0:T(8,128)(2,1)S(1)} %copy-done.71, ...), custom_call_target="tpu_custom_call" | custom-call | flops 2684354560 | bytes 7340032 | tf_op jit(solution)/shard_map/pallas_call | solution.py:249
  213.4 29.4 %shard_map.305 = (f32[128,2048]{1,0:T(8,128)S(1)}, bf16[512,2048]{1,0:T(8,128)(2,1)S(1)}, f32[1,2048]{1,0:T(1,128)S(1)}) custom-call(bf16[512,2048]{1,0:T(8,128)(2,1)S(1)} %shard_map.302.partial, bf16[128,2048]{1,0:T(8,128)(2,1)} %bitcast.8.refs_0_.rows, f32[128,2048]{1,0:T(8,128)S(1)} %get-tuple-element.118.rows.kept, f32[1,2048]{1,0:T(1,128)S(1)} %get-tuple-element.211.gain), custom_call_target="tpu_custom_call" | custom-call | flops 2621440 | bytes 62914560 | tf_op jit(solution)/shard_map/pallas_call | solution.py:761
  242.9 6.0 %shard_map.306 = (bf16[1,256,1280]{2,1,0:T(8,128)(2,1)S(1)}, bf16[3,256,1280]{2,1,0:T(8,128)(2,1)S(1)}) custom-call(s32[4]{0:T(128)S(1)} %broadcast_add_fusion.at_ref, bf16[512,2048]{1,0:T(8,128)(2,1)S(1)} %get-tuple-element.113.in_ref.n_ref.a_ref, bf16[256,1024]{1,0:T(8,128)(2,1)} %collective-permute-done.6.lo_ref, ...), custom_call_target="tpu_custom_call" | custom-call | flops 2684354560 | bytes 7340032 | tf_op jit(solution)/shard_map/pallas_call | solution.py:249
  252.5 9.6 %shard_map.307 = (bf16[512,512]{1,0:T(8,128)(2,1)S(1)}, bf16[2,1024,512]{2,1,0:T(8,128)(2,1)S(1)}) custom-call(bf16[512,512]{1,0:T(8,128)(2,1)S(1)} %copy-done.77, bf16[1024,512]{1,0:T(8,128)(2,1)S(1)} %copy-done.73, bf16[1024,512]{1,0:T(8,128)(2,1)S(1)} %copy-done.75, s32[512,1]{1,0:T(8,128)S(1)} %copy-done.64, s32[1,1024]{1,0:T(1,128)S(1)} %and_select_fusion.col_ref, ...), custom_call_target="tpu_custom_call" | custom-call | flops 2684354560 | bytes 6291456 | tf_op jit(solution)/shard_map/pallas_call | solution.py:150
  264.4 6.4 %shard_map.310 = (bf16[1,256,1280]{2,1,0:T(8,128)(2,1)S(1)}, bf16[3,256,1280]{2,1,0:T(8,128)(2,1)}) custom-call(s32[4]{0:T(128)S(1)} %broadcast_add_fusion.at_ref, bf16[512,2048]{1,0:T(8,128)(2,1)S(1)} %get-tuple-element.113.in_ref.n_ref.a_ref, bf16[256,1024]{1,0:T(8,128)(2,1)} %collective-permute-done.6.lo_ref, ...), custom_call_target="tpu_custom_call" | custom-call | flops 2684354560 | bytes 7340032 | tf_op jit(solution)/shard_map/pallas_call | solution.py:249
  272.5 28.1 %shard_map.311 = (f32[128,2048]{1,0:T(8,128)S(1)}, bf16[512,2048]{1,0:T(8,128)(2,1)S(1)}, f32[1,2048]{1,0:T(1,128)S(1)}) custom-call(bf16[512,2048]{1,0:T(8,128)(2,1)S(1)} %convolution_convert_fusion.2.rest_0_.partial, f32[128,2048]{1,0:T(8,128)S(1)} %get-tuple-element.135.rows, f32[128,2048]{1,0:T(8,128)S(1)} %get-tuple-element.111.rows.kept, ...), custom_call_target="tpu_custom_call" | custom-call | flops 2621440 | bytes 62914560 | tf_op jit(solution)/shard_map/pallas_call | solution.py:761
  313.0 7.3 %shard_map.312 = (bf16[512,512]{1,0:T(8,128)(2,1)S(1)}, bf16[512,512]{1,0:T(8,128)(2,1)S(1)}, bf16[512,512]{1,0:T(8,128)(2,1)S(1)}) custom-call(bf16[512,512]{1,0:T(8,128)(2,1)S(1)} %copy-done.45, bf16[512,512]{1,0:T(8,128)(2,1)S(1)} %copy-done.47, bf16[512,512]{1,0:T(8,128)(2,1)S(1)} %copy-done.49, s32[512,2]{1,0:T(8,128)S(1)} %copy-done.37, ...), custom_call_target="tpu_custom_call" | custom-call | flops 1342177280 | bytes 4194304 | tf_op jit(solution)/shard_map/pallas_call | solution.py:150
  348.2 38.5 %shard_map.319 = (f32[128,2048]{1,0:T(8,128)S(1)}, f32[8,2048]{1,0:T(8,128)S(1)}, bf16[256,1024]{1,0:T(8,128)(2,1)S(1)}, bf16[256,1024]{1,0:T(8,128)(2,1)S(1)}, ...) custom-call(bf16[512,2048]{1,0:T(8,128)(2,1)S(1)} %add_convert_fusio, ...), custom_call_target="tpu_custom_call" | custom-call | flops 2621440 | bytes 62914560 | tf_op jit(solution)/shard_map/pallas_call | solution.py:761
  401.8 4.3 shard_map.321
  407.8 4.3 shard_map.320
  425.7 147.3 %shard_map.326 = (f32[256,1280]{1,0:T(8,128)}, f32[256,1280]{1,0:T(8,128)}, f32[256,1280]{1,0:T(8,128)}, f32[256,512]{1,0:T(8,128)}, f32[256,512]{1,0:T(8,128)},...) custom-call(bf16[2,256,1280]{2,1,0:T(8,128)(2,1)} %copy-done.25, ...), custom_call_target="tpu_custom_call" | custom-call | flops 8568832 | bytes 85688320 | tf_op jit(solution)/shard_map/pallas_call | solution.py:479
  573.6 7.2 %shard_map.327 = (f32[1280,256]{1,0:T(8,128)}, f32[256,1280]{1,0:T(8,128)}, f32[256,1280]{1,0:T(8,128)}, f32[256,512]{1,0:T(8,128)}, f32[256,512]{1,0:T(8,128)},...) custom-call(f32[256,1280]{1,0:T(8,128)} %get-tuple-element.173.refs_, ...), custom_call_target="tpu_custom_call" | custom-call | bytes 19202048 | tf_op jit(solution)/shard_map/pallas_call | solution.py:575
  (341 shorter events, 132.5 us)
Async XLA Ops:
  21.2 49.4 %collective-permute-start = (bf16[128,2048]{1,0:T(8,128)(2,1)}, bf16[128,2048]{1,0:T(8,128)(2,1)}, u32[]{:S(2)}, u32[]{:S(2)}) collective-permute-start(bf16[128,2048]{1,0:T(8,128)(2,1)} %bitcast.8.refs_0_.rows), channel_id=1, source_target_pairs={{0,2},{1,3},{2,0},{3,1},{4,6},{5,7},{6,4},{7,5},{8,10},{9,11},{10,... | collective-permute-start | bytes 1572872 | tf_op jit(solution)/shard_map/ppermute | solution.py:799
  22.3 51.2 %collective-permute-start.1 = (bf16[128,2048]{1,0:T(8,128)(2,1)}, bf16[128,2048]{1,0:T(8,128)(2,1)}, u32[]{:S(2)}, u32[]{:S(2)}) collective-permute-start(bf16[128,2048]{1,0:T(8,128)(2,1)} %bitcast.8.refs_0_.rows), channel_id=1, source_target_pairs={{0,1},{1,0},{2,3},{3,2},{4,5},{5,4},{6,7},{7,6},{8,9},{9,8},{10,11... | collective-permute-start | bytes 1572872 | tf_op jit(solution)/shard_map/ppermute | solution.py:799
  26.1 44.6 %collective-permute-start.3 = (bf16[256,1024]{1,0:T(8,128)(2,1)}, bf16[256,1024]{1,0:T(8,128)(2,1)}, u32[]{:S(2)}, u32[]{:S(2)}) collective-permute-start(bf16[256,1024]{1,0:T(8,128)(2,1)} %shard_map.292), channel_id=1, source_target_pairs={{0,4},{4,0},{8,12},{12,8},{16,20},{20,16},{24,28},{28,24},{1,5},{5... | collective-permute-start | bytes 1572872 | tf_op jit(solution)/shard_map/ppermute | solution.py:799
  47.1 64.3 %collective-permute-start.5 = (bf16[512,512]{1,0:T(8,128)(2,1)}, bf16[512,512]{1,0:T(8,128)(2,1)}, u32[]{:S(2)}, u32[]{:S(2)}) collective-permute-start(bf16[512,512]{1,0:T(8,128)(2,1)} %shard_map.290.g_ref), channel_id=1, source_target_pairs={{0,4},{4,0},{8,12},{12,8},{16,20},{20,16},{24,28},{28,24},{1,5},{5... | collective-permute-start | bytes 1572872 | tf_op jit(solution)/shard_map/ppermute | solution.py:799
  70.6 2.8 collective-permute-start.2
  70.7 6.5 %collective-permute-start.4 = (bf16[256,1024]{1,0:T(8,128)(2,1)}, bf16[256,1024]{1,0:T(8,128)(2,1)S(1)}, u32[]{:S(2)}, u32[]{:S(2)}) collective-permute-start(bf16[256,1024]{1,0:T(8,128)(2,1)} %collective-permute-done.3.refs_20_), channel_id=1, source_target_pairs={{0,1},{1,0},{2,3},{3,2},{4,5},{5,4},{6,7},{7,6},{8,9},{9,8},{10,11... | collective-permute-start | bytes 1572872 | tf_op jit(solution)/shard_map/ppermute | solution.py:799
  156.7 14.6 %collective-permute-start.6 = (bf16[256,1024]{1,0:T(8,128)(2,1)S(1)}, bf16[256,1024]{1,0:T(8,128)(2,1)}, u32[]{:S(2)}, u32[]{:S(2)}) collective-permute-start(bf16[256,1024]{1,0:T(8,128)(2,1)S(1)} %shard_map.300), channel_id=1, source_target_pairs={{0,4},{4,0},{8,12},{12,8},{16,20},{20,16},{24,28},{28,24},{1,5},{5... | collective-permute-start | bytes 1572872 | tf_op jit(solution)/shard_map/ppermute | solution.py:799
  171.2 32.0 %collective-permute-start.7 = (bf16[512,1280]{1,0:T(8,128)(2,1)}, bf16[512,1280]{1,0:T(8,128)(2,1)}, u32[]{:S(2)}, u32[]{:S(2)}) collective-permute-start(bf16[512,1280]{1,0:T(8,128)(2,1)} %get-tuple-element.121.g_ref), channel_id=1, source_target_pairs={{0,4},{4,0},{8,12},{12,8},{16,20},{20,16},{24,28},{28,24},{1,5},{5... | collective-permute-start | bytes 3932168 | tf_op jit(solution)/shard_map/ppermute | solution.py:799
  179.9 63.0 %collective-permute-start.10 = (bf16[512,1280]{1,0:T(8,128)(2,1)}, bf16[512,1280]{1,0:T(8,128)(2,1)S(1)}, u32[]{:S(2)}, u32[]{:S(2)}) collective-permute-start(bf16[512,1280]{1,0:T(8,128)(2,1)} %get-tuple-element.126.gate_ref.g_ref), channel_id=1, source_target_pairs={{0,4},{4,0},{8,12},{12,8},{16,20},{20,16},{24,28},{28,24},{1,5},{5... | collective-permute-start | bytes 3932168 | tf_op jit(solution)/shard_map/ppermute | solution.py:799
  200.9 41.9 %collective-permute-start.9 = (bf16[256,1024]{1,0:T(8,128)(2,1)}, bf16[256,1024]{1,0:T(8,128)(2,1)S(1)}, u32[]{:S(2)}, u32[]{:S(2)}) collective-permute-start(bf16[256,1024]{1,0:T(8,128)(2,1)} %collective-permute-done.6.lo_ref), channel_id=1, source_target_pairs={{0,1},{1,0},{2,3},{3,2},{4,5},{5,4},{6,7},{7,6},{8,9},{9,8},{10,11... | collective-permute-start | bytes 1572872 | tf_op jit(solution)/shard_map/ppermute | solution.py:799
  209.8 62.1 %collective-permute-start.8 = (bf16[3,256,1280]{2,1,0:T(8,128)(2,1)S(1)}, bf16[3,256,1280]{2,1,0:T(8,128)(2,1)S(1)}, u32[]{:S(2)}, u32[]{:S(2)}) collective-permute-start(bf16[3,256,1280]{2,1,0:T(8,128)(2,1)S(1)} %get-tuple-element.123.left_ref), channel_id=1, source_target_pairs={{0,8},{4,12},{8,0},{12,4},{16,24},{20,28},{24,16},{28,20},{1,9},{5... | collective-permute-start | bytes 5898248 | tf_op jit(solution)/shard_map/ppermute | solution.py:799
  212.3 52.2 %collective-permute-start.13 = (bf16[512,1280]{1,0:T(8,128)(2,1)S(1)}, bf16[512,1280]{1,0:T(8,128)(2,1)S(1)}, u32[]{:S(2)}, u32[]{:S(2)}) collective-permute-start(bf16[512,1280]{1,0:T(8,128)(2,1)S(1)} %copy-done.67), channel_id=1, source_target_pairs={{0,4},{4,0},{8,12},{12,8},{16,20},{20,16},{24,28},{28,24},{1,5},{5... | collective-permute-start | bytes 3932168 | tf_op jit(solution)/shard_map/ppermute | solution.py:799
  213.4 120.4 %copy-start.14 = (bf16[512,1024]{1,0:T(8,128)(2,1)}, bf16[512,1024]{1,0:T(8,128)(2,1)S(1)}, u32[]{:S(2)}) copy-start(bf16[512,1024]{1,0:T(8,128)(2,1)S(1)} %get-tuple-element.207.hi_ref) | copy-start | bytes 3145732
  213.4 120.3 %copy-start.16 = (bf16[512,1024]{1,0:T(8,128)(2,1)}, bf16[512,1024]{1,0:T(8,128)(2,1)S(1)}, u32[]{:S(2)}) copy-start(bf16[512,1024]{1,0:T(8,128)(2,1)S(1)} %get-tuple-element.208.lo_ref) | copy-start | bytes 3145732
  249.0 80.4 %collective-permute-start.12 = (bf16[3,256,1280]{2,1,0:T(8,128)(2,1)S(1)}, bf16[3,256,1280]{2,1,0:T(8,128)(2,1)S(1)}, u32[]{:S(2)}, u32[]{:S(2)}) collective-permute-start(bf16[3,256,1280]{2,1,0:T(8,128)(2,1)S(1)} %get-tuple-element.128.left_ref), channel_id=1, source_target_pairs={{0,8},{4,12},{8,0},{12,4},{16,24},{20,28},{24,16},{28,20},{1,9},{5... | collective-permute-start | bytes 5898248 | tf_op jit(solution)/shard_map/ppermute | solution.py:799
  262.1 70.0 %collective-permute-start.17 = (bf16[2,1024,512]{2,1,0:T(8,128)(2,1)S(1)}, bf16[2,1024,512]{2,1,0:T(8,128)(2,1)S(1)}, u32[]{:S(2)}, u32[]{:S(2)}) collective-permute-start(bf16[2,1024,512]{2,1,0:T(8,128)(2,1)S(1)} %get-tuple-element.138.g_ref), channel_id=1, source_target_pairs={{0,4},{4,0},{8,12},{12,8},{16,20},{20,16},{24,28},{28,24},{1,5},{5... | collective-permute-start | bytes 6291464 | tf_op jit(solution)/shard_map/ppermute | solution.py:799
  270.8 120.9 %collective-permute-start.20 = (bf16[3,256,1280]{2,1,0:T(8,128)(2,1)}, bf16[3,256,1280]{2,1,0:T(8,128)(2,1)}, u32[]{:S(2)}, u32[]{:S(2)}) collective-permute-start(bf16[3,256,1280]{2,1,0:T(8,128)(2,1)} %get-tuple-element.133.left_ref), channel_id=1, source_target_pairs={{0,8},{4,12},{8,0},{12,4},{16,24},{20,28},{24,16},{28,20},{1,9},{5... | collective-permute-start | bytes 5898248 | tf_op jit(solution)/shard_map/ppermute | solution.py:799
  301.7 44.7 %collective-permute-start.11 = (bf16[2,256,1280]{2,1,0:T(8,128)(2,1)S(1)}, bf16[2,256,1280]{2,1,0:T(8,128)(2,1)S(1)}, u32[]{:S(2)}, u32[]{:S(2)}) collective-permute-start(bf16[2,256,1280]{2,1,0:T(8,128)(2,1)S(1)} %slice.50), channel_id=1, source_target_pairs={{0,1},{1,0},{2,3},{3,2},{4,5},{5,4},{6,7},{7,6},{8,16},{9,17},{10,... | collective-permute-start | bytes 3932168 | tf_op jit(solution)/shard_map/ppermute | solution.py:839
  303.6 5.9 %collective-permute-start.14 = (bf16[1024,512]{1,0:T(8,128)(2,1)S(1)}, bf16[1024,512]{1,0:T(8,128)(2,1)S(1)}, u32[]{:S(2)}, u32[]{:S(2)}) collective-permute-start(bf16[1024,512]{1,0:T(8,128)(2,1)S(1)} %add_convert_fusion.6), channel_id=1, source_target_pairs={{0,1},{1,0},{2,3},{3,2},{4,5},{5,4},{6,7},{7,6},{8,9},{9,8},{10,11... | collective-permute-start | bytes 3145736 | tf_op jit(solution)/shard_map/ppermute | solution.py:799
  309.5 29.7 %collective-permute-start.18 = (bf16[1024,512]{1,0:T(8,128)(2,1)}, bf16[1024,512]{1,0:T(8,128)(2,1)}, u32[]{:S(2)}, u32[]{:S(2)}) collective-permute-start(bf16[1024,512]{1,0:T(8,128)(2,1)} %add_convert_fusion.3), channel_id=1, source_target_pairs={{0,1},{1,0},{2,3},{3,2},{4,5},{5,4},{6,7},{7,6},{8,9},{9,8},{10,11... | collective-permute-start | bytes 3145736 | tf_op jit(solution)/shard_map/ppermute | solution.py:799
  329.4 14.1 %collective-permute-start.16 = (bf16[512,512]{1,0:T(8,128)(2,1)S(1)}, bf16[512,512]{1,0:T(8,128)(2,1)S(1)}, u32[]{:S(2)}, u32[]{:S(2)}) collective-permute-start(bf16[512,512]{1,0:T(8,128)(2,1)S(1)} %get-tuple-element.130.g_ref), channel_id=1, source_target_pairs={{0,4},{4,0},{8,12},{12,8},{16,20},{20,16},{24,28},{28,24},{1,5},{5... | collective-permute-start | bytes 1572872 | tf_op jit(solution)/shard_map/ppermute | solution.py:799
  332.7 84.4 %collective-permute-start.21 = (bf16[1024,512]{1,0:T(8,128)(2,1)}, bf16[1024,512]{1,0:T(8,128)(2,1)}, u32[]{:S(2)}, u32[]{:S(2)}) collective-permute-start(bf16[1024,512]{1,0:T(8,128)(2,1)} %add_convert_fusion.5), channel_id=1, source_target_pairs={{0,2},{1,3},{2,0},{3,1},{4,6},{5,7},{6,4},{7,5},{8,10},{9,11},{10,... | collective-permute-start | bytes 3145736 | tf_op jit(solution)/shard_map/ppermute | solution.py:799
  339.2 83.7 %collective-permute-start.15 = (bf16[2,256,1280]{2,1,0:T(8,128)(2,1)}, bf16[2,256,1280]{2,1,0:T(8,128)(2,1)}, u32[]{:S(2)}, u32[]{:S(2)}) collective-permute-start(bf16[2,256,1280]{2,1,0:T(8,128)(2,1)} %slice.51), channel_id=1, source_target_pairs={{0,1},{1,0},{2,3},{3,2},{4,5},{5,4},{6,7},{7,6},{8,16},{9,17},{10,... | collective-permute-start | bytes 3932168 | tf_op jit(solution)/shard_map/ppermute | solution.py:839
  388.4 23.7 %collective-permute-start.19 = (bf16[512,512]{1,0:T(8,128)(2,1)}, bf16[512,512]{1,0:T(8,128)(2,1)}, u32[]{:S(2)}, u32[]{:S(2)}) collective-permute-start(bf16[512,512]{1,0:T(8,128)(2,1)} %shard_map.296.g_ref), channel_id=1, source_target_pairs={{0,4},{4,0},{8,12},{12,8},{16,20},{20,16},{24,28},{28,24},{1,5},{5... | collective-permute-start | bytes 1572872 | tf_op jit(solution)/shard_map/ppermute | solution.py:799
  (107 other events, 687.9 us)
